TPU v7x, 256 devices: a whole 4x4x8 slice. The times are simulated.
256 devices in a mesh: left: 8 (over x, z_hi), right: 32 (over y, z_lo, core).
Axes of the slice: x: 4, y: 4, z: 8 (z_hi: 2, z_lo: 4; z = z_hi * 4 + z_lo), core: 2. Of those that a mesh axis runs over, the one named last changes fastest.
Arguments:
- src_embed: float32 [98304, 400], P(('left', 'right')), may hold values from -1.5 to 1.5
- src_state: float32 [98304], P(('left', 'right')), may hold values from 0.002 to 0.05
- dst_embed: float32 [98304, 400], P(('left', 'right')), may hold values from -1.5 to 1.5
- dst_state: float32 [98304], P(('left', 'right')), may hold values from 0.002 to 0.05
- relation: float32 [256, 400], replicated, may hold values from -4 to 4
- rel_state: float32 [256, 400], replicated, may hold values from 5 to 50
- edge_src: int32 [256, 1000], P(('left', 'right')), may hold values from 0 to 383
- edge_dst: int32 [256, 1000], P(('left', 'right')), may hold values from 0 to 383
- edge_rel: int32 [256, 1000], P(('left', 'right')), may hold values from 0 to 255
- neg_rows: int32 [256, 2, 1000], P(('left', 'right')), may hold values from 0 to 383
- edge_count: int32 [256], P(('left', 'right')), may hold values from 250 to 1000, as said below
Outputs:
- src_out: float32 [98304, 400], P(('left', 'right'))
- dst_out: float32 [98304, 400], P(('left', 'right'))
- dst_state_out: float32 [98304], P(('left', 'right'))
- relation_out: float32 [256, 400], replicated
Inputs may be any that keep to these rules, and one draw needn't show every extreme that they name: `edge_count`: each bucket's edge slots are live from the first one up to its count, the rest are padding; some bucket has all 1000 slots live.
All inputs are finite; a program needn't handle non-finite values.
Results may differ from a plain program's by a relative error of at most 0.0003.
Values sent between devices are 32-bit elements; how exact they have to be, the bound alone decides.
No kernel may reach another device: no remote copies, remote signals or barrier semaphores. Data moves between devices by JAX's collectives and lax.ppermute only.
A program may use at most 64 MiB of HBM per device.

v0:
```python
import jax
import jax.numpy as jnp
from jax import lax
from jax.sharding import PartitionSpec as P

BATCH = 500
BATCHES = 2
SHIFT = 5


ROW_RATE = 0.2
REL_RATE = 1.0


def shifted(value, axis, steps):
    count = lax.axis_size(axis)
    pairs = [(source, (source + steps) % count) for source in range(count)]
    return lax.ppermute(value, axis, pairs)


def complex_product(first, second):
    middle = first.shape[-1] // 2
    first_re, first_im = (first[:, :middle], first[:, middle:])
    second_re, second_im = (second[:, :middle], second[:, middle:])
    real_part = first_re * second_re - first_im * second_im
    imag_part = first_re * second_im + first_im * second_re
    return jnp.concatenate([real_part, imag_part], axis=-1)


def split_grads(query_grad, sources, relations):
    middle = sources.shape[-1] // 2
    grad_re, grad_im = (query_grad[:, :middle], query_grad[:, middle:])
    source_re, source_im = (sources[:, :middle], sources[:, middle:])
    rel_re, rel_im = (relations[:, :middle], relations[:, middle:])
    source_grad = jnp.concatenate(
        [grad_re * rel_re + grad_im * rel_im, grad_im * rel_re - grad_re * rel_im], axis=-1
    )
    rho_grad = jnp.concatenate(
        [grad_re * source_re + grad_im * source_im, grad_im * source_re - grad_re * source_im],
        axis=-1,
    )
    return (source_grad, rho_grad)


def partner_side(queries, dst_rows, sample_rows, valid, table):
    targets = jnp.take(table, dst_rows, axis=0)
    samples = jnp.take(table, sample_rows, axis=0)
    positive = jnp.sum(queries * targets, axis=-1)
    negative = jnp.dot(queries, samples.T, precision=lax.Precision.HIGHEST)
    pos_weight = -valid * jax.nn.sigmoid(-positive)
    neg_weight = valid[:, None] * jax.nn.sigmoid(negative) / samples.shape[0]
    query_grad = pos_weight[:, None] * targets + jnp.dot(
        neg_weight, samples, precision=lax.Precision.HIGHEST
    )
    sample_grad = jnp.dot(neg_weight.T, queries, precision=lax.Precision.HIGHEST)
    table_grad = jax.ops.segment_sum(
        pos_weight[:, None] * queries, dst_rows, num_segments=table.shape[0]
    )
    table_grad = table_grad + jax.ops.segment_sum(
        sample_grad, sample_rows, num_segments=table.shape[0]
    )
    return (query_grad, table_grad)


def entity_update(table, state, grad):
    new_state = state + jnp.mean(grad * grad, axis=-1)
    return (table - ROW_RATE * grad / jnp.sqrt(new_state)[..., None], new_state)


def live_mask(live, low):
    positions = lax.iota(jnp.int32, BATCH)
    return (positions + low < live).astype(jnp.float32)


def body(
    src_embed,
    src_state,
    dst_embed,
    dst_state,
    relation,
    rel_state,
    edge_src,
    edge_dst,
    edge_rel,
    neg_rows,
    edge_count,
):
    src_table, src_sums = (src_embed, src_state)
    dst_table, dst_sums = shifted((dst_embed, dst_state), "right", SHIFT)
    rel_sums = rel_state
    for batch_index in range(BATCHES):
        low = batch_index * BATCH
        src_ids = edge_src[0, low : low + BATCH]
        rel_ids = edge_rel[0, low : low + BATCH]
        source_rows = jnp.take(src_table, src_ids, axis=0)
        rel_rows = jnp.take(relation, rel_ids, axis=0)
        queries = complex_product(source_rows, rel_rows)
        valid = live_mask(edge_count[0], low)
        query_grad, dst_grad = partner_side(
            queries, edge_dst[0, low : low + BATCH], neg_rows[0, batch_index], valid, dst_table
        )
        source_grad, rho_grad = split_grads(query_grad, source_rows, rel_rows)
        src_grad = jax.ops.segment_sum(source_grad, src_ids, num_segments=src_table.shape[0])
        rel_grad = jax.ops.segment_sum(rho_grad, rel_ids, num_segments=relation.shape[0])
        src_table, src_sums = entity_update(src_table, src_sums, src_grad)
        dst_table, dst_sums = entity_update(dst_table, dst_sums, dst_grad)
        total_grad = lax.psum(rel_grad, ("left", "right"))
        rel_sums = rel_sums + total_grad * total_grad
        relation = relation - REL_RATE * total_grad / jnp.sqrt(rel_sums)
    dst_table, dst_sums = shifted((dst_table, dst_sums), "right", -SHIFT)
    return (src_table, dst_table, dst_sums, relation)


def solution(mesh):
    in_specs = (
        P(("left", "right"), None),
        P(("left", "right")),
        P(("left", "right"), None),
        P(("left", "right")),
        P(),
        P(),
        P(("left", "right"), None),
        P(("left", "right"), None),
        P(("left", "right"), None),
        P(("left", "right"), None, None),
        P(("left", "right")),
    )
    out_specs = (P(("left", "right"), None), P(("left", "right"), None), P(("left", "right")), P())
    return jax.shard_map(body, mesh=mesh, in_specs=in_specs, out_specs=out_specs, check_vma=False)
```

profile of v0, /device:TPU:1, one launch (start us, length us, event | category | flops | bytes accessed | tf_op | source)
XLA Modules:
  0.0 620.4 jit_solution(17554852066542321966)
XLA Ops:
  7.2 5.8 collective-permute-start
  36.0 4.9 gather_fusion.3
  40.9 2.5 gather_fusion.2
  45.9 5.3 multiply_multiply_fusion.1
  51.2 4.7 fusion.36
  56.1 4.3 multiply_add_fusion
  65.8 5.4 scatter_custom_fusion.1
  74.7 4.4 scatter_custom_fusion
  81.3 7.4 %scatter_custom_fusion.3 = f32[384,400]{1,0:T(8,128)S(1)} fusion(s32[1000]{0:T(1024)S(1)} %bitcast.22, f32[1000,400]{1,0:T(8,128)} %fusion.36, f32[]{:T(128)} %constant.13.clone.1), kind=kCustom, calls=%fused_computation.79 | custom fusion | flops 400000 | bytes 614912 | tf_op jit(solution)/shard_map/scatter-add | solution.py:59
  88.7 2.8 copy.67
  91.5 5.1 scatter_custom_fusion.2
  109.7 4.9 gather_fusion.7
  116.6 205.6 %all-reduce.3.cloned.1.call-done = f32[256,400]{1,0:T(8,128)} async-done(((f32[256,400]{1,0:T(8,128)}), f32[256,400]{1,0:T(8,128)}) %all-reduce.3.cloned.1.call-update) | async-done | bytes 409616 | tf_op jit(solution)/shard_map/psum | solution.py:107
  331.1 3.7 multiply_multiply_fusion
  334.8 4.7 fusion.35
  339.7 4.3 fusion.8
  347.6 2.7 copy.75
  350.3 4.9 scatter_custom_fusion.7
  355.3 7.4 %scatter_custom_fusion.6 = f32[384,400]{1,0:T(8,128)S(1)} fusion(s32[1000]{0:T(1024)S(1)} %bitcast.19, f32[1000,400]{1,0:T(8,128)} %fusion.35, f32[]{:T(128)} %constant.13.clone.1), kind=kCustom, calls=%fused_computation.73 | custom fusion | flops 400000 | bytes 614912 | tf_op jit(solution)/shard_map/scatter-add | solution.py:59
  365.2 5.1 scatter_custom_fusion.5
  375.7 2.8 collective-permute-start.2
  378.4 5.8 collective-permute-start.3
  386.7 4.4 scatter_custom_fusion.4
  392.7 215.7 %all-reduce.5.cloned.1.call-done = f32[256,400]{1,0:T(8,128)} async-done(((f32[256,400]{1,0:T(8,128)}), f32[256,400]{1,0:T(8,128)}) %all-reduce.5.cloned.1.call-update) | async-done | bytes 409616 | tf_op jit(solution)/shard_map/psum | solution.py:107
  (142 shorter events, 80.6 us)
Async XLA Ops:
  7.2 315.1 %all-reduce.3.cloned.1.call-start = ((), (), s32[]{:S(2)}) async-start(), calls=%async_computation | async-start | bytes 1048576 | tf_op jit(solution)/shard_map/psum | solution.py:107
  7.2 27.5 %collective-permute-start = (f32[384,400]{0,1:T(8,128)}, f32[384,400]{0,1:T(8,128)}, u32[]{:S(2)}, u32[]{:S(2)}) collective-permute-start(f32[384,400]{0,1:T(8,128)} %param.19), channel_id=1, source_target_pairs={{0,5},{1,6},{2,7},{3,8},{4,9},{5,10},{6,11},{7,12},{8,13},{9,14},{... | collective-permute-start | bytes 1843208 | tf_op jit(solution)/shard_map/ppermute | solution.py:18
  13.0 89.6 %collective-permute-start.1 = (f32[384]{0:T(512)}, f32[384]{0:T(512)}, u32[]{:S(2)}, u32[]{:S(2)}) collective-permute-start(f32[384]{0:T(512)} %param.20), channel_id=1, source_target_pairs={{0,5},{1,6},{2,7},{3,8},{4,9},{5,10},{6,11},{7,12},{8,13},{9,14},{... | collective-permute-start | bytes 4616 | tf_op jit(solution)/shard_map/ppermute | solution.py:18
  40.9 4.9 copy-start.19
  40.9 4.9 copy-start.23
  51.2 4.7 copy-start.3
  51.2 4.7 copy-start.17
  51.2 4.9 copy-start.1
  60.5 1.7 copy-start.7
  71.2 537.2 %all-reduce.5.cloned.1.call-start = ((), (), s32[]{:S(2)}) async-start(), calls=%async_computation.1 | async-start | bytes 1048576 | tf_op jit(solution)/shard_map/psum | solution.py:107
  72.2 7.8 %copy-start.15 = (f32[384]{0:T(512)S(1)}, f32[384]{0:T(512)}, u32[]{:S(2)}) copy-start(f32[384]{0:T(512)} %param.18) | copy-start | bytes 4612
  88.7 9.1 %copy-start.9 = (f32[384,400]{1,0:T(8,128)}, f32[384,400]{1,0:T(8,128)S(1)}, u32[]{:S(2)}) copy-start(f32[384,400]{1,0:T(8,128)S(1)} %scatter_custom_fusion.3) | copy-start | bytes 1843204
  109.7 4.9 copy-start.21
  109.7 212.6 %copy-start.12 = (f32[256,400]{1,0:T(8,128)S(1)}, f32[256,400]{1,0:T(8,128)}, u32[]{:S(2)}) copy-start(f32[256,400]{1,0:T(8,128)} %copy.64) | copy-start | bytes 1228804
  323.4 4.9 copy-start.20
  328.4 2.7 copy-start
  328.4 2.7 copy-start.18
  328.4 2.7 copy-start.22
  334.8 4.7 copy-start.2
  334.8 4.7 copy-start.16
  344.1 1.4 copy-start.8
  370.3 2.1 copy-start.10
  375.7 235.1 %collective-permute-start.2 = (f32[384,400]{0,1:T(8,128)}, f32[384,400]{0,1:T(8,128)}, u32[]{:S(2)}, u32[]{:S(2)}) collective-permute-start(f32[384,400]{0,1:T(8,128)} %copy.74), channel_id=1, source_target_pairs={{0,27},{1,28},{2,29},{3,30},{4,31},{5,0},{6,1},{7,2},{8,3},{9,4},{... | collective-permute-start | bytes 1843208 | tf_op jit(solution)/shard_map/ppermute | solution.py:18
  378.4 14.3 %collective-permute-start.3 = (f32[384]{0:T(512)S(1)}, f32[384]{0:T(512)S(1)}, u32[]{:S(2)}, u32[]{:S(2)}) collective-permute-start(f32[384]{0:T(512)S(1)} %get-tuple-element.20), channel_id=1, source_target_pairs={{0,27},{1,28},{2,29},{3,30},{4,31},{5,0},{6,1},{7,2},{8,3},{9,4},{... | collective-permute-start | bytes 4616 | tf_op jit(solution)/shard_map/ppermute | solution.py:18
  (6 other events, 6.8 us)
Sparse Core Ops, SparseCore 0:
  71.3 250.8 all-reduce.2
  355.4 252.9 all-reduce.4
where the time goes:
time: 627 us; the launch traced here: 620 us
  waiting for transfers between devices  424 us (68%)
  other arithmetic  74.1 us (12%)
  local copies, waits for them, and re-layouts  65.8 us (10%)
  matrix products  27.1 us (4%)
  between operations  15.4 us (2%)
  starting transfers between devices  14.5 us (2%)
    psum x2, waiting for transfers between devices, body(): total_grad = lax.psum(rel_grad, ('left', 'right'))  421 us
    scatter-add x2, other arithmetic, partner_side(): jax.ops.segment_sum(sample_grad, sample_rows, num_segments=table.shape[0])  14.9 us
    ppermute x4, starting transfers between devices, shifted(): return lax.ppermute(value, axis, pairs)  14.5 us
  transfers between devices with their start and end apart: 6, of which 4 were waited for; matrix products, arithmetic and copies ran while one was open for 21% of the time, Pallas kernels for 0%

commit v1 on v0

v1 whole, which is shorter than its diff:
```python
import jax
import jax.numpy as jnp
from jax import lax
from jax.experimental import pallas as pl
from jax.experimental.pallas import tpu as pltpu
from jax.sharding import Mesh, PartitionSpec as P

BATCH = 500
BATCHES = 2
NEG = 1000
SHIFT = 5
SLAB = 384
REL = 256
HALF = 128
W = 400
MID = 200
EP = 512
NP = 1024

ROW_RATE = 0.2
REL_RATE = 1.0

AXES = ("x", "zh", "y", "zl", "c")
PLANE = ("x", "y")
COLUMN = ("zh", "zl")
RIGHT = ("y", "zl", "c")

NN = (((1,), (0,)), ((), ()))
NT = (((1,), (1,)), ((), ()))
TN = (((0,), (0,)), ((), ()))


def parts(value):
    high = value.astype(jnp.bfloat16)
    low = (value - high.astype(jnp.float32)).astype(jnp.bfloat16)
    return (high, low)


def dot(first, second, dims):
    return lax.dot_general(first, second, dims, preferred_element_type=jnp.float32)


def dot3(first, second, dims):
    return (
        dot(first[0], second[0], dims) + dot(first[0], second[1], dims) + dot(first[1], second[0], dims)
    )


def pick(rows, ids):
    return (lax.broadcasted_iota(jnp.int32, (rows, EP), 0) == ids).astype(jnp.bfloat16)


def gather(table, hot):
    high, low = parts(table)
    return dot(high, hot, TN) + dot(low, hot, TN)


def scatter(hot, values):
    high, low = parts(values)
    return dot(hot, high, NT) + dot(hot, low, NT)


def column(row):
    return jnp.transpose(jnp.broadcast_to(row, (128, SLAB)))[:, :1]


def row(col):
    return jnp.transpose(jnp.broadcast_to(col, (SLAB, 128)))[:1, :]


def entity_update(table, state, grad):
    state = state + jnp.sum(grad * grad, axis=1, keepdims=True) * (1.0 / W)
    return (table - grad * (ROW_RATE / jnp.sqrt(state)), state)


def bucket(sources, relations, table, src_hot, dst_ids, rel_hot, src_ids, counts):
    s_re, s_im = (sources[:MID], sources[MID:])
    r_re, r_im = (relations[:MID], relations[MID:])
    queries = parts(jnp.concatenate([s_re * r_re - s_im * r_im, s_re * r_im + s_im * r_re], axis=0))
    rows = parts(table)
    logits = dot3(rows, queries, NN)
    tail = jnp.exp(-jnp.abs(logits))
    scale = jnp.where(src_ids >= 0, 1.0, 0.0) / (1.0 + tail)
    above = logits >= 0.0
    negative = jnp.where(above, 1.0, tail) * counts
    hit = lax.broadcasted_iota(jnp.int32, (SLAB, EP), 0) == dst_ids
    positive = jnp.where(hit, jnp.where(above, tail, 1.0), 0.0)
    weights = parts((negative - positive) * scale)
    grads = dot3(rows, weights, TN)
    g_re, g_im = (grads[:MID], grads[MID:])
    rho_grad = jnp.concatenate([g_re * s_re + g_im * s_im, g_im * s_re - g_re * s_im], axis=0)
    rel_grad = scatter(rel_hot, rho_grad)
    src_grad = jnp.concatenate([g_re * r_re + g_im * r_im, g_im * r_re - g_re * r_im], axis=0)
    src_grad = scatter(src_hot, src_grad)
    dst_grad = dot3(weights, queries, NT)
    return (rel_grad, src_grad, dst_grad)


def prepare_kernel(src_ref, rel_ref, ids_ref, neg_ref, sources_ref, relations_ref, counts_ref):
    sources_ref[...] = gather(src_ref[...], pick(SLAB, ids_ref[0:1, :]))
    relations_ref[...] = gather(rel_ref[...], pick(REL, ids_ref[4:5, :]))
    for batch in range(BATCHES):
        same = lax.broadcasted_iota(jnp.int32, (SLAB, NP), 0) == neg_ref[batch : batch + 1, :]
        total = jnp.sum(jnp.where(same, 1.0, 0.0), axis=1, keepdims=True)
        counts_ref[:, batch : batch + 1] = total * (1.0 / NEG)


def first_kernel(
    sources_ref, relations_ref, dst_ref, dst_state_ref, src_ref, src_state_ref, ids_ref, counts_ref,
    mine_ref, other_ref, src_out, src_state_out, dst_out, dst_state_out,
):
    rel_grad, src_grad, dst_grad = bucket(
        sources_ref[...], relations_ref[...], dst_ref[...], pick(SLAB, ids_ref[0:1, :]), ids_ref[2:3, :],
        pick(REL, ids_ref[5:6, :]), ids_ref[0:1, :], counts_ref[:, 0:1],
    )
    mine_ref[...] = rel_grad[:HALF]
    other_ref[...] = rel_grad[HALF:]
    src_out[...], src_state = entity_update(src_ref[...], column(src_state_ref[...]), src_grad)
    src_state_out[...] = row(src_state)
    dst_out[...], dst_state = entity_update(dst_ref[...], column(dst_state_ref[...]), dst_grad)
    dst_state_out[...] = row(dst_state)


def second_kernel(
    rel_mine_ref, rel_other_ref, dst_ref, dst_state_ref, src_ref, src_state_ref, ids_ref, counts_ref,
    mine_ref, other_ref, src_out, dst_out, dst_state_out,
):
    src_hot = pick(SLAB, ids_ref[1:2, :])
    rel_hot = pick(REL, ids_ref[6:7, :])
    relation = jnp.concatenate([rel_mine_ref[...], rel_other_ref[...]], axis=0)
    rel_grad, src_grad, dst_grad = bucket(
        gather(src_ref[...], src_hot), gather(relation, rel_hot), dst_ref[...], src_hot, ids_ref[3:4, :],
        rel_hot, ids_ref[1:2, :], counts_ref[:, 1:2],
    )
    mine_ref[...] = rel_grad[:HALF]
    other_ref[...] = rel_grad[HALF:]
    src_out[...], _ = entity_update(src_ref[...], column(src_state_ref[...]), src_grad)
    dst_out[...], dst_state = entity_update(dst_ref[...], column(dst_state_ref[...]), dst_grad)
    dst_state_out[...] = row(dst_state)


def call(kernel, outs, *args):
    shapes = [jax.ShapeDtypeStruct(shape, jnp.float32) for shape in outs]
    return pl.pallas_call(
        kernel,
        out_shape=shapes,
        in_specs=[pl.BlockSpec(memory_space=pltpu.VMEM)] * len(args),
        out_specs=[pl.BlockSpec(memory_space=pltpu.VMEM)] * len(shapes),
        compiler_params=pltpu.CompilerParams(vmem_limit_bytes=48 * 1024 * 1024),
    )(*args)


def shifted(value, steps):
    count = lax.axis_size(RIGHT)
    pairs = [(source, (source + steps) % count) for source in range(count)]
    return lax.ppermute(value, RIGHT, pairs)


def swapped(value):
    return lax.ppermute(value, "c", [(0, 1), (1, 0)])


def exchanged(value, axes):
    return lax.all_to_all(value, axes, split_axis=0, concat_axis=0, tiled=True)


def relation_update(mine, other, own, own_sums):
    lanes, layers = (lax.axis_size(PLANE), lax.axis_size(COLUMN))
    height = own.shape[0]
    half = mine + swapped(other)
    total = jnp.sum(exchanged(half.reshape(lanes, height, W), PLANE), axis=0)
    total = jnp.sum(exchanged(jnp.broadcast_to(total, (layers, height, W)), COLUMN), axis=0)
    own_sums = own_sums + total * total
    own = own - REL_RATE * total / jnp.sqrt(own_sums)
    half = exchanged(jnp.broadcast_to(own, (lanes, height, W)), PLANE).reshape(HALF, W)
    return (half, swapped(half), own, own_sums)


def padded(value, live, low):
    picked = value[low : low + BATCH]
    spot = lax.iota(jnp.int32, BATCH) + low
    return jnp.pad(jnp.where(spot < live, picked, -1), (0, EP - BATCH), constant_values=-1)


def body(
    src_embed, src_state, dst_embed, dst_state, relation, rel_state, edge_src, edge_dst, edge_rel, neg_rows, edge_count
):
    dst_table, dst_sums = (shifted(dst_embed, SHIFT), shifted(dst_state.reshape(1, SLAB), SHIFT))
    core = lax.axis_index("c")
    live = edge_count[0]
    near_rel = edge_rel[0] ^ (core * HALF)
    ids = jnp.stack(
        [
            padded(edge_src[0], live, 0),
            padded(edge_src[0], live, BATCH),
            padded(edge_dst[0], live, 0),
            padded(edge_dst[0], live, BATCH),
            padded(edge_rel[0], live, 0),
            padded(near_rel, live, 0),
            padded(near_rel, live, BATCH),
            jnp.full((EP,), -1, jnp.int32),
        ]
    )
    negs = jnp.pad(neg_rows[0], ((0, 0), (0, NP - NEG)), constant_values=-1)
    height = HALF // lax.axis_size(PLANE)
    start = core * HALF + lax.axis_index(PLANE) * height
    own = lax.dynamic_slice_in_dim(relation, start, height, 0)
    own_sums = lax.dynamic_slice_in_dim(rel_state, start, height, 0)
    src_sums = src_state.reshape(1, SLAB)

    sources, relations, counts = call(
        prepare_kernel, [(W, EP), (W, EP), (SLAB, BATCHES)], src_embed, relation, ids, negs
    )
    mine, other, src_table, src_sums, dst_table, dst_sums = call(
        first_kernel,
        [(HALF, W), (HALF, W), (SLAB, W), (1, SLAB), (SLAB, W), (1, SLAB)],
        sources, relations, dst_table, dst_sums, src_embed, src_sums, ids, counts,
    )
    near, far, own, own_sums = relation_update(mine, other, own, own_sums)
    mine, other, src_table, dst_table, dst_sums = call(
        second_kernel,
        [(HALF, W), (HALF, W), (SLAB, W), (SLAB, W), (1, SLAB)],
        near, far, dst_table, dst_sums, src_table, src_sums, ids, counts,
    )
    dst_table, dst_sums = (shifted(dst_table, -SHIFT), shifted(dst_sums, -SHIFT))
    near, far, own, own_sums = relation_update(mine, other, own, own_sums)
    first = core == 0
    relation = jnp.concatenate([jnp.where(first, near, far), jnp.where(first, far, near)], axis=0)
    return (src_table, dst_table, dst_sums.reshape(SLAB), relation)


def solution(mesh):
    left, right = (mesh.shape["left"], mesh.shape["right"])
    devices = mesh.devices.reshape(left // 2, 2, 4, right // 8, 2)
    inner = Mesh(devices, AXES)
    in_specs = (
        P(AXES, None),
        P(AXES),
        P(AXES, None),
        P(AXES),
        P(),
        P(),
        P(AXES, None),
        P(AXES, None),
        P(AXES, None),
        P(AXES, None, None),
        P(AXES),
    )
    out_specs = (P(AXES, None), P(AXES, None), P(AXES), P())
    return jax.shard_map(body, mesh=inner, in_specs=in_specs, out_specs=out_specs, check_vma=False)
```

time: 627 us -> 138 us (0.22)
  waiting for transfers between devices: 424 us -> 28.9 us
  other arithmetic: 74.1 us -> 0.88 us
  local copies, waits for them, and re-layouts: 65.8 us -> 18 us
  blocking collectives: 0 us -> 45 us
  matrix products: 27.1 us -> 0 us
  starting transfers between devices: 14.5 us -> 33.2 us
  between operations: 15.4 us -> 1.63 us
  Pallas kernels: 0 us -> 9.72 us
    psum x2 -> x0, waiting for transfers between devices: 421 us -> none  [body(): total_grad = lax.psum(rel_grad, ('left', 'right'))]
    all_to_all x0 -> x4, blocking collectives: none -> 45 us  [exchanged(): return lax.all_to_all(value, axes, split_axis=0, concat_axis=0, tiled=True)]
    scatter-add x8 -> x0, other arithmetic: 44.1 us -> none  [the longest x2 14.9 us: partner_side(): jax.ops.segment_sum(sample_grad, sample_rows, num_segments=table.shape[0])]
    gather x14 -> x0, local copies, waits for them, and re-layouts: 35 us -> none  [the longest x2 9.8 us: partner_side(): samples = jnp.take(table, sample_rows, axis=0)]
    dot_general x6 -> x0, matrix products: 27.1 us -> none  [the longest x2 9.36 us: partner_side(): jnp.dot(neg_weight.T, queries, precision=lax.Precision.HIGHEST)]
    ppermute x4 -> x8, waiting for transfers between devices: 2.21 us -> 18.2 us  [the longest x4 14.4 us: shifted(): return lax.ppermute(value, RIGHT, pairs)]
    all_to_all x0 -> x2, starting transfers between devices: none -> 11.3 us  [exchanged(): return lax.all_to_all(value, axes, split_axis=0, concat_axis=0, tiled=True)]
    all_to_all x0 -> x2, waiting for transfers between devices: none -> 10.7 us  [exchanged(): return lax.all_to_all(value, axes, split_axis=0, concat_axis=0, tiled=True)]
  transfers between devices with their start and end apart: 6 -> 10, of which waited for: 4 -> 7; matrix products, arithmetic and copies ran while one was open for 21% -> 4% of each run, Pallas kernels for 0% -> 1%
where the time goes in v1:
time: 138 us; the launch traced here: 137 us
  blocking collectives  45 us (33%)
  starting transfers between devices  33.2 us (24%)
  waiting for transfers between devices  28.9 us (21%)
  local copies, waits for them, and re-layouts  18 us (13%)
  Pallas kernels  9.72 us (7%)
  between operations  1.63 us (1%)
    all_to_all x4, blocking collectives, exchanged(): return lax.all_to_all(value, axes, split_axis=0, concat_axis=0, tiled=True)  45 us
    ppermute x4, waiting for transfers between devices, shifted(): return lax.ppermute(value, RIGHT, pairs)  14.4 us
    unnamed x44, local copies, waits for them, and re-layouts  13.3 us
    ppermute x4, starting transfers between devices, shifted(): return lax.ppermute(value, RIGHT, pairs)  13 us
    all_to_all x2, starting transfers between devices, exchanged(): return lax.all_to_all(value, axes, split_axis=0, concat_axis=0, tiled=True)  11.3 us
    all_to_all x2, waiting for transfers between devices, exchanged(): return lax.all_to_all(value, axes, split_axis=0, concat_axis=0, tiled=True)  10.7 us
    pallas_call x3, Pallas kernels, call(): pl.pallas_call(kernel, out_shape=shapes, in_specs=[pl.BlockSpec(memory_sp...  9.72 us
    ppermute x4, starting transfers between devices, swapped(): return lax.ppermute(value, 'c', [(0, 1), (1, 0)])  8.84 us
  transfers between devices with their start and end apart: 10, of which 7 were waited for; matrix products, arithmetic and copies ran while one was open for 4% of the time, Pallas kernels for 1%

profile of v1, /device:TPU:1, one launch (start us, length us, event | category | flops | bytes accessed | tf_op | source)
XLA Modules:
  0.0 137.3 jit_solution(90950213128666446)
XLA Ops:
  0.6 5.8 %collective-permute-start = (f32[384,400]{0,1:T(8,128)}, f32[384,400]{0,1:T(8,128)}, u32[]{:S(2)}, u32[]{:S(2)}) collective-permute-start(f32[384,400]{0,1:T(8,128)} %param.13), channel_id=1, source_target_pairs={{0,5},{1,6},{2,7},{3,8},{4,9},{5,10},{6,11},{7,12},{8,13},{9,14},{... | collective-permute-start | bytes 1843208 | tf_op jit(solution)/shard_map/ppermute | solution.py:156
  10.2 1.4 %copy.41.src_ref = f32[384,400]{1,0:T(8,128)S(1)} copy(f32[384,400]{0,1:T(8,128)} %param.11) | data formatting | bytes 1228800 | tf_op args[0]
  13.1 1.2 shard_map.138
  15.2 12.9 %collective-permute-done = f32[384,400]{0,1:T(8,128)} collective-permute-done((f32[384,400]{0,1:T(8,128)}, f32[384,400]{0,1:T(8,128)}, u32[]{:S(2)}, u32[]{:S(2)}) %collective-permute-start) | collective-permute-done | bytes 614432 | tf_op jit(solution)/shard_map/ppermute | solution.py:156
  28.1 1.3 copy.43.dst_ref
  29.5 1.1 copy-done.2
  30.6 3.9 %shard_map.139 = (f32[128,400]{1,0:T(8,128)S(1)}, f32[128,400]{1,0:T(8,128)S(1)}, f32[384,400]{1,0:T(8,128)S(1)}, f32[1,384]{1,0:T(1,128)S(1)}, f32[384,400]{1,0:T(8,128)S(1)}, /*index=5*/f32[1,384]{1,0:T(1,128)S(1)}) custom-call(f32[400,512]{1,0:T(8,128)S(1)} %get-tuple-element.18.sources_ref, f32[400,512]{1,0:T(8,128)S(1)} %copy-done.2, ...), custom_call_target="tpu_custom_call" | custom-call | tf_op jit(solution)/shard_map/pallas_call | solution.py:144
  36.3 1.5 %collective-permute-done.2 = f32[128,400]{1,0:T(8,128)S(1)} collective-permute-done((f32[128,400]{1,0:T(8,128)S(1)}, f32[128,400]{1,0:T(8,128)S(1)}, u32[]{:S(2)}, u32[]{:S(2)}) %collective-permute-start.2) | collective-permute-done | bytes 204832 | tf_op jit(solution)/shard_map/ppermute | solution.py:160
  37.9 12.4 %all_to_all.30 = f32[16,8,400]{2,1,0:T(8,128)S(1)} all-to-all(f32[16,8,400]{2,1,0:T(8,128)S(1)} %add_bitcast_fusion.1), channel_id=1, replica_groups=mesh['x'=4,'zh'=2,'y'=4,'zl'=4,'c'=2] {'x','y'}, dimensions={0} | all-to-all | bytes 409600 | tf_op jit(solution)/shard_map/all_to_all | solution.py:164
  51.0 8.0 %all-to-all-start.1 = ((f32[8,8,400]{2,1,0:T(8,128)}), f32[8,8,400]{2,1,0:T(8,128)S(1)}, u32[]{:S(2)}, u32[]{:S(2)}) async-start(f32[8,8,400]{2,1,0:T(8,128)} %broadcast_in_dim.23), calls=%async_computation.1 | async-start | bytes 262144 | tf_op jit(solution)/shard_map/all_to_all | solution.py:164
  59.3 7.8 %all-to-all-done.1 = f32[8,8,400]{2,1,0:T(8,128)S(1)} async-done(((f32[8,8,400]{2,1,0:T(8,128)}), f32[8,8,400]{2,1,0:T(8,128)S(1)}, u32[]{:S(2)}, u32[]{:S(2)}) %all-to-all-start.1) | async-done | bytes 102432 | tf_op jit(solution)/shard_map/all_to_all | solution.py:164
  67.7 10.8 %all_to_all.31 = f32[16,8,400]{2,1,0:T(8,128)S(1)} all-to-all(f32[16,8,400]{2,1,0:T(8,128)S(1)} %broadcast_in_dim.24), channel_id=1, replica_groups=mesh['x'=4,'zh'=2,'y'=4,'zl'=4,'c'=2] {'x','y'}, dimensions={0} | all-to-all | bytes 409600 | tf_op jit(solution)/shard_map/all_to_all | solution.py:164
  78.5 4.1 %collective-permute-start.3 = (f32[128,400]{1,0:T(8,128)S(1)}, f32[128,400]{1,0:T(8,128)S(1)}, u32[]{:S(2)}, u32[]{:S(2)}) collective-permute-start(f32[128,400]{1,0:T(8,128)S(1)} %bitcast.28), channel_id=1, source_target_pairs={{0,1},{1,0},{2,3},{3,2},{4,5},{5,4},{6,7},{7,6},{8,9},{9,8},{10,11... | collective-permute-start | bytes 614408 | tf_op jit(solution)/shard_map/ppermute | solution.py:160
  82.6 1.2 collective-permute-done.3.rel_other_ref
  83.8 4.6 %shard_map.140 = (f32[128,400]{1,0:T(8,128)S(1)}, f32[128,400]{1,0:T(8,128)S(1)}, f32[384,400]{1,0:T(8,128)S(1)}, f32[384,400]{1,0:T(8,128)S(1)}, f32[1,384]{1,0:T(1,128)S(1)}) custom-call(f32[128,400]{1,0:T(8,128)S(1)} %bitcast.29, f32[128,400]{1,0:T(8,128)S(1)} %collective-permute-done.3.rel_other_ref, f32[384,400]{1,0:T(8,128)S(1)} %copy-done.6, ...), custom_call_target="tpu_custom_call" | custom-call | tf_op jit(solution)/shard_map/pallas_call | solution.py:144
  89.7 1.2 collective-permute-done.6
  90.9 10.9 %all_to_all.32 = f32[16,8,400]{2,1,0:T(8,128)S(1)} all-to-all(f32[16,8,400]{2,1,0:T(8,128)S(1)} %add_bitcast_fusion), channel_id=1, replica_groups=mesh['x'=4,'zh'=2,'y'=4,'zl'=4,'c'=2] {'x','y'}, dimensions={0} | all-to-all | bytes 409600 | tf_op jit(solution)/shard_map/all_to_all | solution.py:164
  102.5 3.4 %all-to-all-start.4 = ((f32[8,8,400]{2,1,0:T(8,128)}), f32[8,8,400]{2,1,0:T(8,128)S(1)}, u32[]{:S(2)}, u32[]{:S(2)}) async-start(f32[8,8,400]{2,1,0:T(8,128)} %broadcast_in_dim.25), calls=%async_computation.4 | async-start | bytes 262144 | tf_op jit(solution)/shard_map/all_to_all | solution.py:164
  106.1 4.8 %collective-permute-start.4 = (f32[384,400]{0,1:T(8,128)S(1)}, f32[384,400]{0,1:T(8,128)S(1)}, u32[]{:S(2)}, u32[]{:S(2)}) collective-permute-start(f32[384,400]{0,1:T(8,128)S(1)} %copy.46), channel_id=1, source_target_pairs={{0,27},{1,28},{2,29},{3,30},{4,31},{5,0},{6,1},{7,2},{8,3},{9,4},{... | collective-permute-start | bytes 1843208 | tf_op jit(solution)/shard_map/ppermute | solution.py:156
  110.9 2.9 %all-to-all-done.4 = f32[8,8,400]{2,1,0:T(8,128)S(1)} async-done(((f32[8,8,400]{2,1,0:T(8,128)}), f32[8,8,400]{2,1,0:T(8,128)S(1)}, u32[]{:S(2)}, u32[]{:S(2)}) %all-to-all-start.4) | async-done | bytes 102432 | tf_op jit(solution)/shard_map/all_to_all | solution.py:164
  113.9 10.9 %all_to_all.33 = f32[16,8,400]{2,1,0:T(8,128)S(1)} all-to-all(f32[16,8,400]{2,1,0:T(8,128)S(1)} %broadcast_in_dim.26), channel_id=1, replica_groups=mesh['x'=4,'zh'=2,'y'=4,'zl'=4,'c'=2] {'x','y'}, dimensions={0} | all-to-all | bytes 409600 | tf_op jit(solution)/shard_map/all_to_all | solution.py:164
  124.7 4.4 %collective-permute-start.7 = (f32[128,400]{1,0:T(8,128)S(1)}, f32[128,400]{1,0:T(8,128)S(1)}, u32[]{:S(2)}, u32[]{:S(2)}) collective-permute-start(f32[128,400]{1,0:T(8,128)S(1)} %bitcast.30), channel_id=1, source_target_pairs={{0,1},{1,0},{2,3},{3,2},{4,5},{5,4},{6,7},{7,6},{8,9},{9,8},{10,11... | collective-permute-start | bytes 614408 | tf_op jit(solution)/shard_map/ppermute | solution.py:160
  129.1 2.3 %collective-permute-start.5 = (f32[1,384]{1,0:T(1,128)S(1)}, f32[1,384]{1,0:T(1,128)S(1)}, u32[]{:S(2)}, u32[]{:S(2)}) collective-permute-start(f32[1,384]{1,0:T(1,128)S(1)} %get-tuple-element.29), channel_id=1, source_target_pairs={{0,27},{1,28},{2,29},{3,30},{4,31},{5,0},{6,1},{7,2},{8,3},{9,4},{... | collective-permute-start | bytes 4616 | tf_op jit(solution)/shard_map/ppermute | solution.py:156
  132.5 1.4 %collective-permute-done.5 = f32[1,384]{1,0:T(1,128)S(1)} collective-permute-done((f32[1,384]{1,0:T(1,128)S(1)}, f32[1,384]{1,0:T(1,128)S(1)}, u32[]{:S(2)}, u32[]{:S(2)}) %collective-permute-start.5) | collective-permute-done | bytes 1568 | tf_op jit(solution)/shard_map/ppermute | solution.py:156
  (87 shorter events, 15.5 us)
Async XLA Ops:
  0.6 58.4 %copy-start = (f32[256,400]{0,1:T(8,128)S(1)}, f32[256,400]{0,1:T(8,128)}, u32[]{:S(2)}) copy-start(f32[256,400]{0,1:T(8,128)} %param.16) | copy-start | bytes 1228804
  0.6 27.4 %collective-permute-start = (f32[384,400]{0,1:T(8,128)}, f32[384,400]{0,1:T(8,128)}, u32[]{:S(2)}, u32[]{:S(2)}) collective-permute-start(f32[384,400]{0,1:T(8,128)} %param.13), channel_id=1, source_target_pairs={{0,5},{1,6},{2,7},{3,8},{4,9},{5,10},{6,11},{7,12},{8,13},{9,14},{... | collective-permute-start | bytes 1843208 | tf_op jit(solution)/shard_map/ppermute | solution.py:156
  7.1 22.3 %collective-permute-start.1 = (f32[1,384]{1,0:T(1,128)S(1)}, f32[1,384]{1,0:T(1,128)S(1)}, u32[]{:S(2)}, u32[]{:S(2)}) collective-permute-start(f32[1,384]{1,0:T(1,128)S(1)} %reshape.38), channel_id=1, source_target_pairs={{0,5},{1,6},{2,7},{3,8},{4,9},{5,10},{6,11},{7,12},{8,13},{9,14},{... | collective-permute-start | bytes 4616 | tf_op jit(solution)/shard_map/ppermute | solution.py:156
  7.9 0.7 copy-start.16
  10.2 1.4 %copy-start.11 = (f32[256,400]{0,1:T(8,128)S(1)}, f32[256,400]{0,1:T(8,128)}, u32[]{:S(2)}) copy-start(f32[256,400]{0,1:T(8,128)} %param.15) | copy-start | bytes 1228804
  14.3 0.9 copy-start.1
  29.4 1.1 copy-start.2
  34.5 0.9 copy-start.3
  35.4 0.9 copy-start.5
  36.3 1.5 %collective-permute-start.2 = (f32[128,400]{1,0:T(8,128)S(1)}, f32[128,400]{1,0:T(8,128)S(1)}, u32[]{:S(2)}, u32[]{:S(2)}) collective-permute-start(f32[128,400]{1,0:T(8,128)S(1)} %get-tuple-element.22), channel_id=1, source_target_pairs={{0,1},{1,0},{2,3},{3,2},{4,5},{5,4},{6,7},{7,6},{8,9},{9,8},{10,11... | collective-permute-start | bytes 614408 | tf_op jit(solution)/shard_map/ppermute | solution.py:160
  51.0 16.0 %all-to-all-start.1 = ((f32[8,8,400]{2,1,0:T(8,128)}), f32[8,8,400]{2,1,0:T(8,128)S(1)}, u32[]{:S(2)}, u32[]{:S(2)}) async-start(f32[8,8,400]{2,1,0:T(8,128)} %broadcast_in_dim.23), calls=%async_computation.1 | async-start | bytes 262144 | tf_op jit(solution)/shard_map/all_to_all | solution.py:164
  59.0 24.7 %copy-start.4 = (f32[384,400]{1,0:T(8,128)S(1)}, f32[384,400]{1,0:T(8,128)}, u32[]{:S(2)}) copy-start(f32[384,400]{1,0:T(8,128)} %copy-done.3) | copy-start | bytes 1843204
  59.0 24.7 %copy-start.6 = (f32[384,400]{1,0:T(8,128)S(1)}, f32[384,400]{1,0:T(8,128)}, u32[]{:S(2)}) copy-start(f32[384,400]{1,0:T(8,128)} %copy-done.5) | copy-start | bytes 1843204
  78.5 5.3 %collective-permute-start.3 = (f32[128,400]{1,0:T(8,128)S(1)}, f32[128,400]{1,0:T(8,128)S(1)}, u32[]{:S(2)}, u32[]{:S(2)}) collective-permute-start(f32[128,400]{1,0:T(8,128)S(1)} %bitcast.28), channel_id=1, source_target_pairs={{0,1},{1,0},{2,3},{3,2},{4,5},{5,4},{6,7},{7,6},{8,9},{9,8},{10,11... | collective-permute-start | bytes 614408 | tf_op jit(solution)/shard_map/ppermute | solution.py:160
  88.4 0.9 copy-start.7
  89.3 1.5 %collective-permute-start.6 = (f32[128,400]{1,0:T(8,128)S(1)}, f32[128,400]{1,0:T(8,128)S(1)}, u32[]{:S(2)}, u32[]{:S(2)}) collective-permute-start(f32[128,400]{1,0:T(8,128)S(1)} %get-tuple-element.31), channel_id=1, source_target_pairs={{0,1},{1,0},{2,3},{3,2},{4,5},{5,4},{6,7},{7,6},{8,9},{9,8},{10,11... | collective-permute-start | bytes 614408 | tf_op jit(solution)/shard_map/ppermute | solution.py:160
  90.9 15.0 %copy-start.8 = (f32[384,400]{1,0:T(8,128)S(1)}, f32[384,400]{1,0:T(8,128)}, u32[]{:S(2)}) copy-start(f32[384,400]{1,0:T(8,128)} %copy-done.7) | copy-start | bytes 1843204
  102.5 11.3 %all-to-all-start.4 = ((f32[8,8,400]{2,1,0:T(8,128)}), f32[8,8,400]{2,1,0:T(8,128)S(1)}, u32[]{:S(2)}, u32[]{:S(2)}) async-start(f32[8,8,400]{2,1,0:T(8,128)} %broadcast_in_dim.25), calls=%async_computation.4 | async-start | bytes 262144 | tf_op jit(solution)/shard_map/all_to_all | solution.py:164
  106.1 7.7 %copy-start.13 = (f32[8,400]{1,0:T(8,128)S(1)}, f32[8,400]{1,0:T(8,128)}, u32[]{:S(2)}) copy-start(f32[8,400]{1,0:T(8,128)} %copy-done.12) | copy-start | bytes 38404
  106.1 28.4 %collective-permute-start.4 = (f32[384,400]{0,1:T(8,128)S(1)}, f32[384,400]{0,1:T(8,128)S(1)}, u32[]{:S(2)}, u32[]{:S(2)}) collective-permute-start(f32[384,400]{0,1:T(8,128)S(1)} %copy.46), channel_id=1, source_target_pairs={{0,27},{1,28},{2,29},{3,30},{4,31},{5,0},{6,1},{7,2},{8,3},{9,4},{... | collective-permute-start | bytes 1843208 | tf_op jit(solution)/shard_map/ppermute | solution.py:156
  124.7 10.6 %collective-permute-start.7 = (f32[128,400]{1,0:T(8,128)S(1)}, f32[128,400]{1,0:T(8,128)S(1)}, u32[]{:S(2)}, u32[]{:S(2)}) collective-permute-start(f32[128,400]{1,0:T(8,128)S(1)} %bitcast.30), channel_id=1, source_target_pairs={{0,1},{1,0},{2,3},{3,2},{4,5},{5,4},{6,7},{7,6},{8,9},{9,8},{10,11... | collective-permute-start | bytes 614408 | tf_op jit(solution)/shard_map/ppermute | solution.py:160
  129.1 4.8 %collective-permute-start.5 = (f32[1,384]{1,0:T(1,128)S(1)}, f32[1,384]{1,0:T(1,128)S(1)}, u32[]{:S(2)}, u32[]{:S(2)}) collective-permute-start(f32[1,384]{1,0:T(1,128)S(1)} %get-tuple-element.29), channel_id=1, source_target_pairs={{0,27},{1,28},{2,29},{3,30},{4,31},{5,0},{6,1},{7,2},{8,3},{9,4},{... | collective-permute-start | bytes 4616 | tf_op jit(solution)/shard_map/ppermute | solution.py:156
  134.5 0.8 copy-start.9
  135.4 1.1 copy-start.10
  (6 other events, 4.1 us)

commit v2 on v1

v2 whole, which is shorter than its diff:
```python
import jax
import jax.numpy as jnp
from jax import lax
from jax.experimental import pallas as pl
from jax.experimental.pallas import tpu as pltpu
from jax.sharding import Mesh, PartitionSpec as P

BATCH = 500
BATCHES = 2
NEG = 1000
SHIFT = 5
SLAB = 384
REL = 256
HALF = 128
W = 400
MID = 200
EP = 512
NP = 1024

ROW_RATE = 0.2
REL_RATE = 1.0

AXES = ("x", "zh", "y", "zl", "c")
PLANE = ("x", "y")
COLUMN = ("zh", "zl")
RIGHT = ("y", "zl", "c")

NN = (((1,), (0,)), ((), ()))
NT = (((1,), (1,)), ((), ()))
TN = (((0,), (0,)), ((), ()))


def parts(value):
    high = value.astype(jnp.bfloat16)
    low = (value - high.astype(jnp.float32)).astype(jnp.bfloat16)
    return (high, low)


def dot(first, second, dims):
    return lax.dot_general(first, second, dims, preferred_element_type=jnp.float32)


def dot3(first, second, dims):
    return (
        dot(first[0], second[0], dims) + dot(first[0], second[1], dims) + dot(first[1], second[0], dims)
    )


def pick(rows, ids):
    return (lax.broadcasted_iota(jnp.int32, (rows, EP), 0) == ids).astype(jnp.bfloat16)


def gather(table, hot):
    high, low = parts(table)
    return dot(high, hot, NN) + dot(low, hot, NN)


def scatter(values, hot):
    high, low = parts(values)
    return dot(high, hot, NT) + dot(low, hot, NT)


def entity_update(table, state, grad):
    state = state + jnp.sum(grad * grad, axis=0, keepdims=True) * (1.0 / W)
    return (table - grad * (ROW_RATE / jnp.sqrt(state)), state)


def bucket(sources, relations, table, src_hot, dst_ids, rel_hot, src_ids, counts):
    s_re, s_im = (sources[:MID], sources[MID:])
    r_re, r_im = (relations[:MID], relations[MID:])
    queries = parts(jnp.concatenate([s_re * r_re - s_im * r_im, s_re * r_im + s_im * r_re], axis=0))
    rows = parts(table)
    logits = dot3(rows, queries, TN)
    tail = jnp.exp(-jnp.abs(logits))
    scale = jnp.where(src_ids >= 0, 1.0, 0.0) / (1.0 + tail)
    above = logits >= 0.0
    negative = jnp.where(above, 1.0, tail) * counts
    hit = lax.broadcasted_iota(jnp.int32, (SLAB, EP), 0) == dst_ids
    positive = jnp.where(hit, jnp.where(above, tail, 1.0), 0.0)
    weights = parts((negative - positive) * scale)
    grads = dot3(rows, weights, NN)
    g_re, g_im = (grads[:MID], grads[MID:])
    rho_grad = jnp.concatenate([g_re * s_re + g_im * s_im, g_im * s_re - g_re * s_im], axis=0)
    rel_grad = scatter(rho_grad, rel_hot)
    src_grad = jnp.concatenate([g_re * r_re + g_im * r_im, g_im * r_re - g_re * r_im], axis=0)
    src_grad = scatter(src_grad, src_hot)
    dst_grad = dot3(queries, weights, NT)
    return (rel_grad, src_grad, dst_grad)


def put_halves(grad, mine_ref, other_ref):
    for ref, low in ((mine_ref, 0), (other_ref, HALF)):
        ref[:W, :] = grad[:, low : low + HALF]
        ref[W:, :] = jnp.zeros((EP - W, HALF), jnp.float32)


def prepare_kernel(
    place_ref, src_ref, rel_ref, rel_state_ref, ids_ref, neg_ref,
    sources_ref, relations_ref, counts_ref, own_ref, own_sums_ref, wide_ref,
):
    sources_ref[...] = gather(src_ref[...], pick(SLAB, ids_ref[0:1, :]))
    relations_ref[...] = gather(rel_ref[...], pick(REL, ids_ref[4:5, :]))
    for batch in range(BATCHES):
        same = lax.broadcasted_iota(jnp.int32, (SLAB, NP), 0) == neg_ref[batch : batch + 1, :]
        total = jnp.sum(jnp.where(same, 1.0, 0.0), axis=1, keepdims=True)
        counts_ref[:, batch : batch + 1] = total * (1.0 / NEG)
    height = own_ref.shape[0]
    wide_ref[W:, :] = jnp.ones((EP - W, HALF), jnp.float32)
    for source, target in ((rel_ref, own_ref), (rel_state_ref, own_sums_ref)):
        wide_ref[:W, :] = jnp.where(place_ref[0] == 0, source[:, :HALF], source[:, HALF:])
        target[...] = wide_ref[pl.ds(pl.multiple_of(place_ref[1] * height, height), height), :]


def first_kernel(
    sources_ref, relations_ref, dst_ref, dst_state_ref, src_ref, src_state_ref, ids_ref, counts_ref,
    mine_ref, other_ref, src_out, src_state_out, dst_out, dst_state_out,
):
    rel_grad, src_grad, dst_grad = bucket(
        sources_ref[...], relations_ref[...], dst_ref[...], pick(SLAB, ids_ref[0:1, :]), ids_ref[2:3, :],
        pick(REL, ids_ref[5:6, :]), ids_ref[0:1, :], counts_ref[:, 0:1],
    )
    put_halves(rel_grad, mine_ref, other_ref)
    src_out[...], src_state_out[...] = entity_update(src_ref[...], src_state_ref[...], src_grad)
    dst_out[...], dst_state_out[...] = entity_update(dst_ref[...], dst_state_ref[...], dst_grad)


def second_kernel(
    rel_mine_ref, rel_other_ref, dst_ref, dst_state_ref, src_ref, src_state_ref, ids_ref, counts_ref,
    mine_ref, other_ref, src_out, dst_out, dst_state_out,
):
    src_hot = pick(SLAB, ids_ref[1:2, :])
    rel_hot = pick(REL, ids_ref[6:7, :])
    relation = jnp.concatenate([rel_mine_ref[:W, :], rel_other_ref[:W, :]], axis=1)
    rel_grad, src_grad, dst_grad = bucket(
        gather(src_ref[...], src_hot), gather(relation, rel_hot), dst_ref[...], src_hot, ids_ref[3:4, :],
        rel_hot, ids_ref[1:2, :], counts_ref[:, 1:2],
    )
    put_halves(rel_grad, mine_ref, other_ref)
    src_out[...], _ = entity_update(src_ref[...], src_state_ref[...], src_grad)
    dst_out[...], dst_state_out[...] = entity_update(dst_ref[...], dst_state_ref[...], dst_grad)


def call(kernel, outs, *args, scalars=0, scratch=()):
    shapes = [jax.ShapeDtypeStruct(shape, jnp.float32) for shape in outs]
    vector = pl.BlockSpec(memory_space=pltpu.VMEM)
    scalar = pl.BlockSpec(memory_space=pltpu.SMEM)
    return pl.pallas_call(
        kernel,
        out_shape=shapes,
        in_specs=[scalar] * scalars + [vector] * (len(args) - scalars),
        out_specs=[vector] * len(shapes),
        scratch_shapes=scratch,
        compiler_params=pltpu.CompilerParams(vmem_limit_bytes=20 * 1024 * 1024),
    )(*args)


def shifted(value, steps):
    count = lax.axis_size(RIGHT)
    pairs = [(source, (source + steps) % count) for source in range(count)]
    return lax.ppermute(value, RIGHT, pairs)


def swapped(value):
    return lax.ppermute(value, "c", [(0, 1), (1, 0)])


def exchanged(value, axes):
    return lax.all_to_all(value, axes, split_axis=0, concat_axis=0, tiled=True)


def relation_update(mine, other, own, own_sums):
    lanes, layers = (lax.axis_size(PLANE), lax.axis_size(COLUMN))
    half = mine + swapped(other)
    total = jnp.sum(exchanged(half.reshape(lanes, *own.shape), PLANE), axis=0)
    total = jnp.sum(exchanged(jnp.broadcast_to(total, (layers, *own.shape)), COLUMN), axis=0)
    own_sums = own_sums + total * total
    own = own - REL_RATE * total / jnp.sqrt(own_sums)
    half = exchanged(jnp.broadcast_to(own, (lanes, *own.shape)), PLANE).reshape(EP, HALF)
    return (half, swapped(half), own, own_sums)


def padded(value, live, low):
    picked = value[low : low + BATCH]
    spot = lax.iota(jnp.int32, BATCH) + low
    return jnp.pad(jnp.where(spot < live, picked, -1), (0, EP - BATCH), constant_values=-1)


def body(
    src_embed, src_state, dst_embed, dst_state, relation, rel_state, edge_src, edge_dst, edge_rel, neg_rows, edge_count
):
    dst_table, dst_sums = (shifted(dst_embed.T, SHIFT), shifted(dst_state.reshape(1, SLAB), SHIFT))
    core = lax.axis_index("c")
    live = edge_count[0]
    near_rel = edge_rel[0] ^ (core * HALF)
    ids = jnp.stack(
        [
            padded(edge_src[0], live, 0),
            padded(edge_src[0], live, BATCH),
            padded(edge_dst[0], live, 0),
            padded(edge_dst[0], live, BATCH),
            padded(edge_rel[0], live, 0),
            padded(near_rel, live, 0),
            padded(near_rel, live, BATCH),
            jnp.full((EP,), -1, jnp.int32),
        ]
    )
    negs = jnp.pad(neg_rows[0], ((0, 0), (0, NP - NEG)), constant_values=-1)
    place = jnp.stack([core, lax.axis_index(PLANE)]).astype(jnp.int32)
    height = EP // lax.axis_size(PLANE)
    src_table, src_sums = (src_embed.T, src_state.reshape(1, SLAB))

    sources, relations, counts, own, own_sums = call(
        prepare_kernel,
        [(W, EP), (W, EP), (SLAB, BATCHES), (height, HALF), (height, HALF)],
        place, src_table, relation.T, rel_state.T, ids, negs,
        scalars=1,
        scratch=[pltpu.VMEM((EP, HALF), jnp.float32)],
    )
    mine, other, src_table, src_sums, dst_table, dst_sums = call(
        first_kernel,
        [(EP, HALF), (EP, HALF), (W, SLAB), (1, SLAB), (W, SLAB), (1, SLAB)],
        sources, relations, dst_table, dst_sums, src_table, src_sums, ids, counts,
    )
    near, far, own, own_sums = relation_update(mine, other, own, own_sums)
    mine, other, src_table, dst_table, dst_sums = call(
        second_kernel,
        [(EP, HALF), (EP, HALF), (W, SLAB), (W, SLAB), (1, SLAB)],
        near, far, dst_table, dst_sums, src_table, src_sums, ids, counts,
    )
    dst_table, dst_sums = (shifted(dst_table, -SHIFT), shifted(dst_sums, -SHIFT))
    near, far, own, own_sums = relation_update(mine, other, own, own_sums)
    first = core == 0
    relation = jnp.concatenate([jnp.where(first, near, far), jnp.where(first, far, near)], axis=1)
    return (src_table.T, dst_table.T, dst_sums.reshape(SLAB), relation[:W].T)


def solution(mesh):
    left, right = (mesh.shape["left"], mesh.shape["right"])
    devices = mesh.devices.reshape(left // 2, 2, 4, right // 8, 2)
    inner = Mesh(devices, AXES)
    in_specs = (
        P(AXES, None),
        P(AXES),
        P(AXES, None),
        P(AXES),
        P(),
        P(),
        P(AXES, None),
        P(AXES, None),
        P(AXES, None),
        P(AXES, None, None),
        P(AXES),
    )
    out_specs = (P(AXES, None), P(AXES, None), P(AXES), P())
    return jax.shard_map(body, mesh=inner, in_specs=in_specs, out_specs=out_specs, check_vma=False)
```

time: 138 us -> 141 us (1.022)
  blocking collectives: 45 us -> 59.1 us
  local copies, waits for them, and re-layouts: 18 us -> 8.86 us
  starting transfers between devices: 33.2 us -> 25.7 us
  waiting for transfers between devices: 28.9 us -> 32.8 us
    all_to_all x4 -> x5, blocking collectives: 45 us -> 59.1 us  [exchanged(): return lax.all_to_all(value, axes, split_axis=0, concat_axis=0, tiled=True)]
    ppermute x4, waiting for transfers between devices: 14.4 us -> 25.7 us  [shifted(): return lax.ppermute(value, RIGHT, pairs)]
    all_to_all x2 -> x1, starting transfers between devices: 11.3 us -> 3.37 us  [exchanged(): return lax.all_to_all(value, axes, split_axis=0, concat_axis=0, tiled=True)]
    all_to_all x2 -> x1, waiting for transfers between devices: 10.7 us -> 3.23 us  [exchanged(): return lax.all_to_all(value, axes, split_axis=0, concat_axis=0, tiled=True)]
    unnamed x44 -> x19, local copies, waits for them, and re-layouts: 13.3 us -> 6.48 us
  transfers between devices with their start and end apart: 10 -> 9, of which waited for: 7 -> 6; matrix products, arithmetic and copies ran while one was open for 4% -> 1% of each run, Pallas kernels for 1% -> 1%
where the time goes in v2:
time: 141 us; the launch traced here: 140 us
  blocking collectives  59.1 us (42%)
  waiting for transfers between devices  32.8 us (23%)
  starting transfers between devices  25.7 us (18%)
  Pallas kernels  10.3 us (7%)
  local copies, waits for them, and re-layouts  8.86 us (6%)
  other arithmetic  1.67 us (1%)
  between operations  1.5 us (1%)
    all_to_all x5, blocking collectives, exchanged(): return lax.all_to_all(value, axes, split_axis=0, concat_axis=0, tiled=True)  59.1 us
    ppermute x4, waiting for transfers between devices, shifted(): return lax.ppermute(value, RIGHT, pairs)  25.7 us
    ppermute x4, starting transfers between devices, shifted(): return lax.ppermute(value, RIGHT, pairs)  13 us
    pallas_call x3, Pallas kernels, call(): pl.pallas_call(kernel, out_shape=shapes, in_specs=[scalar] * scalars + [v...  10.3 us
    ppermute x4, starting transfers between devices, swapped(): return lax.ppermute(value, 'c', [(0, 1), (1, 0)])  9.34 us
    unnamed x19, local copies, waits for them, and re-layouts  6.48 us
    ppermute x4, waiting for transfers between devices, swapped(): return lax.ppermute(value, 'c', [(0, 1), (1, 0)])  3.85 us
    all_to_all x1, starting transfers between devices, exchanged(): return lax.all_to_all(value, axes, split_axis=0, concat_axis=0, tiled=True)  3.37 us
  transfers between devices with their start and end apart: 9, of which 6 were waited for; matrix products, arithmetic and copies ran while one was open for 1% of the time, Pallas kernels for 1%

profile of v2, /device:TPU:1, one launch (start us, length us, event | category | flops | bytes accessed | tf_op | source)
XLA Modules:
  0.0 139.9 jit_solution(9580274001777803876)
XLA Ops:
  1.3 5.7 %collective-permute-start.1 = (f32[1,384]{1,0:T(1,128)S(1)}, f32[1,384]{1,0:T(1,128)S(1)}, u32[]{:S(2)}, u32[]{:S(2)}) collective-permute-start(f32[1,384]{1,0:T(1,128)S(1)} %reshape.38), channel_id=1, source_target_pairs={{0,5},{1,6},{2,7},{3,8},{4,9},{5,10},{6,11},{7,12},{8,13},{9,14},{... | collective-permute-start | bytes 4616 | tf_op jit(solution)/shard_map/ppermute | solution.py:160
  11.6 1.1 copy-done
  12.7 1.0 copy-done.2
  13.7 1.0 copy-done.3
  14.7 1.6 %shard_map.138 = (f32[400,512]{1,0:T(8,128)S(1)}, f32[400,512]{1,0:T(8,128)S(1)}, f32[384,2]{1,0:T(8,128)S(1)}, f32[32,128]{1,0:T(8,128)S(1)}, f32[32,128]{1,0:T(8,128)S(1)}) custom-call(s32[2]{0:T(128)S(1)} %pad_add_fusion.place_ref, f32[400,384]{1,0:T(8,128)S(1)} %bitcast.36, f32[400,256]{1,0:T(8,128)S(1)} %bitcast.40, f32[400,256]{1,0:T(8,128)S(1)} %bitcast.41, ...), custom_call_target="tpu_custom_call" | custom-call | tf_op jit(solution)/shard_map/pallas_call | solution.py:147
  16.3 14.8 %collective-permute-done.dst_ref = f32[400,384]{1,0:T(8,128)S(1)} collective-permute-done((f32[400,384]{1,0:T(8,128)}, f32[400,384]{1,0:T(8,128)S(1)}, u32[]{:S(2)}, u32[]{:S(2)}) %collective-permute-start) | collective-permute-done | bytes 614432 | tf_op jit(solution)/shard_map/ppermute | solution.py:160
  31.0 4.0 %shard_map.139 = (f32[512,128]{1,0:T(8,128)S(1)}, f32[512,128]{1,0:T(8,128)S(1)}, f32[400,384]{1,0:T(8,128)S(1)}, f32[1,384]{1,0:T(1,128)S(1)}, f32[400,384]{1,0:T(8,128)S(1)}, /*index=5*/f32[1,384]{1,0:T(1,128)S(1)}) custom-call(f32[400,512]{1,0:T(8,128)S(1)} %get-tuple-element.21.sources_ref, f32[400,512]{1,0:T(8,128)S(1)} %get-tuple-element.22.relations_ref, ...), custom_call_target="tpu_custom_call" | custom-call | tf_op jit(solution)/shard_map/pallas_call | solution.py:147
  35.2 1.5 %collective-permute-done.2 = f32[512,128]{1,0:T(8,128)S(1)} collective-permute-done((f32[512,128]{1,0:T(8,128)S(1)}, f32[512,128]{1,0:T(8,128)S(1)}, u32[]{:S(2)}, u32[]{:S(2)}) %collective-permute-start.2) | collective-permute-done | bytes 262176 | tf_op jit(solution)/shard_map/ppermute | solution.py:164
  36.7 13.0 %all_to_all.30 = f32[16,32,128]{2,1,0:T(8,128)S(1)} all-to-all(f32[16,32,128]{2,1,0:T(8,128)S(1)} %bitcast.42), channel_id=1, replica_groups=mesh['x'=4,'zh'=2,'y'=4,'zl'=4,'c'=2] {'x','y'}, dimensions={0} | all-to-all | bytes 524288 | tf_op jit(solution)/shard_map/all_to_all | solution.py:168
  49.7 13.7 %all_to_all.31 = f32[8,32,128]{2,1,0:T(8,128)S(1)} all-to-all(f32[8,32,128]{2,1,0:T(8,128)S(1)} %broadcast_in_dim.23), channel_id=1, replica_groups=mesh['x'=4,'zh'=2,'y'=4,'zl'=4,'c'=2] {'zh','zl'}, dimensions={0} | all-to-all | bytes 262144 | tf_op jit(solution)/shard_map/all_to_all | solution.py:168
  63.5 10.8 %all_to_all.32 = f32[16,32,128]{2,1,0:T(8,128)S(1)} all-to-all(f32[16,32,128]{2,1,0:T(8,128)S(1)} %broadcast_in_dim.24), channel_id=1, replica_groups=mesh['x'=4,'zh'=2,'y'=4,'zl'=4,'c'=2] {'x','y'}, dimensions={0} | all-to-all | bytes 524288 | tf_op jit(solution)/shard_map/all_to_all | solution.py:168
  74.3 4.1 %collective-permute-start.3 = (f32[512,128]{1,0:T(8,128)S(1)}, f32[512,128]{1,0:T(8,128)S(1)}, u32[]{:S(2)}, u32[]{:S(2)}) collective-permute-start(f32[512,128]{1,0:T(8,128)S(1)} %bitcast.38), channel_id=1, source_target_pairs={{0,1},{1,0},{2,3},{3,2},{4,5},{5,4},{6,7},{7,6},{8,9},{9,8},{10,11... | collective-permute-start | bytes 786440 | tf_op jit(solution)/shard_map/ppermute | solution.py:164
  78.4 1.2 collective-permute-done.3.rel_other_ref
  79.5 4.7 %shard_map.140 = (f32[512,128]{1,0:T(8,128)S(1)}, f32[512,128]{1,0:T(8,128)S(1)}, f32[400,384]{1,0:T(8,128)}, f32[400,384]{1,0:T(8,128)S(1)}, f32[1,384]{1,0:T(1,128)S(1)}) custom-call(f32[512,128]{1,0:T(8,128)S(1)} %bitcast.39, f32[512,128]{1,0:T(8,128)S(1)} %collective-permute-done.3.rel_other_ref, f32[400,384]{1,0:T(8,128)S(1)} %get-tuple-element.27.dst_ref, ...), custom_call_target="tpu_custom_call" | custom-call | tf_op jit(solution)/shard_map/pallas_call | solution.py:147
  84.9 1.2 collective-permute-done.6
  86.1 10.8 %all_to_all.33 = f32[16,32,128]{2,1,0:T(8,128)S(1)} all-to-all(f32[16,32,128]{2,1,0:T(8,128)S(1)} %bitcast.43), channel_id=1, replica_groups=mesh['x'=4,'zh'=2,'y'=4,'zl'=4,'c'=2] {'x','y'}, dimensions={0} | all-to-all | bytes 524288 | tf_op jit(solution)/shard_map/all_to_all | solution.py:168
  97.5 3.4 %all-to-all-start.4 = ((f32[8,32,128]{2,1,0:T(8,128)}), f32[8,32,128]{2,1,0:T(8,128)S(1)}, u32[]{:S(2)}, u32[]{:S(2)}) async-start(f32[8,32,128]{2,1,0:T(8,128)} %broadcast_in_dim.25), calls=%async_computation.4 | async-start | bytes 262144 | tf_op jit(solution)/shard_map/all_to_all | solution.py:168
  100.9 4.7 %collective-permute-start.4 = (f32[400,384]{1,0:T(8,128)S(1)}, f32[400,384]{1,0:T(8,128)S(1)}, u32[]{:S(2)}, u32[]{:S(2)}) collective-permute-start(f32[400,384]{1,0:T(8,128)S(1)} %get-tuple-element.32), channel_id=1, source_target_pairs={{0,27},{1,28},{2,29},{3,30},{4,31},{5,0},{6,1},{7,2},{8,3},{9,4},{... | collective-permute-start | bytes 1843208 | tf_op jit(solution)/shard_map/ppermute | solution.py:160
  105.6 3.2 %all-to-all-done.4 = f32[8,32,128]{2,1,0:T(8,128)S(1)} async-done(((f32[8,32,128]{2,1,0:T(8,128)}), f32[8,32,128]{2,1,0:T(8,128)S(1)}, u32[]{:S(2)}, u32[]{:S(2)}) %all-to-all-start.4) | async-done | bytes 131104 | tf_op jit(solution)/shard_map/all_to_all | solution.py:168
  108.9 10.9 %all_to_all.34 = f32[16,32,128]{2,1,0:T(8,128)S(1)} all-to-all(f32[16,32,128]{2,1,0:T(8,128)S(1)} %broadcast_in_dim.26), channel_id=1, replica_groups=mesh['x'=4,'zh'=2,'y'=4,'zl'=4,'c'=2] {'x','y'}, dimensions={0} | all-to-all | bytes 524288 | tf_op jit(solution)/shard_map/all_to_all | solution.py:168
  119.8 4.5 %collective-permute-start.7 = (f32[512,128]{1,0:T(8,128)S(1)}, f32[512,128]{1,0:T(8,128)S(1)}, u32[]{:S(2)}, u32[]{:S(2)}) collective-permute-start(f32[512,128]{1,0:T(8,128)S(1)} %bitcast.44), channel_id=1, source_target_pairs={{0,1},{1,0},{2,3},{3,2},{4,5},{5,4},{6,7},{7,6},{8,9},{9,8},{10,11... | collective-permute-start | bytes 786440 | tf_op jit(solution)/shard_map/ppermute | solution.py:164
  124.3 2.5 %collective-permute-start.5 = (f32[1,384]{1,0:T(1,128)S(1)}, f32[1,384]{1,0:T(1,128)S(1)}, u32[]{:S(2)}, u32[]{:S(2)}) collective-permute-start(f32[1,384]{1,0:T(1,128)S(1)} %get-tuple-element.33), channel_id=1, source_target_pairs={{0,27},{1,28},{2,29},{3,30},{4,31},{5,0},{6,1},{7,2},{8,3},{9,4},{... | collective-permute-start | bytes 4616 | tf_op jit(solution)/shard_map/ppermute | solution.py:160
  126.8 10.9 %collective-permute-done.5 = f32[1,384]{1,0:T(1,128)S(1)} collective-permute-done((f32[1,384]{1,0:T(1,128)S(1)}, f32[1,384]{1,0:T(1,128)S(1)}, u32[]{:S(2)}, u32[]{:S(2)}) %collective-permute-start.5) | collective-permute-done | bytes 1568 | tf_op jit(solution)/shard_map/ppermute | solution.py:160
  139.1 0.8 copy.17
  (59 shorter events, 7.5 us)
Async XLA Ops:
  1.3 15.0 %collective-permute-start.1 = (f32[1,384]{1,0:T(1,128)S(1)}, f32[1,384]{1,0:T(1,128)S(1)}, u32[]{:S(2)}, u32[]{:S(2)}) collective-permute-start(f32[1,384]{1,0:T(1,128)S(1)} %reshape.38), channel_id=1, source_target_pairs={{0,5},{1,6},{2,7},{3,8},{4,9},{5,10},{6,11},{7,12},{8,13},{9,14},{... | collective-permute-start | bytes 4616 | tf_op jit(solution)/shard_map/ppermute | solution.py:160
  7.0 24.0 %collective-permute-start = (f32[400,384]{1,0:T(8,128)}, f32[400,384]{1,0:T(8,128)S(1)}, u32[]{:S(2)}, u32[]{:S(2)}) collective-permute-start(f32[400,384]{1,0:T(8,128)} %bitcast.61), channel_id=1, source_target_pairs={{0,5},{1,6},{2,7},{3,8},{4,9},{5,10},{6,11},{7,12},{8,13},{9,14},{... | collective-permute-start | bytes 1843208 | tf_op jit(solution)/shard_map/ppermute | solution.py:160
  7.2 0.7 copy-start.4
  7.9 0.7 copy-start.6
  8.5 0.7 copy-start.7
  9.3 0.7 slice-start
  10.0 0.7 copy-start.8
  10.8 0.7 copy-start.5
  11.6 1.1 copy-start
  12.6 1.0 copy-start.2
  13.7 1.0 copy-start.3
  14.7 16.4 %copy-start.1 = (f32[384,400]{0,1:T(8,128)S(1)}, f32[384,400]{0,1:T(8,128)}, u32[]{:S(2)}) copy-start(f32[384,400]{0,1:T(8,128)} %param.11) | copy-start | bytes 1843204
  35.1 1.6 %collective-permute-start.2 = (f32[512,128]{1,0:T(8,128)S(1)}, f32[512,128]{1,0:T(8,128)S(1)}, u32[]{:S(2)}, u32[]{:S(2)}) collective-permute-start(f32[512,128]{1,0:T(8,128)S(1)} %get-tuple-element.25), channel_id=1, source_target_pairs={{0,1},{1,0},{2,3},{3,2},{4,5},{5,4},{6,7},{7,6},{8,9},{9,8},{10,11... | collective-permute-start | bytes 786440 | tf_op jit(solution)/shard_map/ppermute | solution.py:164
  74.3 5.3 %collective-permute-start.3 = (f32[512,128]{1,0:T(8,128)S(1)}, f32[512,128]{1,0:T(8,128)S(1)}, u32[]{:S(2)}, u32[]{:S(2)}) collective-permute-start(f32[512,128]{1,0:T(8,128)S(1)} %bitcast.38), channel_id=1, source_target_pairs={{0,1},{1,0},{2,3},{3,2},{4,5},{5,4},{6,7},{7,6},{8,9},{9,8},{10,11... | collective-permute-start | bytes 786440 | tf_op jit(solution)/shard_map/ppermute | solution.py:164
  84.2 1.8 %collective-permute-start.6 = (f32[512,128]{1,0:T(8,128)S(1)}, f32[512,128]{1,0:T(8,128)S(1)}, u32[]{:S(2)}, u32[]{:S(2)}) collective-permute-start(f32[512,128]{1,0:T(8,128)S(1)} %get-tuple-element.35), channel_id=1, source_target_pairs={{0,1},{1,0},{2,3},{3,2},{4,5},{5,4},{6,7},{7,6},{8,9},{9,8},{10,11... | collective-permute-start | bytes 786440 | tf_op jit(solution)/shard_map/ppermute | solution.py:164
  97.5 11.3 %all-to-all-start.4 = ((f32[8,32,128]{2,1,0:T(8,128)}), f32[8,32,128]{2,1,0:T(8,128)S(1)}, u32[]{:S(2)}, u32[]{:S(2)}) async-start(f32[8,32,128]{2,1,0:T(8,128)} %broadcast_in_dim.25), calls=%async_computation.4 | async-start | bytes 262144 | tf_op jit(solution)/shard_map/all_to_all | solution.py:168
  100.9 37.4 %collective-permute-start.4 = (f32[400,384]{1,0:T(8,128)S(1)}, f32[400,384]{1,0:T(8,128)S(1)}, u32[]{:S(2)}, u32[]{:S(2)}) collective-permute-start(f32[400,384]{1,0:T(8,128)S(1)} %get-tuple-element.32), channel_id=1, source_target_pairs={{0,27},{1,28},{2,29},{3,30},{4,31},{5,0},{6,1},{7,2},{8,3},{9,4},{... | collective-permute-start | bytes 1843208 | tf_op jit(solution)/shard_map/ppermute | solution.py:160
  119.8 18.5 %collective-permute-start.7 = (f32[512,128]{1,0:T(8,128)S(1)}, f32[512,128]{1,0:T(8,128)S(1)}, u32[]{:S(2)}, u32[]{:S(2)}) collective-permute-start(f32[512,128]{1,0:T(8,128)S(1)} %bitcast.44), channel_id=1, source_target_pairs={{0,1},{1,0},{2,3},{3,2},{4,5},{5,4},{6,7},{7,6},{8,9},{9,8},{10,11... | collective-permute-start | bytes 786440 | tf_op jit(solution)/shard_map/ppermute | solution.py:164
  124.3 13.4 %collective-permute-start.5 = (f32[1,384]{1,0:T(1,128)S(1)}, f32[1,384]{1,0:T(1,128)S(1)}, u32[]{:S(2)}, u32[]{:S(2)}) collective-permute-start(f32[1,384]{1,0:T(1,128)S(1)} %get-tuple-element.33), channel_id=1, source_target_pairs={{0,27},{1,28},{2,29},{3,30},{4,31},{5,0},{6,1},{7,2},{8,3},{9,4},{... | collective-permute-start | bytes 4616 | tf_op jit(solution)/shard_map/ppermute | solution.py:160

commit v3 on v2

v3 whole, which is shorter than its diff:
```python
import jax
import jax.numpy as jnp
from jax import lax
from jax.experimental import pallas as pl
from jax.experimental.pallas import tpu as pltpu
from jax.sharding import Mesh, PartitionSpec as P

BATCH = 500
BATCHES = 2
NEG = 1000
SHIFT = 5
SLAB = 384
REL = 256
HALF = 128
W = 400
MID = 200
EP = 512
NP = 1024

ROW_RATE = 0.2
REL_RATE = 1.0

AXES = ("x", "zh", "y", "zl", "c")
PLANE = ("x", "y")
COLUMN = ("zh", "zl")
RIGHT = ("y", "zl", "c")

NN = (((1,), (0,)), ((), ()))
NT = (((1,), (1,)), ((), ()))
TN = (((0,), (0,)), ((), ()))


def parts(value):
    high = value.astype(jnp.bfloat16)
    low = (value - high.astype(jnp.float32)).astype(jnp.bfloat16)
    return (high, low)


def dot(first, second, dims):
    return lax.dot_general(first, second, dims, preferred_element_type=jnp.float32)


def dot3(first, second, dims):
    return (
        dot(first[0], second[0], dims) + dot(first[0], second[1], dims) + dot(first[1], second[0], dims)
    )


def pick(rows, ids):
    return (lax.broadcasted_iota(jnp.int32, (rows, EP), 0) == ids).astype(jnp.bfloat16)


def gather(table, hot):
    high, low = parts(table)
    return dot(high, hot, NN) + dot(low, hot, NN)


def scatter(values, hot):
    high, low = parts(values)
    return dot(high, hot, NT) + dot(low, hot, NT)


def entity_update(table, state, grad):
    state = state + jnp.sum(grad * grad, axis=0, keepdims=True) * (1.0 / W)
    return (table - grad * (ROW_RATE / jnp.sqrt(state)), state)


def query(sources, relations):
    s_re, s_im = (sources[:MID], sources[MID:])
    r_re, r_im = (relations[:MID], relations[MID:])
    return parts(jnp.concatenate([s_re * r_re - s_im * r_im, s_re * r_im + s_im * r_re], axis=0))


def against(grads, other):
    g_re, g_im = (grads[:MID], grads[MID:])
    o_re, o_im = (other[:MID], other[MID:])
    return jnp.concatenate([g_re * o_re + g_im * o_im, g_im * o_re - g_re * o_im], axis=0)


def edge_weights(logits, src_ids, dst_ids, counts):
    tail = jnp.exp(-jnp.abs(logits))
    scale = jnp.where(src_ids >= 0, 1.0, 0.0) / (1.0 + tail)
    above = logits >= 0.0
    negative = jnp.where(above, 1.0, tail) * counts
    hit = lax.broadcasted_iota(jnp.int32, (SLAB, EP), 0) == dst_ids
    positive = jnp.where(hit, jnp.where(above, tail, 1.0), 0.0)
    return parts((negative - positive) * scale)


def put(refs, values):
    for ref, value in zip(refs, values, strict=True):
        ref[...] = value


def relation_side(batch, queries, sources, relations, dst_ref, ids_ref, counts_ref, mine_ref, other_ref, weight_refs, way_ref):
    rows = parts(dst_ref[...])
    src_ids, dst_ids = (ids_ref[batch : batch + 1, :], ids_ref[2 + batch : 3 + batch, :])
    weights = edge_weights(dot3(rows, queries, TN), src_ids, dst_ids, counts_ref[:, batch : batch + 1])
    grads = dot3(rows, weights, NN)
    rel_grad = scatter(against(grads, sources), pick(REL, ids_ref[5 + batch : 6 + batch, :]))
    for ref, low in ((mine_ref, 0), (other_ref, HALF)):
        ref[:W, :] = rel_grad[:, low : low + HALF]
        ref[W:, :] = jnp.zeros((EP - W, HALF), jnp.float32)
    put(weight_refs, weights)
    way_ref[...] = against(grads, relations)


def prepare_kernel(
    place_ref, src_ref, rel_ref, rel_state_ref, ids_ref, neg_ref, dst_state_ref,
    sources_ref, relations_ref, high_ref, low_ref, counts_ref, own_ref, own_sums_ref, dst_state_out, wide_ref,
):
    sources = gather(src_ref[...], pick(SLAB, ids_ref[0:1, :]))
    relations = gather(rel_ref[...], pick(REL, ids_ref[4:5, :]))
    put((sources_ref, relations_ref), (sources, relations))
    put((high_ref, low_ref), query(sources, relations))
    for batch in range(BATCHES):
        same = lax.broadcasted_iota(jnp.int32, (SLAB, NP), 0) == neg_ref[batch : batch + 1, :]
        total = jnp.sum(jnp.where(same, 1.0, 0.0), axis=1, keepdims=True)
        counts_ref[:, batch : batch + 1] = total * (1.0 / NEG)
    height = own_ref.shape[0]
    wide_ref[W:, :] = jnp.ones((EP - W, HALF), jnp.float32)
    for source, target in ((rel_ref, own_ref), (rel_state_ref, own_sums_ref)):
        wide_ref[:W, :] = jnp.where(place_ref[0] == 0, source[:, :HALF], source[:, HALF:])
        target[...] = wide_ref[pl.ds(pl.multiple_of(place_ref[1] * height, height), height), :]
    dst_state_out[...] = dst_state_ref[...]


def first_relation_kernel(
    sources_ref, relations_ref, high_ref, low_ref, dst_ref, ids_ref, counts_ref,
    mine_ref, other_ref, weight_high_ref, weight_low_ref, way_ref,
):
    relation_side(
        0, (high_ref[...], low_ref[...]), sources_ref[...], relations_ref[...], dst_ref, ids_ref, counts_ref,
        mine_ref, other_ref, (weight_high_ref, weight_low_ref), way_ref,
    )


def first_entity_kernel(
    high_ref, low_ref, weight_high_ref, weight_low_ref, way_ref, dst_ref, dst_state_ref, src_ref, src_state_ref, ids_ref,
    src_out, src_state_out, dst_out, dst_state_out, sources_ref,
):
    src_grad = scatter(way_ref[...], pick(SLAB, ids_ref[0:1, :]))
    src_table, src_state_out[...] = entity_update(src_ref[...], src_state_ref[...], src_grad)
    src_out[...] = src_table
    sources_ref[...] = gather(src_table, pick(SLAB, ids_ref[1:2, :]))
    dst_grad = dot3((high_ref[...], low_ref[...]), (weight_high_ref[...], weight_low_ref[...]), NT)
    dst_out[...], dst_state_out[...] = entity_update(dst_ref[...], dst_state_ref[...], dst_grad)


def second_relation_kernel(
    rel_mine_ref, rel_other_ref, sources_ref, dst_ref, ids_ref, counts_ref,
    mine_ref, other_ref, high_ref, low_ref, weight_high_ref, weight_low_ref, way_ref,
):
    relation = jnp.concatenate([rel_mine_ref[:W, :], rel_other_ref[:W, :]], axis=1)
    sources, relations = (sources_ref[...], gather(relation, pick(REL, ids_ref[6:7, :])))
    queries = query(sources, relations)
    put((high_ref, low_ref), queries)
    relation_side(
        1, queries, sources, relations, dst_ref, ids_ref, counts_ref,
        mine_ref, other_ref, (weight_high_ref, weight_low_ref), way_ref,
    )


def second_target_kernel(high_ref, low_ref, weight_high_ref, weight_low_ref, dst_ref, dst_state_ref, out_ref):
    dst_grad = dot3((high_ref[...], low_ref[...]), (weight_high_ref[...], weight_low_ref[...]), NT)
    out_ref[:W, :], state = entity_update(dst_ref[...], dst_state_ref[...], dst_grad)
    out_ref[W:, :] = jnp.broadcast_to(state, (8, SLAB))


def second_source_kernel(way_ref, src_ref, src_state_ref, ids_ref, src_out):
    src_grad = scatter(way_ref[...], pick(SLAB, ids_ref[1:2, :]))
    src_out[...], _ = entity_update(src_ref[...], src_state_ref[...], src_grad)


def call(kernel, outs, *args, scalars=0, scratch=(), passes=0):
    shapes = [shape if isinstance(shape, jax.ShapeDtypeStruct) else jax.ShapeDtypeStruct(shape, jnp.float32) for shape in outs]
    vector = pl.BlockSpec(memory_space=pltpu.VMEM)
    scalar = pl.BlockSpec(memory_space=pltpu.SMEM)
    moved = sum(value.size * value.dtype.itemsize for value in (*args, *shapes))
    return pl.pallas_call(
        kernel,
        out_shape=shapes,
        in_specs=[scalar] * scalars + [vector] * (len(args) - scalars),
        out_specs=[vector] * len(shapes),
        scratch_shapes=scratch,
        cost_estimate=pl.CostEstimate(flops=passes * 2 * EP * EP * SLAB, bytes_accessed=moved, transcendentals=0),
        compiler_params=pltpu.CompilerParams(vmem_limit_bytes=20 * 1024 * 1024),
    )(*args)


def shifted(value, steps):
    count = lax.axis_size(RIGHT)
    pairs = [(source, (source + steps) % count) for source in range(count)]
    return lax.ppermute(value, RIGHT, pairs)


def swapped(value):
    return lax.ppermute(value, "c", [(0, 1), (1, 0)])


def exchanged(value, axes):
    return lax.all_to_all(value, axes, split_axis=0, concat_axis=0, tiled=True)


def relation_update(mine, other, own, own_sums, beside=None):
    lanes, layers = (lax.axis_size(PLANE), lax.axis_size(COLUMN))
    half = mine + swapped(other)
    total = jnp.sum(exchanged(half.reshape(lanes, *own.shape), PLANE), axis=0)
    total = jnp.sum(exchanged(jnp.broadcast_to(total, (layers, *own.shape)), COLUMN), axis=0)
    own_sums = own_sums + total * total
    own = own - REL_RATE * total / jnp.sqrt(own_sums)
    if beside is not None:
        own, beside = lax.optimization_barrier((own, beside))
    half = exchanged(jnp.broadcast_to(own, (lanes, *own.shape)), PLANE).reshape(EP, HALF)
    return (half, swapped(half), own, own_sums, beside)


def padded(value, live, low):
    picked = value[low : low + BATCH]
    spot = lax.iota(jnp.int32, BATCH) + low
    return jnp.pad(jnp.where(spot < live, picked, -1), (0, EP - BATCH), constant_values=-1)


def body(
    src_embed, src_state, dst_embed, dst_state, relation, rel_state, edge_src, edge_dst, edge_rel, neg_rows, edge_count
):
    dst_table = shifted(dst_embed.T, SHIFT)
    core = lax.axis_index("c")
    live = edge_count[0]
    near_rel = edge_rel[0] ^ (core * HALF)
    ids = jnp.stack(
        [
            padded(edge_src[0], live, 0),
            padded(edge_src[0], live, BATCH),
            padded(edge_dst[0], live, 0),
            padded(edge_dst[0], live, BATCH),
            padded(edge_rel[0], live, 0),
            padded(near_rel, live, 0),
            padded(near_rel, live, BATCH),
            jnp.full((EP,), -1, jnp.int32),
        ]
    )
    negs = jnp.pad(neg_rows[0], ((0, 0), (0, NP - NEG)), constant_values=-1)
    place = jnp.stack([core, lax.axis_index(PLANE)]).astype(jnp.int32)
    height = EP // lax.axis_size(PLANE)
    src_table, src_sums = (src_embed.T, src_state.reshape(1, SLAB))

    high, low = [jax.ShapeDtypeStruct((W, EP), jnp.bfloat16)] * 2
    weight_high, weight_low = [jax.ShapeDtypeStruct((SLAB, EP), jnp.bfloat16)] * 2
    halves = [(EP, HALF), (EP, HALF)]
    flat = (1, SLAB)

    sources, relations, *queries, counts, own, own_sums, dst_sums = call(
        prepare_kernel,
        [(W, EP), (W, EP), high, low, (SLAB, BATCHES), (height, HALF), (height, HALF), flat],
        place, src_table, relation.T, rel_state.T, ids, negs, dst_state.reshape(flat),
        scalars=1, scratch=[pltpu.VMEM((EP, HALF), jnp.float32)], passes=4,
    )
    dst_table, dst_sums = lax.optimization_barrier((dst_table, shifted(dst_sums, SHIFT)))
    mine, other, *weights, way = call(
        first_relation_kernel,
        [*halves, weight_high, weight_low, (W, EP)],
        sources, relations, *queries, dst_table, ids, counts, passes=8,
    )
    near, far, own, own_sums, _ = relation_update(mine, other, own, own_sums)
    src_table, src_sums, dst_table, dst_sums, sources = call(
        first_entity_kernel,
        [(W, SLAB), flat, (W, SLAB), flat, (W, EP)],
        *queries, *weights, way, dst_table, dst_sums, src_table, src_sums, ids, passes=7,
    )
    mine, other, high, low, weight_high, weight_low, way = call(
        second_relation_kernel,
        [*halves, high, low, weight_high, weight_low, (W, EP)],
        near, far, sources, dst_table, ids, counts, passes=10,
    )
    (home,) = call(second_target_kernel, [(W + 8, SLAB)], high, low, weight_high, weight_low, dst_table, dst_sums, passes=3)
    home = shifted(home, -SHIFT)
    (src_table,) = call(second_source_kernel, [(W, SLAB)], way, src_table, src_sums, ids, passes=2)
    near, far, own, own_sums, home = relation_update(mine, other, own, own_sums, home)
    first = core == 0
    relation = jnp.concatenate([jnp.where(first, near, far), jnp.where(first, far, near)], axis=1)
    return (src_table.T, home[:W].T, home[W], relation[:W].T)


def solution(mesh):
    left, right = (mesh.shape["left"], mesh.shape["right"])
    devices = mesh.devices.reshape(left // 2, 2, 4, right // 8, 2)
    inner = Mesh(devices, AXES)
    in_specs = (
        P(AXES, None),
        P(AXES),
        P(AXES, None),
        P(AXES),
        P(),
        P(),
        P(AXES, None),
        P(AXES, None),
        P(AXES, None),
        P(AXES, None, None),
        P(AXES),
    )
    out_specs = (P(AXES, None), P(AXES, None), P(AXES), P())
    return jax.shard_map(body, mesh=inner, in_specs=in_specs, out_specs=out_specs, check_vma=False)
```

time: 141 us -> 144 us (1.021)
  local copies, waits for them, and re-layouts: 8.86 us -> 17.9 us
  waiting for transfers between devices: 32.8 us -> 24.1 us
  starting transfers between devices: 25.7 us -> 23.4 us
  blocking collectives: 59.1 us -> 60.9 us
  Pallas kernels: 10.3 us -> 12 us
    ppermute x4 -> x3, waiting for transfers between devices: 25.7 us -> 11.9 us  [shifted(): return lax.ppermute(value, RIGHT, pairs)]
    unnamed x19 -> x56, local copies, waits for them, and re-layouts: 6.48 us -> 14.7 us
    all_to_all x1 -> x2, starting transfers between devices: 3.37 us -> 9.77 us  [exchanged(): return lax.all_to_all(value, axes, split_axis=0, concat_axis=0, tiled=True)]
    all_to_all x1 -> x2, waiting for transfers between devices: 3.23 us -> 9.13 us  [exchanged(): return lax.all_to_all(value, axes, split_axis=0, concat_axis=0, tiled=True)]
    ppermute x4 -> x3, starting transfers between devices: 13 us -> 8.06 us  [shifted(): return lax.ppermute(value, RIGHT, pairs)]
    ppermute x4, starting transfers between devices: 9.34 us -> 5.59 us  [swapped(): return lax.ppermute(value, 'c', [(0, 1), (1, 0)])]
    all_to_all x5 -> x4, blocking collectives: 59.1 us -> 60.9 us  [exchanged(): return lax.all_to_all(value, axes, split_axis=0, concat_axis=0, tiled=True)]
    pallas_call x3 -> x6, Pallas kernels: 10.3 us -> 12 us  [call(): pl.pallas_call(kernel, out_shape=shapes, in_specs=[scalar] * scalars + [v...]
  transfers between devices with their start and end apart: 9 -> 9, of which waited for: 6 -> 5; matrix products, arithmetic and copies ran while one was open for 1% -> 2% of each run, Pallas kernels for 1% -> 5%
where the time goes in v3:
time: 144 us; the launch traced here: 143 us
  blocking collectives  60.9 us (42%)
  waiting for transfers between devices  24.1 us (17%)
  starting transfers between devices  23.4 us (16%)
  local copies, waits for them, and re-layouts  17.9 us (12%)
  Pallas kernels  12 us (8%)
  other arithmetic  2.73 us (2%)
  between operations  1.64 us (1%)
    all_to_all x4, blocking collectives, exchanged(): return lax.all_to_all(value, axes, split_axis=0, concat_axis=0, tiled=True)  60.9 us
    unnamed x56, local copies, waits for them, and re-layouts  14.7 us
    pallas_call x6, Pallas kernels, call(): pl.pallas_call(kernel, out_shape=shapes, in_specs=[scalar] * scalars + [v...  12 us
    ppermute x3, waiting for transfers between devices, shifted(): return lax.ppermute(value, RIGHT, pairs)  11.9 us
    all_to_all x2, starting transfers between devices, exchanged(): return lax.all_to_all(value, axes, split_axis=0, concat_axis=0, tiled=True)  9.77 us
    all_to_all x2, waiting for transfers between devices, exchanged(): return lax.all_to_all(value, axes, split_axis=0, concat_axis=0, tiled=True)  9.13 us
    ppermute x3, starting transfers between devices, shifted(): return lax.ppermute(value, RIGHT, pairs)  8.06 us
    ppermute x4, starting transfers between devices, swapped(): return lax.ppermute(value, 'c', [(0, 1), (1, 0)])  5.59 us
  transfers between devices with their start and end apart: 9, of which 5 were waited for; matrix products, arithmetic and copies ran while one was open for 2% of the time, Pallas kernels for 5%

profile of v3, /device:TPU:1, one launch (start us, length us, event | category | flops | bytes accessed | tf_op | source)
XLA Modules:
  0.0 142.7 jit_solution(6976543354651423523)
XLA Ops:
  0.6 5.8 %collective-permute-start = (f32[400,384]{1,0:T(8,128)}, f32[400,384]{1,0:T(8,128)S(1)}, u32[]{:S(2)}, u32[]{:S(2)}) collective-permute-start(f32[400,384]{1,0:T(8,128)} %bitcast.62), channel_id=1, source_target_pairs={{0,5},{1,6},{2,7},{3,8},{4,9},{5,10},{6,11},{7,12},{8,13},{9,14},{... | collective-permute-start | bytes 1843208 | tf_op jit(solution)/shard_map/ppermute | solution.py:194
  11.0 1.1 copy-done.4
  12.0 1.0 copy-done.6
  13.0 1.0 copy-done.7
  14.0 1.8 %shard_map.138 = (f32[400,512]{1,0:T(8,128)S(1)}, f32[400,512]{1,0:T(8,128)S(1)}, bf16[400,512]{1,0:T(8,128)(2,1)S(1)}, bf16[400,512]{1,0:T(8,128)(2,1)S(1)}, f3...) custom-call(s32[2]{0:T(128)S(1)} %pad_add_fusion.place_ref, ...), custom_call_target="tpu_custom_call" | custom-call | flops 805306368 | bytes 3954696 | tf_op jit(solution)/shard_map/pallas_call | solution.py:180
  16.1 11.9 %collective-permute-done.1.dst_state_ref = f32[1,384]{1,0:T(1,128)S(1)} collective-permute-done((f32[1,384]{1,0:T(1,128)S(1)}, f32[1,384]{1,0:T(1,128)S(1)}, u32[]{:S(2)}, u32[]{:S(2)}) %collective-permute-start.1) | collective-permute-done | bytes 1568 | tf_op jit(solution)/shard_map/ppermute | solution.py:194
  28.0 2.5 %shard_map.139 = (f32[512,128]{1,0:T(8,128)S(1)}, f32[512,128]{1,0:T(8,128)S(1)}, bf16[384,512]{1,0:T(8,128)(2,1)S(1)}, bf16[384,512]{1,0:T(8,128)(2,1)S(1)}, f32[400,512]{1,0:T(8,128)S(1)}) custom-call(f32[400,512]{1,0:T(8,128)S(1)} %get-tuple-element.34.sources_ref, f32[400,512]{1,0:T(8,128)S(1)} %get-tuple-element.35.relations_ref, ...), custom_call_target="tpu_custom_call" | custom-call | flops 1610612736 | bytes 5221376 | tf_op jit(solution)/shard_map/pallas_call | solution.py:180
  32.1 1.5 %collective-permute-done.2 = f32[512,128]{1,0:T(8,128)S(1)} collective-permute-done((f32[512,128]{1,0:T(8,128)S(1)}, f32[512,128]{1,0:T(8,128)S(1)}, u32[]{:S(2)}, u32[]{:S(2)}) %collective-permute-start.2) | collective-permute-done | bytes 262176 | tf_op jit(solution)/shard_map/ppermute | solution.py:198
  33.6 12.4 %all_to_all.30 = f32[16,32,128]{2,1,0:T(8,128)S(1)} all-to-all(f32[16,32,128]{2,1,0:T(8,128)S(1)} %bitcast.44), channel_id=1, replica_groups=mesh['x'=4,'zh'=2,'y'=4,'zl'=4,'c'=2] {'x','y'}, dimensions={0} | all-to-all | bytes 524288 | tf_op jit(solution)/shard_map/all_to_all | solution.py:202
  46.1 16.0 %all_to_all.31 = f32[8,32,128]{2,1,0:T(8,128)S(1)} all-to-all(f32[8,32,128]{2,1,0:T(8,128)S(1)} %broadcast_in_dim.23), channel_id=1, replica_groups=mesh['x'=4,'zh'=2,'y'=4,'zl'=4,'c'=2] {'zh','zl'}, dimensions={0} | all-to-all | bytes 262144 | tf_op jit(solution)/shard_map/all_to_all | solution.py:202
  62.7 11.0 %all_to_all.32 = f32[16,32,128]{2,1,0:T(8,128)S(1)} all-to-all(f32[16,32,128]{2,1,0:T(8,128)S(1)} %broadcast_in_dim.24), channel_id=1, replica_groups=mesh['x'=4,'zh'=2,'y'=4,'zl'=4,'c'=2] {'x','y'}, dimensions={0} | all-to-all | bytes 524288 | tf_op jit(solution)/shard_map/all_to_all | solution.py:202
  73.7 4.1 %collective-permute-start.3 = (f32[512,128]{1,0:T(8,128)S(1)}, f32[512,128]{1,0:T(8,128)S(1)}, u32[]{:S(2)}, u32[]{:S(2)}) collective-permute-start(f32[512,128]{1,0:T(8,128)S(1)} %bitcast.37), channel_id=1, source_target_pairs={{0,1},{1,0},{2,3},{3,2},{4,5},{5,4},{6,7},{7,6},{8,9},{9,8},{10,11... | collective-permute-start | bytes 786440 | tf_op jit(solution)/shard_map/ppermute | solution.py:198
  77.8 1.1 copy-done.9
  81.9 2.1 %shard_map.140 = (f32[400,384]{1,0:T(8,128)S(1)}, f32[1,384]{1,0:T(1,128)S(1)}, f32[400,384]{1,0:T(8,128)S(1)}, f32[1,384]{1,0:T(1,128)S(1)}, f32[400,512]{1,0:T(8,128)S(1)}) custom-call(bf16[400,512]{1,0:T(8,128)(2,1)S(1)} %copy-done.11, bf16[400,512]{1,0:T(8,128)(2,1)S(1)} %copy-done.13, bf16[384,512]{1,0:T(8,128)(2,1)S(1)} %copy-done.15, ...), custom_call_target="tpu_custom_call" | custom-call | flops 1409286144 | bytes 5724160 | tf_op jit(solution)/shard_map/pallas_call | solution.py:180
  84.0 3.0 %shard_map.141 = (f32[512,128]{1,0:T(8,128)S(1)}, f32[512,128]{1,0:T(8,128)S(1)}, bf16[400,512]{1,0:T(8,128)(2,1)S(1)}, bf16[400,512]{1,0:T(8,128)(2,1)S(1)}, bf...) custom-call(f32[512,128]{1,0:T(8,128)S(1)} %bitcast.38, ...), custom_call_target="tpu_custom_call" | custom-call | flops 2013265920 | bytes 4926464 | tf_op jit(solution)/shard_map/pallas_call | solution.py:180
  87.2 1.5 %collective-permute-done.4 = f32[512,128]{1,0:T(8,128)S(1)} collective-permute-done((f32[512,128]{1,0:T(8,128)S(1)}, f32[512,128]{1,0:T(8,128)S(1)}, u32[]{:S(2)}, u32[]{:S(2)}) %collective-permute-start.4) | collective-permute-done | bytes 262176 | tf_op jit(solution)/shard_map/ppermute | solution.py:198
  89.4 4.4 %all-to-all-start.3 = ((f32[16,32,128]{2,1,0:T(8,128)}), f32[16,32,128]{2,1,0:T(8,128)}, u32[]{:S(2)}, u32[]{:S(2)}) async-start(f32[16,32,128]{2,1,0:T(8,128)} %bitcast.43), calls=%async_computation.3 | async-start | bytes 524288 | tf_op jit(solution)/shard_map/all_to_all | solution.py:202
  96.8 2.1 %collective-permute-start.5 = (f32[408,384]{1,0:T(8,128)S(1)}, f32[408,384]{1,0:T(8,128)S(1)}, u32[]{:S(2)}, u32[]{:S(2)}) collective-permute-start(f32[408,384]{1,0:T(8,128)S(1)} %shard_map.143), channel_id=1, source_target_pairs={{0,27},{1,28},{2,29},{3,30},{4,31},{5,0},{6,1},{7,2},{8,3},{9,4},{... | collective-permute-start | bytes 1880072 | tf_op jit(solution)/shard_map/ppermute | solution.py:194
  98.8 2.8 %all-to-all-done.3 = f32[16,32,128]{2,1,0:T(8,128)} async-done(((f32[16,32,128]{2,1,0:T(8,128)}), f32[16,32,128]{2,1,0:T(8,128)}, u32[]{:S(2)}, u32[]{:S(2)}) %all-to-all-start.3) | async-done | bytes 262176 | tf_op jit(solution)/shard_map/all_to_all | solution.py:202
  102.6 21.6 %all_to_all.33 = f32[8,32,128]{2,1,0:T(8,128)S(1)} all-to-all(f32[8,32,128]{2,1,0:T(8,128)S(1)} %broadcast_in_dim.25), channel_id=1, replica_groups=mesh['x'=4,'zh'=2,'y'=4,'zl'=4,'c'=2] {'zh','zl'}, dimensions={0} | all-to-all | bytes 262144 | tf_op jit(solution)/shard_map/all_to_all | solution.py:202
  125.7 5.4 %all-to-all-start.5 = ((f32[16,32,128]{2,1,0:T(8,128)}), f32[16,32,128]{2,1,0:T(8,128)S(1)}, u32[]{:S(2)}, u32[]{:S(2)}) async-start(f32[16,32,128]{2,1,0:T(8,128)} %broadcast_in_dim.26), calls=%async_computation.5 | async-start | bytes 524288 | tf_op jit(solution)/shard_map/all_to_all | solution.py:202
  131.1 1.6 %shard_map.142 = f32[400,384]{1,0:T(8,128)} custom-call(f32[400,512]{1,0:T(8,128)S(1)} %get-tuple-element.50.way_ref, f32[400,384]{1,0:T(8,128)S(1)} %get-tuple-element.51.src_ref, f32[1,384]{1,0:T(1,128)S(1)} %get-tuple-element.52.src_state_ref, s32[8,512]{1,0:T(8,128)S(1)} %stack.43.ids_ref), custom_call_target="tpu_custom_call" | custom-call | flops 402653184 | bytes 2065920 | tf_op jit(solution)/shard_map/pallas_call | solution.py:180
  132.7 6.4 %all-to-all-done.5 = f32[16,32,128]{2,1,0:T(8,128)S(1)} async-done(((f32[16,32,128]{2,1,0:T(8,128)}), f32[16,32,128]{2,1,0:T(8,128)S(1)}, u32[]{:S(2)}, u32[]{:S(2)}) %all-to-all-start.5) | async-done | bytes 262176 | tf_op jit(solution)/shard_map/all_to_all | solution.py:202
  139.0 1.4 collective-permute-start.6
  (99 shorter events, 17.7 us)
Async XLA Ops:
  0.6 27.4 %collective-permute-start = (f32[400,384]{1,0:T(8,128)}, f32[400,384]{1,0:T(8,128)S(1)}, u32[]{:S(2)}, u32[]{:S(2)}) collective-permute-start(f32[400,384]{1,0:T(8,128)} %bitcast.62), channel_id=1, source_target_pairs={{0,5},{1,6},{2,7},{3,8},{4,9},{5,10},{6,11},{7,12},{8,13},{9,14},{... | collective-permute-start | bytes 1843208 | tf_op jit(solution)/shard_map/ppermute | solution.py:194
  11.0 1.1 copy-start.4
  12.0 1.0 copy-start.6
  13.0 1.0 copy-start.7
  15.9 14.6 %copy-start.10 = (bf16[400,512]{1,0:T(8,128)(2,1)}, bf16[400,512]{1,0:T(8,128)(2,1)S(1)}, u32[]{:S(2)}) copy-start(bf16[400,512]{1,0:T(8,128)(2,1)S(1)} %get-tuple-element.36.high_ref) | copy-start | bytes 1228804
  15.9 14.6 %copy-start.12 = (bf16[400,512]{1,0:T(8,128)(2,1)}, bf16[400,512]{1,0:T(8,128)(2,1)S(1)}, u32[]{:S(2)}) copy-start(bf16[400,512]{1,0:T(8,128)(2,1)S(1)} %get-tuple-element.37.low_ref) | copy-start | bytes 1228804
  15.9 14.6 %copy-start.18 = (f32[384,2]{1,0:T(8,128)}, f32[384,2]{1,0:T(8,128)S(1)}, u32[]{:S(2)}) copy-start(f32[384,2]{1,0:T(8,128)S(1)} %get-tuple-element.40.counts_ref) | copy-start | bytes 9220
  15.9 12.1 %collective-permute-start.1 = (f32[1,384]{1,0:T(1,128)S(1)}, f32[1,384]{1,0:T(1,128)S(1)}, u32[]{:S(2)}, u32[]{:S(2)}) collective-permute-start(f32[1,384]{1,0:T(1,128)S(1)} %get-tuple-element.38), channel_id=1, source_target_pairs={{0,5},{1,6},{2,7},{3,8},{4,9},{5,10},{6,11},{7,12},{8,13},{9,14},{... | collective-permute-start | bytes 4616 | tf_op jit(solution)/shard_map/ppermute | solution.py:194
  32.1 14.0 %copy-start.8 = (f32[400,512]{1,0:T(8,128)}, f32[400,512]{1,0:T(8,128)S(1)}, u32[]{:S(2)}) copy-start(f32[400,512]{1,0:T(8,128)S(1)} %get-tuple-element.46.way_ref) | copy-start | bytes 2457604
  32.1 1.5 %collective-permute-start.2 = (f32[512,128]{1,0:T(8,128)S(1)}, f32[512,128]{1,0:T(8,128)S(1)}, u32[]{:S(2)}, u32[]{:S(2)}) collective-permute-start(f32[512,128]{1,0:T(8,128)S(1)} %get-tuple-element.42), channel_id=1, source_target_pairs={{0,1},{1,0},{2,3},{3,2},{4,5},{5,4},{6,7},{7,6},{8,9},{9,8},{10,11... | collective-permute-start | bytes 786440 | tf_op jit(solution)/shard_map/ppermute | solution.py:198
  46.1 31.7 %copy-start.5 = (f32[384,400]{0,1:T(8,128)S(1)}, f32[384,400]{0,1:T(8,128)}, u32[]{:S(2)}) copy-start(f32[384,400]{0,1:T(8,128)} %param.11) | copy-start | bytes 1843204
  62.7 15.1 %copy-start.11 = (bf16[400,512]{1,0:T(8,128)(2,1)S(1)}, bf16[400,512]{1,0:T(8,128)(2,1)}, u32[]{:S(2)}) copy-start(bf16[400,512]{1,0:T(8,128)(2,1)} %copy-done.10) | copy-start | bytes 1228804
  62.7 15.1 %copy-start.27 = (f32[384]{0:T(512)S(1)}, f32[384]{0:T(512)}, u32[]{:S(2)}) copy-start(f32[384]{0:T(512)} %param.12) | copy-start | bytes 4612
  73.7 10.4 %collective-permute-start.3 = (f32[512,128]{1,0:T(8,128)S(1)}, f32[512,128]{1,0:T(8,128)S(1)}, u32[]{:S(2)}, u32[]{:S(2)}) collective-permute-start(f32[512,128]{1,0:T(8,128)S(1)} %bitcast.37), channel_id=1, source_target_pairs={{0,1},{1,0},{2,3},{3,2},{4,5},{5,4},{6,7},{7,6},{8,9},{9,8},{10,11... | collective-permute-start | bytes 786440 | tf_op jit(solution)/shard_map/ppermute | solution.py:198
  77.8 1.1 copy-start.9
  78.9 1.0 copy-start.13
  81.9 2.1 %copy-start.19 = (f32[384,2]{1,0:T(8,128)S(1)}, f32[384,2]{1,0:T(8,128)}, u32[]{:S(2)}) copy-start(f32[384,2]{1,0:T(8,128)} %copy-done.18) | copy-start | bytes 9220
  87.0 2.4 %copy-start = (bf16[384,512]{1,0:T(8,128)(2,1)}, bf16[384,512]{1,0:T(8,128)(2,1)S(1)}, u32[]{:S(2)}) copy-start(bf16[384,512]{1,0:T(8,128)(2,1)S(1)} %get-tuple-element.57.weight_high_ref) | copy-start | bytes 1179652
  87.0 2.4 %copy-start.2 = (bf16[384,512]{1,0:T(8,128)(2,1)}, bf16[384,512]{1,0:T(8,128)(2,1)S(1)}, u32[]{:S(2)}) copy-start(bf16[384,512]{1,0:T(8,128)(2,1)S(1)} %get-tuple-element.58.weight_low_ref) | copy-start | bytes 1179652
  87.1 1.6 %collective-permute-start.4 = (f32[512,128]{1,0:T(8,128)S(1)}, f32[512,128]{1,0:T(8,128)S(1)}, u32[]{:S(2)}, u32[]{:S(2)}) collective-permute-start(f32[512,128]{1,0:T(8,128)S(1)} %get-tuple-element.54), channel_id=1, source_target_pairs={{0,1},{1,0},{2,3},{3,2},{4,5},{5,4},{6,7},{7,6},{8,9},{9,8},{10,11... | collective-permute-start | bytes 786440 | tf_op jit(solution)/shard_map/ppermute | solution.py:198
  89.4 12.2 %all-to-all-start.3 = ((f32[16,32,128]{2,1,0:T(8,128)}), f32[16,32,128]{2,1,0:T(8,128)}, u32[]{:S(2)}, u32[]{:S(2)}) async-start(f32[16,32,128]{2,1,0:T(8,128)} %bitcast.43), calls=%async_computation.3 | async-start | bytes 524288 | tf_op jit(solution)/shard_map/all_to_all | solution.py:202
  96.8 28.2 %collective-permute-start.5 = (f32[408,384]{1,0:T(8,128)S(1)}, f32[408,384]{1,0:T(8,128)S(1)}, u32[]{:S(2)}, u32[]{:S(2)}) collective-permute-start(f32[408,384]{1,0:T(8,128)S(1)} %shard_map.143), channel_id=1, source_target_pairs={{0,27},{1,28},{2,29},{3,30},{4,31},{5,0},{6,1},{7,2},{8,3},{9,4},{... | collective-permute-start | bytes 1880072 | tf_op jit(solution)/shard_map/ppermute | solution.py:194
  125.7 13.4 %all-to-all-start.5 = ((f32[16,32,128]{2,1,0:T(8,128)}), f32[16,32,128]{2,1,0:T(8,128)S(1)}, u32[]{:S(2)}, u32[]{:S(2)}) async-start(f32[16,32,128]{2,1,0:T(8,128)} %broadcast_in_dim.26), calls=%async_computation.5 | async-start | bytes 524288 | tf_op jit(solution)/shard_map/all_to_all | solution.py:202
  139.0 2.9 %collective-permute-start.6 = (f32[512,128]{1,0:T(8,128)S(1)}, f32[512,128]{1,0:T(8,128)S(1)}, u32[]{:S(2)}, u32[]{:S(2)}) collective-permute-start(f32[512,128]{1,0:T(8,128)S(1)} %bitcast.45), channel_id=1, source_target_pairs={{0,1},{1,0},{2,3},{3,2},{4,5},{5,4},{6,7},{7,6},{8,9},{9,8},{10,11... | collective-permute-start | bytes 786440 | tf_op jit(solution)/shard_map/ppermute | solution.py:198
  (14 other events, 11.0 us)

commit v4 on v2

v4 whole, which is shorter than its diff:
```python
import jax
import jax.numpy as jnp
from jax import lax
from jax.experimental import pallas as pl
from jax.experimental.pallas import tpu as pltpu
from jax.sharding import Mesh, PartitionSpec as P

BATCH = 500
BATCHES = 2
NEG = 1000
SHIFT = 5
SLAB = 384
REL = 256
HALF = 128
W = 400
MID = 200
EP = 512
NP = 1024
CUT = 200

ROW_RATE = 0.2
REL_RATE = 1.0

AXES = ("x", "zh", "y", "zl", "c")
PLANE = ("x", "y")
COLUMN = ("zh", "zl")
RIGHT = ("y", "zl", "c")

NN = (((1,), (0,)), ((), ()))
NT = (((1,), (1,)), ((), ()))
TN = (((0,), (0,)), ((), ()))


def parts(value):
    high = value.astype(jnp.bfloat16)
    low = (value - high.astype(jnp.float32)).astype(jnp.bfloat16)
    return (high, low)


def dot(first, second, dims):
    return lax.dot_general(first, second, dims, preferred_element_type=jnp.float32)


def dot3(first, second, dims):
    return (
        dot(first[0], second[0], dims) + dot(first[0], second[1], dims) + dot(first[1], second[0], dims)
    )


def pick(rows, ids):
    return (lax.broadcasted_iota(jnp.int32, (rows, EP), 0) == ids).astype(jnp.bfloat16)


def gather(table, hot):
    high, low = parts(table)
    return dot(high, hot, NN) + dot(low, hot, NN)


def scatter(values, hot):
    high, low = parts(values)
    return dot(high, hot, NT) + dot(low, hot, NT)


def entity_update(table, state, grad):
    state = state + jnp.sum(grad * grad, axis=0, keepdims=True) * (1.0 / W)
    return (table - grad * (ROW_RATE / jnp.sqrt(state)), state)


def query(sources, relations):
    s_re, s_im = (sources[:MID], sources[MID:])
    r_re, r_im = (relations[:MID], relations[MID:])
    return parts(jnp.concatenate([s_re * r_re - s_im * r_im, s_re * r_im + s_im * r_re], axis=0))


def against(grads, other):
    g_re, g_im = (grads[:MID], grads[MID:])
    o_re, o_im = (other[:MID], other[MID:])
    return jnp.concatenate([g_re * o_re + g_im * o_im, g_im * o_re - g_re * o_im], axis=0)


def edge_weights(logits, src_ids, dst_ids, counts):
    tail = jnp.exp(-jnp.abs(logits))
    scale = jnp.where(src_ids >= 0, 1.0, 0.0) / (1.0 + tail)
    above = logits >= 0.0
    negative = jnp.where(above, 1.0, tail) * counts
    hit = lax.broadcasted_iota(jnp.int32, (SLAB, EP), 0) == dst_ids
    positive = jnp.where(hit, jnp.where(above, tail, 1.0), 0.0)
    return parts((negative - positive) * scale)


def put(refs, values):
    for ref, value in zip(refs, values, strict=True):
        ref[...] = value


def bucket(batch, sources, relations, dst_ref, ids_ref, counts_ref, mine_ref, other_ref):
    queries, rows = (query(sources, relations), parts(dst_ref[...]))
    src_ids, dst_ids = (ids_ref[batch : batch + 1, :], ids_ref[2 + batch : 3 + batch, :])
    weights = edge_weights(dot3(rows, queries, TN), src_ids, dst_ids, counts_ref[:, batch : batch + 1])
    grads = dot3(rows, weights, NN)
    rel_grad = scatter(against(grads, sources), pick(REL, ids_ref[5 + batch : 6 + batch, :]))
    for ref, low in ((mine_ref, 0), (other_ref, HALF)):
        ref[:W, :] = rel_grad[:, low : low + HALF]
        ref[W:, :] = jnp.zeros((EP - W, HALF), jnp.float32)
    src_grad = scatter(against(grads, relations), pick(SLAB, src_ids))
    return (src_grad, dot3(queries, weights, NT))


def prepare_kernel(
    place_ref, src_ref, rel_ref, rel_state_ref, ids_ref, neg_ref, dst_state_ref,
    sources_ref, relations_ref, counts_ref, own_ref, own_sums_ref, dst_state_out, wide_ref,
):
    sources_ref[...] = gather(src_ref[...], pick(SLAB, ids_ref[0:1, :]))
    relations_ref[...] = gather(rel_ref[...], pick(REL, ids_ref[4:5, :]))
    for batch in range(BATCHES):
        same = lax.broadcasted_iota(jnp.int32, (SLAB, NP), 0) == neg_ref[batch : batch + 1, :]
        total = jnp.sum(jnp.where(same, 1.0, 0.0), axis=1, keepdims=True)
        counts_ref[:, batch : batch + 1] = total * (1.0 / NEG)
    height = own_ref.shape[0]
    wide_ref[W:, :] = jnp.ones((EP - W, HALF), jnp.float32)
    for source, target in ((rel_ref, own_ref), (rel_state_ref, own_sums_ref)):
        wide_ref[:W, :] = jnp.where(place_ref[0] == 0, source[:, :HALF], source[:, HALF:])
        target[...] = wide_ref[pl.ds(pl.multiple_of(place_ref[1] * height, height), height), :]
    dst_state_out[...] = dst_state_ref[...]


def first_kernel(
    sources_ref, relations_ref, dst_ref, dst_state_ref, src_ref, src_state_ref, ids_ref, counts_ref,
    mine_ref, other_ref, src_out, src_state_out, dst_out, dst_state_out,
):
    src_grad, dst_grad = bucket(
        0, sources_ref[...], relations_ref[...], dst_ref, ids_ref, counts_ref, mine_ref, other_ref
    )
    src_out[...], src_state_out[...] = entity_update(src_ref[...], src_state_ref[...], src_grad)
    dst_out[...], dst_state_out[...] = entity_update(dst_ref[...], dst_state_ref[...], dst_grad)


def second_kernel(
    rel_mine_ref, rel_other_ref, dst_ref, dst_state_ref, src_ref, src_state_ref, ids_ref, counts_ref,
    mine_ref, other_ref, src_out, upper_out, lower_out,
):
    relation = jnp.concatenate([rel_mine_ref[:W, :], rel_other_ref[:W, :]], axis=1)
    sources = gather(src_ref[...], pick(SLAB, ids_ref[1:2, :]))
    relations = gather(relation, pick(REL, ids_ref[6:7, :]))
    src_grad, dst_grad = bucket(1, sources, relations, dst_ref, ids_ref, counts_ref, mine_ref, other_ref)
    dst_table, dst_state = entity_update(dst_ref[...], dst_state_ref[...], dst_grad)
    upper_out[...] = dst_table[:CUT]
    lower_out[: W - CUT, :] = dst_table[CUT:]
    lower_out[W - CUT :, :] = jnp.broadcast_to(dst_state, (8, SLAB))
    src_out[...], _ = entity_update(src_ref[...], src_state_ref[...], src_grad)


def call(kernel, outs, *args, scalars=0, scratch=(), passes=0):
    shapes = [shape if isinstance(shape, jax.ShapeDtypeStruct) else jax.ShapeDtypeStruct(shape, jnp.float32) for shape in outs]
    vector = pl.BlockSpec(memory_space=pltpu.VMEM)
    scalar = pl.BlockSpec(memory_space=pltpu.SMEM)
    moved = sum(value.size * value.dtype.itemsize for value in (*args, *shapes))
    return pl.pallas_call(
        kernel,
        out_shape=shapes,
        in_specs=[scalar] * scalars + [vector] * (len(args) - scalars),
        out_specs=[vector] * len(shapes),
        scratch_shapes=scratch,
        cost_estimate=pl.CostEstimate(flops=passes * 2 * EP * EP * SLAB, bytes_accessed=moved, transcendentals=0),
        compiler_params=pltpu.CompilerParams(vmem_limit_bytes=16 * 1024 * 1024),
    )(*args)


def shifted(value, steps):
    count = lax.axis_size(RIGHT)
    pairs = [(source, (source + steps) % count) for source in range(count)]
    return lax.ppermute(value, RIGHT, pairs)


def swapped(value):
    return lax.ppermute(value, "c", [(0, 1), (1, 0)])


def exchanged(value, axes):
    return lax.all_to_all(value, axes, split_axis=0, concat_axis=0, tiled=True)


def relation_update(mine, other, own, own_sums, upper=None, lower=None):
    lanes, layers = (lax.axis_size(PLANE), lax.axis_size(COLUMN))
    half = mine + swapped(other)
    total = jnp.sum(exchanged(half.reshape(lanes, *own.shape), PLANE), axis=0)
    if upper is not None:
        total, upper = lax.optimization_barrier((total, shifted(upper, -SHIFT)))
    total = jnp.sum(exchanged(jnp.broadcast_to(total, (layers, *own.shape)), COLUMN), axis=0)
    if lower is not None:
        total, lower = lax.optimization_barrier((total, lower))
        lower = shifted(lower, -SHIFT)
    own_sums = own_sums + total * total
    own = own - REL_RATE * total / jnp.sqrt(own_sums)
    half = exchanged(jnp.broadcast_to(own, (lanes, *own.shape)), PLANE).reshape(EP, HALF)
    return (half, swapped(half), own, own_sums, upper, lower)


def padded(value, live, low):
    picked = value[low : low + BATCH]
    spot = lax.iota(jnp.int32, BATCH) + low
    return jnp.pad(jnp.where(spot < live, picked, -1), (0, EP - BATCH), constant_values=-1)


def body(
    src_embed, src_state, dst_embed, dst_state, relation, rel_state, edge_src, edge_dst, edge_rel, neg_rows, edge_count
):
    dst_table = shifted(dst_embed.T, SHIFT)
    core = lax.axis_index("c")
    live = edge_count[0]
    near_rel = edge_rel[0] ^ (core * HALF)
    ids = jnp.stack(
        [
            padded(edge_src[0], live, 0),
            padded(edge_src[0], live, BATCH),
            padded(edge_dst[0], live, 0),
            padded(edge_dst[0], live, BATCH),
            padded(edge_rel[0], live, 0),
            padded(near_rel, live, 0),
            padded(near_rel, live, BATCH),
            jnp.full((EP,), -1, jnp.int32),
        ]
    )
    negs = jnp.pad(neg_rows[0], ((0, 0), (0, NP - NEG)), constant_values=-1)
    place = jnp.stack([core, lax.axis_index(PLANE)]).astype(jnp.int32)
    height = EP // lax.axis_size(PLANE)
    src_table, src_sums = (src_embed.T, src_state.reshape(1, SLAB))

    flat = (1, SLAB)
    sources, relations, counts, own, own_sums, dst_sums = call(
        prepare_kernel,
        [(W, EP), (W, EP), (SLAB, BATCHES), (height, HALF), (height, HALF), flat],
        place, src_table, relation.T, rel_state.T, ids, negs, dst_state.reshape(flat),
        scalars=1, scratch=[pltpu.VMEM((EP, HALF), jnp.float32)], passes=4,
    )
    dst_table, dst_sums = lax.optimization_barrier((dst_table, shifted(dst_sums, SHIFT)))
    mine, other, src_table, src_sums, dst_table, dst_sums = call(
        first_kernel,
        [(EP, HALF), (EP, HALF), (W, SLAB), flat, (W, SLAB), flat],
        sources, relations, dst_table, dst_sums, src_table, src_sums, ids, counts, passes=13,
    )
    near, far, own, own_sums, _, _ = relation_update(mine, other, own, own_sums)
    mine, other, src_table, upper, lower = call(
        second_kernel,
        [(EP, HALF), (EP, HALF), (W, SLAB), (CUT, SLAB), (W + 8 - CUT, SLAB)],
        near, far, dst_table, dst_sums, src_table, src_sums, ids, counts, passes=17,
    )
    near, far, own, own_sums, upper, lower = relation_update(mine, other, own, own_sums, upper, lower)
    first = core == 0
    relation = jnp.concatenate([jnp.where(first, near, far), jnp.where(first, far, near)], axis=1)
    dst_table = jnp.concatenate([upper, lower[: W - CUT]], axis=0)
    return (src_table.T, dst_table.T, lower[W - CUT], relation[:W].T)


def solution(mesh):
    left, right = (mesh.shape["left"], mesh.shape["right"])
    devices = mesh.devices.reshape(left // 2, 2, 4, right // 8, 2)
    inner = Mesh(devices, AXES)
    in_specs = (
        P(AXES, None),
        P(AXES),
        P(AXES, None),
        P(AXES),
        P(),
        P(),
        P(AXES, None),
        P(AXES, None),
        P(AXES, None),
        P(AXES, None, None),
        P(AXES),
    )
    out_specs = (P(AXES, None), P(AXES, None), P(AXES), P())
    return jax.shard_map(body, mesh=inner, in_specs=in_specs, out_specs=out_specs, check_vma=False)
```

time: 141 us -> 126 us (0.89)
  waiting for transfers between devices: 32.8 us -> 15.8 us
  blocking collectives: 59.1 us -> 71.7 us
  starting transfers between devices: 25.7 us -> 16.7 us
  local copies, waits for them, and re-layouts: 8.86 us -> 7.44 us
    ppermute x4, waiting for transfers between devices: 25.7 us -> 12.1 us  [shifted(): return lax.ppermute(value, RIGHT, pairs)]
    all_to_all x5 -> x6, blocking collectives: 59.1 us -> 71.7 us  [exchanged(): return lax.all_to_all(value, axes, split_axis=0, concat_axis=0, tiled=True)]
    all_to_all x1 -> x0, starting transfers between devices: 3.37 us -> none  [exchanged(): return lax.all_to_all(value, axes, split_axis=0, concat_axis=0, tiled=True)]
    all_to_all x1 -> x0, waiting for transfers between devices: 3.23 us -> none  [exchanged(): return lax.all_to_all(value, axes, split_axis=0, concat_axis=0, tiled=True)]
    ppermute x4, starting transfers between devices: 9.34 us -> 6.51 us  [swapped(): return lax.ppermute(value, 'c', [(0, 1), (1, 0)])]
    ppermute x4, starting transfers between devices: 13 us -> 10.2 us  [shifted(): return lax.ppermute(value, RIGHT, pairs)]
    unnamed x19 -> x18, local copies, waits for them, and re-layouts: 6.48 us -> 5.78 us
  transfers between devices with their start and end apart: 9 -> 8, of which waited for: 6 -> 4; matrix products, arithmetic and copies ran while one was open for 1% -> 2% of each run, Pallas kernels for 1% -> 1%
where the time goes in v4:
time: 126 us; the launch traced here: 125 us
  blocking collectives  71.7 us (57%)
  starting transfers between devices  16.7 us (13%)
  waiting for transfers between devices  15.8 us (13%)
  Pallas kernels  10.4 us (8%)
  local copies, waits for them, and re-layouts  7.44 us (6%)
  other arithmetic  1.94 us (2%)
  between operations  1.49 us (1%)
    all_to_all x6, blocking collectives, exchanged(): return lax.all_to_all(value, axes, split_axis=0, concat_axis=0, tiled=True)  71.7 us
    ppermute x4, waiting for transfers between devices, shifted(): return lax.ppermute(value, RIGHT, pairs)  12.1 us
    pallas_call x3, Pallas kernels, call(): pl.pallas_call(kernel, out_shape=shapes, in_specs=[scalar] * scalars + [v...  10.4 us
    ppermute x4, starting transfers between devices, shifted(): return lax.ppermute(value, RIGHT, pairs)  10.2 us
    ppermute x4, starting transfers between devices, swapped(): return lax.ppermute(value, 'c', [(0, 1), (1, 0)])  6.51 us
    unnamed x18, local copies, waits for them, and re-layouts  5.78 us
    ppermute x4, waiting for transfers between devices, swapped(): return lax.ppermute(value, 'c', [(0, 1), (1, 0)])  3.62 us
  transfers between devices with their start and end apart: 8, of which 4 were waited for; matrix products, arithmetic and copies ran while one was open for 2% of the time, Pallas kernels for 1%

profile of v4, /device:TPU:1, one launch (start us, length us, event | category | flops | bytes accessed | tf_op | source)
XLA Modules:
  0.0 125.4 jit_solution(5694101174829175047)
XLA Ops:
  0.6 5.8 %collective-permute-start = (f32[400,384]{1,0:T(8,128)}, f32[400,384]{1,0:T(8,128)S(1)}, u32[]{:S(2)}, u32[]{:S(2)}) collective-permute-start(f32[400,384]{1,0:T(8,128)} %bitcast.61), channel_id=1, source_target_pairs={{0,5},{1,6},{2,7},{3,8},{4,9},{5,10},{6,11},{7,12},{8,13},{9,14},{... | collective-permute-start | bytes 1843208 | tf_op jit(solution)/shard_map/ppermute | solution.py:172
  7.9 0.7 slice-done
  9.4 0.7 copy-done.6
  11.0 1.1 copy-done
  12.0 1.0 copy-done.1
  13.0 1.0 copy-done.2
  14.1 1.6 %shard_map.138 = (f32[400,512]{1,0:T(8,128)S(1)}, f32[400,512]{1,0:T(8,128)S(1)}, f32[384,2]{1,0:T(8,128)S(1)}, f32[32,128]{1,0:T(8,128)S(1)}, f32[32,128]{1,0:T(8,128)S(1)}, /*index=5*/f32[1,384]{1,0:T(1,128)S(1)}) custom-call(s32[2]{0:T(128)S(1)} %pad_add_fusion.place_ref, f32[400,384]{1,0:T(8,128)S(1)} %bitcast.39, f32[400,256]{1,0:T(8,128)S(1)} %bitcast.41, ...), custom_call_target="tpu_custom_call" | custom-call | flops 805306368 | bytes 3135496 | tf_op jit(solution)/shard_map/pallas_call | solution.py:158
  15.9 12.1 %collective-permute-done.1.dst_state_ref = f32[1,384]{1,0:T(1,128)S(1)} collective-permute-done((f32[1,384]{1,0:T(1,128)S(1)}, f32[1,384]{1,0:T(1,128)S(1)}, u32[]{:S(2)}, u32[]{:S(2)}) %collective-permute-start.1) | collective-permute-done | bytes 1568 | tf_op jit(solution)/shard_map/ppermute | solution.py:172
  28.0 4.0 %shard_map.139 = (f32[512,128]{1,0:T(8,128)S(1)}, f32[512,128]{1,0:T(8,128)S(1)}, f32[400,384]{1,0:T(8,128)S(1)}, f32[1,384]{1,0:T(1,128)S(1)}, f32[400,384]{1,0:T(8,128)S(1)}, /*index=5*/f32[1,384]{1,0:T(1,128)S(1)}) custom-call(f32[400,512]{1,0:T(8,128)S(1)} %get-tuple-element.28.sources_ref, f32[400,512]{1,0:T(8,128)S(1)} %get-tuple-element.29.relations_ref, ...), custom_call_target="tpu_custom_call" | custom-call | flops 2617245696 | bytes 4645888 | tf_op jit(solution)/shard_map/pallas_call | solution.py:158
  32.1 1.5 %collective-permute-done.2 = f32[512,128]{1,0:T(8,128)S(1)} collective-permute-done((f32[512,128]{1,0:T(8,128)S(1)}, f32[512,128]{1,0:T(8,128)S(1)}, u32[]{:S(2)}, u32[]{:S(2)}) %collective-permute-start.2) | collective-permute-done | bytes 262176 | tf_op jit(solution)/shard_map/ppermute | solution.py:176
  33.7 12.4 %all_to_all.30 = f32[16,32,128]{2,1,0:T(8,128)S(1)} all-to-all(f32[16,32,128]{2,1,0:T(8,128)S(1)} %bitcast.43), channel_id=1, replica_groups=mesh['x'=4,'zh'=2,'y'=4,'zl'=4,'c'=2] {'x','y'}, dimensions={0} | all-to-all | bytes 524288 | tf_op jit(solution)/shard_map/all_to_all | solution.py:180
  46.2 15.8 %all_to_all.31 = f32[8,32,128]{2,1,0:T(8,128)S(1)} all-to-all(f32[8,32,128]{2,1,0:T(8,128)S(1)} %broadcast_in_dim.23), channel_id=1, replica_groups=mesh['x'=4,'zh'=2,'y'=4,'zl'=4,'c'=2] {'zh','zl'}, dimensions={0} | all-to-all | bytes 262144 | tf_op jit(solution)/shard_map/all_to_all | solution.py:180
  62.0 10.8 %all_to_all.32 = f32[16,32,128]{2,1,0:T(8,128)S(1)} all-to-all(f32[16,32,128]{2,1,0:T(8,128)S(1)} %broadcast_in_dim.24), channel_id=1, replica_groups=mesh['x'=4,'zh'=2,'y'=4,'zl'=4,'c'=2] {'x','y'}, dimensions={0} | all-to-all | bytes 524288 | tf_op jit(solution)/shard_map/all_to_all | solution.py:180
  72.9 4.1 %collective-permute-start.3 = (f32[512,128]{1,0:T(8,128)S(1)}, f32[512,128]{1,0:T(8,128)S(1)}, u32[]{:S(2)}, u32[]{:S(2)}) collective-permute-start(f32[512,128]{1,0:T(8,128)S(1)} %bitcast.37), channel_id=1, source_target_pairs={{0,1},{1,0},{2,3},{3,2},{4,5},{5,4},{6,7},{7,6},{8,9},{9,8},{10,11... | collective-permute-start | bytes 786440 | tf_op jit(solution)/shard_map/ppermute | solution.py:176
  76.9 1.2 collective-permute-done.3.rel_other_ref
  78.1 4.7 %shard_map.140 = (f32[512,128]{1,0:T(8,128)S(1)}, f32[512,128]{1,0:T(8,128)S(1)}, f32[400,384]{1,0:T(8,128)}, f32[200,384]{1,0:T(8,128)S(1)}, f32[208,384]{1,0:T(8,128)S(1)}) custom-call(f32[512,128]{1,0:T(8,128)S(1)} %bitcast.38, f32[512,128]{1,0:T(8,128)S(1)} %collective-permute-done.3.rel_other_ref, f32[400,384]{1,0:T(8,128)S(1)} %get-tuple-element.37.dst_ref, ...), custom_call_target="tpu_custom_call" | custom-call | flops 3422552064 | bytes 3540992 | tf_op jit(solution)/shard_map/pallas_call | solution.py:158
  83.7 0.9 collective-permute-done.4
  84.7 10.7 %all_to_all.33 = f32[16,32,128]{2,1,0:T(8,128)S(1)} all-to-all(f32[16,32,128]{2,1,0:T(8,128)S(1)} %bitcast.44), channel_id=1, replica_groups=mesh['x'=4,'zh'=2,'y'=4,'zl'=4,'c'=2] {'x','y'}, dimensions={0} | all-to-all | bytes 524288 | tf_op jit(solution)/shard_map/all_to_all | solution.py:180
  95.5 11.3 %all_to_all.34 = f32[8,32,128]{2,1,0:T(8,128)S(1)} all-to-all(f32[8,32,128]{2,1,0:T(8,128)S(1)} %broadcast_in_dim.25), channel_id=1, replica_groups=mesh['x'=4,'zh'=2,'y'=4,'zl'=4,'c'=2] {'zh','zl'}, dimensions={0} | all-to-all | bytes 262144 | tf_op jit(solution)/shard_map/all_to_all | solution.py:180
  106.8 4.0 %collective-permute-start.6 = (f32[208,384]{1,0:T(8,128)S(1)}, f32[208,384]{1,0:T(8,128)S(1)}, u32[]{:S(2)}, u32[]{:S(2)}) collective-permute-start(f32[208,384]{1,0:T(8,128)S(1)} %get-tuple-element.48), channel_id=1, source_target_pairs={{0,27},{1,28},{2,29},{3,30},{4,31},{5,0},{6,1},{7,2},{8,3},{9,4},{... | collective-permute-start | bytes 958472 | tf_op jit(solution)/shard_map/ppermute | solution.py:172
  110.8 10.6 %all_to_all.35 = f32[16,32,128]{2,1,0:T(8,128)S(1)} all-to-all(f32[16,32,128]{2,1,0:T(8,128)S(1)} %broadcast_in_dim.26), channel_id=1, replica_groups=mesh['x'=4,'zh'=2,'y'=4,'zl'=4,'c'=2] {'x','y'}, dimensions={0} | all-to-all | bytes 524288 | tf_op jit(solution)/shard_map/all_to_all | solution.py:180
  121.4 1.7 %collective-permute-start.7 = (f32[512,128]{1,0:T(8,128)S(1)}, f32[512,128]{1,0:T(8,128)S(1)}, u32[]{:S(2)}, u32[]{:S(2)}) collective-permute-start(f32[512,128]{1,0:T(8,128)S(1)} %bitcast.45), channel_id=1, source_target_pairs={{0,1},{1,0},{2,3},{3,2},{4,5},{5,4},{6,7},{7,6},{8,9},{9,8},{10,11... | collective-permute-start | bytes 786440 | tf_op jit(solution)/shard_map/ppermute | solution.py:176
  123.7 0.9 maximum_bitcast_fusion
  124.7 0.8 fusion
  (59 shorter events, 4.5 us)
Async XLA Ops:
  0.6 27.4 %collective-permute-start = (f32[400,384]{1,0:T(8,128)}, f32[400,384]{1,0:T(8,128)S(1)}, u32[]{:S(2)}, u32[]{:S(2)}) collective-permute-start(f32[400,384]{1,0:T(8,128)} %bitcast.61), channel_id=1, source_target_pairs={{0,5},{1,6},{2,7},{3,8},{4,9},{5,10},{6,11},{7,12},{8,13},{9,14},{... | collective-permute-start | bytes 1843208 | tf_op jit(solution)/shard_map/ppermute | solution.py:172
  6.4 0.7 copy-start.7
  7.1 0.7 copy-start.3
  7.9 0.7 slice-start
  8.6 0.7 copy-start.5
  9.3 0.7 copy-start.6
  10.1 0.7 copy-start.4
  11.0 1.1 copy-start
  12.0 1.0 copy-start.1
  13.0 1.0 copy-start.2
  14.0 1.8 %copy-start.8 = (f32[384]{0:T(512)S(1)}, f32[384]{0:T(512)}, u32[]{:S(2)}) copy-start(f32[384]{0:T(512)} %param.12) | copy-start | bytes 4612
  15.7 12.3 %collective-permute-start.1 = (f32[1,384]{1,0:T(1,128)S(1)}, f32[1,384]{1,0:T(1,128)S(1)}, u32[]{:S(2)}, u32[]{:S(2)}) collective-permute-start(f32[1,384]{1,0:T(1,128)S(1)} %get-tuple-element.30), channel_id=1, source_target_pairs={{0,5},{1,6},{2,7},{3,8},{4,9},{5,10},{6,11},{7,12},{8,13},{9,14},{... | collective-permute-start | bytes 4616 | tf_op jit(solution)/shard_map/ppermute | solution.py:172
  32.0 1.6 %collective-permute-start.2 = (f32[512,128]{1,0:T(8,128)S(1)}, f32[512,128]{1,0:T(8,128)S(1)}, u32[]{:S(2)}, u32[]{:S(2)}) collective-permute-start(f32[512,128]{1,0:T(8,128)S(1)} %get-tuple-element.35), channel_id=1, source_target_pairs={{0,1},{1,0},{2,3},{3,2},{4,5},{5,4},{6,7},{7,6},{8,9},{9,8},{10,11... | collective-permute-start | bytes 786440 | tf_op jit(solution)/shard_map/ppermute | solution.py:176
  72.9 5.3 %collective-permute-start.3 = (f32[512,128]{1,0:T(8,128)S(1)}, f32[512,128]{1,0:T(8,128)S(1)}, u32[]{:S(2)}, u32[]{:S(2)}) collective-permute-start(f32[512,128]{1,0:T(8,128)S(1)} %bitcast.37), channel_id=1, source_target_pairs={{0,1},{1,0},{2,3},{3,2},{4,5},{5,4},{6,7},{7,6},{8,9},{9,8},{10,11... | collective-permute-start | bytes 786440 | tf_op jit(solution)/shard_map/ppermute | solution.py:176
  82.8 1.8 %collective-permute-start.4 = (f32[512,128]{1,0:T(8,128)S(1)}, f32[512,128]{1,0:T(8,128)S(1)}, u32[]{:S(2)}, u32[]{:S(2)}) collective-permute-start(f32[512,128]{1,0:T(8,128)S(1)} %get-tuple-element.43), channel_id=1, source_target_pairs={{0,1},{1,0},{2,3},{3,2},{4,5},{5,4},{6,7},{7,6},{8,9},{9,8},{10,11... | collective-permute-start | bytes 786440 | tf_op jit(solution)/shard_map/ppermute | solution.py:176
  83.5 12.0 %collective-permute-start.5 = (f32[200,384]{1,0:T(8,128)S(1)}, f32[200,384]{1,0:T(8,128)S(1)}, u32[]{:S(2)}, u32[]{:S(2)}) collective-permute-start(f32[200,384]{1,0:T(8,128)S(1)} %get-tuple-element.44), channel_id=1, source_target_pairs={{0,27},{1,28},{2,29},{3,30},{4,31},{5,0},{6,1},{7,2},{8,3},{9,4},{... | collective-permute-start | bytes 921608 | tf_op jit(solution)/shard_map/ppermute | solution.py:172
  106.8 16.3 %collective-permute-start.6 = (f32[208,384]{1,0:T(8,128)S(1)}, f32[208,384]{1,0:T(8,128)S(1)}, u32[]{:S(2)}, u32[]{:S(2)}) collective-permute-start(f32[208,384]{1,0:T(8,128)S(1)} %get-tuple-element.48), channel_id=1, source_target_pairs={{0,27},{1,28},{2,29},{3,30},{4,31},{5,0},{6,1},{7,2},{8,3},{9,4},{... | collective-permute-start | bytes 958472 | tf_op jit(solution)/shard_map/ppermute | solution.py:172
  121.4 3.2 %collective-permute-start.7 = (f32[512,128]{1,0:T(8,128)S(1)}, f32[512,128]{1,0:T(8,128)S(1)}, u32[]{:S(2)}, u32[]{:S(2)}) collective-permute-start(f32[512,128]{1,0:T(8,128)S(1)} %bitcast.45), channel_id=1, source_target_pairs={{0,1},{1,0},{2,3},{3,2},{4,5},{5,4},{6,7},{7,6},{8,9},{9,8},{10,11... | collective-permute-start | bytes 786440 | tf_op jit(solution)/shard_map/ppermute | solution.py:176

commit v5 on v4

v5 whole, which is shorter than its diff:
```python
import jax
import jax.numpy as jnp
from jax import lax
from jax.experimental import pallas as pl
from jax.experimental.pallas import tpu as pltpu
from jax.sharding import Mesh, PartitionSpec as P

BATCH = 500
BATCHES = 2
NEG = 1000
SHIFT = 5
SLAB = 384
REL = 256
HALF = 128
W = 400
MID = 200
EP = 512
NP = 1024
CUT = 200

ROW_RATE = 0.2
REL_RATE = 1.0

AXES = ("x", "zh", "y", "zl", "c")
PLANE = ("x", "y")
COLUMN = ("zh", "zl")
RIGHT = ("y", "zl", "c")

NN = (((1,), (0,)), ((), ()))
NT = (((1,), (1,)), ((), ()))
TN = (((0,), (0,)), ((), ()))


def parts(value):
    high = value.astype(jnp.bfloat16)
    low = (value - high.astype(jnp.float32)).astype(jnp.bfloat16)
    return (high, low)


def dot(first, second, dims):
    return lax.dot_general(first, second, dims, preferred_element_type=jnp.float32)


def joined(values, axis):
    return jnp.concatenate(values, axis=axis)


def dot3(first, second, dims):
    (one,), (two,) = dims[0]
    return dot(joined([first[0], first[0], first[1]], one), joined([second[0], second[1], second[0]], two), dims)


def pick(rows, ids):
    return (lax.broadcasted_iota(jnp.int32, (rows, EP), 0) == ids).astype(jnp.bfloat16)


def gather(table, hot):
    return dot(joined(parts(table), 1), joined([hot, hot], 0), NN)


def scatter(values, hot):
    high, low = parts(values)
    return dot(high, hot, NT) + dot(low, hot, NT)


def entity_update(table, state, grad):
    state = state + jnp.sum(grad * grad, axis=0, keepdims=True) * (1.0 / W)
    return (table - grad * (ROW_RATE / jnp.sqrt(state)), state)


def query(sources, relations):
    s_re, s_im = (sources[:MID], sources[MID:])
    r_re, r_im = (relations[:MID], relations[MID:])
    return parts(jnp.concatenate([s_re * r_re - s_im * r_im, s_re * r_im + s_im * r_re], axis=0))


def against(grads, other):
    g_re, g_im = (grads[:MID], grads[MID:])
    o_re, o_im = (other[:MID], other[MID:])
    return jnp.concatenate([g_re * o_re + g_im * o_im, g_im * o_re - g_re * o_im], axis=0)


def edge_weights(logits, dst_ids, counts):
    hit = lax.broadcasted_iota(jnp.int32, (SLAB, EP), 0) == dst_ids
    positive = jnp.where(hit, 0.5, 0.0)
    return parts((counts - positive) + (counts + positive) * jnp.tanh(0.5 * logits))


def put(refs, values):
    for ref, value in zip(refs, values, strict=True):
        ref[...] = value


def put(refs, values):
    for ref, value in zip(refs, values, strict=True):
        ref[...] = value


def relation_side(batch, sources, relations, dst_ref, ids_ref, counts_ref, mine_ref, other_ref, way_ref, query_refs, weight_refs):
    queries, rows = (query(sources, relations), parts(dst_ref[...]))
    put(query_refs, queries)
    dst_ids = ids_ref[2 + batch : 3 + batch, :]
    weights = edge_weights(dot3(rows, queries, TN), dst_ids, counts_ref[:, batch : batch + 1])
    put(weight_refs, weights)
    grads = dot3(rows, weights, NN)
    rel_grad = scatter(against(grads, sources), pick(REL, ids_ref[5 + batch : 6 + batch, :]))
    put((mine_ref, other_ref), (rel_grad[:, :HALF], rel_grad[:, HALF:]))
    way_ref[...] = against(grads, relations)


def target_update(query_refs, weight_refs, dst_ref, dst_state_ref):
    queries, weights = [tuple(ref[...] for ref in refs) for refs in (query_refs, weight_refs)]
    return entity_update(dst_ref[...], dst_state_ref[...], dot3(queries, weights, NT))


def source_update(batch, way_ref, src_ref, src_state_ref, ids_ref):
    src_grad = scatter(way_ref[...], pick(SLAB, ids_ref[batch : batch + 1, :]))
    return entity_update(src_ref[...], src_state_ref[...], src_grad)


def prepare_kernel(
    place_ref, src_ref, rel_ref, rel_state_ref, ids_ref, neg_ref, dst_state_ref,
    sources_ref, relations_ref, counts_ref, own_ref, own_sums_ref, dst_state_out,
):
    sources_ref[...] = gather(src_ref[...], pick(SLAB, ids_ref[0:1, :]))
    relations_ref[...] = gather(rel_ref[...], pick(REL, ids_ref[4:5, :]))
    for batch in range(BATCHES):
        same = lax.broadcasted_iota(jnp.int32, (SLAB, NP), 0) == neg_ref[batch : batch + 1, :]
        total = jnp.sum(jnp.where(same, 1.0, 0.0), axis=1, keepdims=True)
        counts_ref[:, batch : batch + 1] = total * (0.5 / NEG)
    for source, target in ((rel_ref, own_ref), (rel_state_ref, own_sums_ref)):
        target[...] = jnp.where(place_ref[0] == 0, source[:, :HALF], source[:, HALF:])
    dst_state_out[...] = dst_state_ref[...]


def first_relation_kernel(sources_ref, relations_ref, dst_ref, ids_ref, counts_ref, mine_ref, other_ref, way_ref, *kept):
    relation_side(
        0, sources_ref[...], relations_ref[...], dst_ref, ids_ref, counts_ref, mine_ref, other_ref, way_ref, kept[:2], kept[2:]
    )


def first_entity_kernel(
    way_ref, high_ref, low_ref, weight_high_ref, weight_low_ref, dst_ref, dst_state_ref, src_ref, src_state_ref, ids_ref,
    src_out, src_state_out, dst_out, dst_state_out,
):
    src_out[...], src_state_out[...] = source_update(0, way_ref, src_ref, src_state_ref, ids_ref)
    dst_out[...], dst_state_out[...] = target_update(
        (high_ref, low_ref), (weight_high_ref, weight_low_ref), dst_ref, dst_state_ref
    )


def gather_kernel(src_ref, ids_ref, sources_ref):
    sources_ref[...] = gather(src_ref[...], pick(SLAB, ids_ref[1:2, :]))


def second_relation_kernel(
    rel_mine_ref, rel_other_ref, sources_ref, dst_ref, ids_ref, counts_ref, mine_ref, other_ref, way_ref, *kept
):
    relation = jnp.concatenate([rel_mine_ref[...], rel_other_ref[...]], axis=1)
    relations = gather(relation, pick(REL, ids_ref[6:7, :]))
    relation_side(
        1, sources_ref[...], relations, dst_ref, ids_ref, counts_ref, mine_ref, other_ref, way_ref, kept[:2], kept[2:]
    )


def second_target_kernel(
    high_ref, low_ref, weight_high_ref, weight_low_ref, dst_ref, dst_state_ref, upper_out, lower_out
):
    dst_table, dst_state = target_update((high_ref, low_ref), (weight_high_ref, weight_low_ref), dst_ref, dst_state_ref)
    upper_out[...] = dst_table[:CUT]
    lower_out[: W - CUT, :] = dst_table[CUT:]
    lower_out[W - CUT :, :] = jnp.broadcast_to(dst_state, (8, SLAB))


def last_kernel(
    way_ref, src_ref, src_state_ref, ids_ref, upper_ref, lower_ref, src_out, dst_out, dst_state_out, sem
):
    copies = [
        pltpu.make_async_copy(upper_ref, dst_out.at[pl.ds(0, CUT)], sem.at[0]),
        pltpu.make_async_copy(lower_ref.at[pl.ds(0, W - CUT)], dst_out.at[pl.ds(CUT, W - CUT)], sem.at[1]),
    ]
    for copy in copies:
        copy.start()
    dst_state_out[...] = lower_ref[W - CUT :, :][0]
    src_out[...], _ = source_update(1, way_ref, src_ref, src_state_ref, ids_ref)
    for copy in copies:
        copy.wait()


def call(kernel, outs, *args, scalars=0, scratch=(), passes=0, spaces=None):
    shapes = [shape if isinstance(shape, jax.ShapeDtypeStruct) else jax.ShapeDtypeStruct(shape, jnp.float32) for shape in outs]
    vector = pl.BlockSpec(memory_space=pltpu.VMEM)
    scalar = pl.BlockSpec(memory_space=pltpu.SMEM)
    moved = sum(value.size * value.dtype.itemsize for value in (*args, *shapes))
    return pl.pallas_call(
        kernel,
        out_shape=shapes,
        in_specs=[scalar] * scalars + [vector] * (len(args) - scalars),
        out_specs=spaces or [vector] * len(shapes),
        scratch_shapes=scratch,
        cost_estimate=pl.CostEstimate(flops=passes * 2 * EP * EP * SLAB, bytes_accessed=moved, transcendentals=0),
        compiler_params=pltpu.CompilerParams(vmem_limit_bytes=16 * 1024 * 1024),
    )(*args)


def shifted(value, steps):
    count = lax.axis_size(RIGHT)
    pairs = [(source, (source + steps) % count) for source in range(count)]
    return lax.ppermute(value, RIGHT, pairs)


def swapped(value):
    return lax.ppermute(value, "c", [(0, 1), (1, 0)])


def exchanged(value, axes):
    return lax.all_to_all(value, axes, split_axis=0, concat_axis=0, tiled=True)


def chip_half(mine, other):
    return mine + swapped(other)


def own_part(half):
    height = W // lax.axis_size(PLANE)
    return lax.dynamic_slice_in_dim(half, lax.axis_index(PLANE) * height, height, 0).reshape(-1)


def relation_update(half, own, own_sums, upper=None, lower=None, late=None):
    lanes, layers = (lax.axis_size(PLANE), lax.axis_size(COLUMN))
    total = jnp.sum(exchanged(half.reshape(lanes, 1, -1), PLANE), axis=(0, 1))
    if upper is not None:
        total, upper = lax.optimization_barrier((total, shifted(upper, -SHIFT)))
    total = jnp.sum(exchanged(jnp.broadcast_to(total, (layers, 1, *own.shape)), COLUMN), axis=(0, 1))
    if lower is not None:
        total, lower, late = lax.optimization_barrier((total, lower, late))
        lower = shifted(lower, -SHIFT)
    own_sums = own_sums + total * total
    own = own - REL_RATE * total / jnp.sqrt(own_sums)
    half = exchanged(jnp.broadcast_to(own, (lanes, 1, *own.shape)), PLANE).reshape(W, HALF)
    return (half, own, own_sums, upper, lower, late)


def padded(value, live, low):
    picked = value[low : low + BATCH]
    spot = lax.iota(jnp.int32, BATCH) + low
    return jnp.pad(jnp.where(spot < live, picked, -1), (0, EP - BATCH), constant_values=-1)


def body(
    src_embed, src_state, dst_embed, dst_state, relation, rel_state, edge_src, edge_dst, edge_rel, neg_rows, edge_count
):
    dst_table = shifted(dst_embed.T, SHIFT)
    core = lax.axis_index("c")
    live = edge_count[0]
    near_rel = edge_rel[0] ^ (core * HALF)
    ids = jnp.stack(
        [
            padded(edge_src[0], live, 0),
            padded(edge_src[0], live, BATCH),
            padded(edge_dst[0], live, 0),
            padded(edge_dst[0], live, BATCH),
            padded(edge_rel[0], live, 0),
            padded(near_rel, live, 0),
            padded(near_rel, live, BATCH),
            jnp.full((EP,), -1, jnp.int32),
        ]
    )
    negs = jnp.pad(neg_rows[0], ((0, 0), (0, NP - NEG)), constant_values=-1)
    place = core.reshape(1).astype(jnp.int32)
    src_table, src_sums = (src_embed.T, src_state.reshape(1, SLAB))

    flat = (1, SLAB)
    sources, relations, counts, own, own_sums, dst_sums = call(
        prepare_kernel,
        [(W, EP), (W, EP), (SLAB, BATCHES), (W, HALF), (W, HALF), flat],
        place, src_table, relation.T, rel_state.T, ids, negs, dst_state.reshape(flat),
        scalars=1, passes=4,
    )
    dst_sums, own, own_sums = lax.optimization_barrier((dst_sums, own_part(own), own_part(own_sums)))
    dst_table, dst_sums = lax.optimization_barrier((dst_table, shifted(dst_sums, SHIFT)))
    kept = [
        (W, EP),
        *[jax.ShapeDtypeStruct((W, EP), jnp.bfloat16)] * 2,
        *[jax.ShapeDtypeStruct((SLAB, EP), jnp.bfloat16)] * 2,
    ]
    mine, other, *kept_values = call(
        first_relation_kernel, [(W, HALF), (W, HALF), *kept], sources, relations, dst_table, ids, counts, passes=8
    )
    half = chip_half(mine, other)
    half, *tables = lax.optimization_barrier(
        (
            half,
            *call(
                first_entity_kernel,
                [(W, SLAB), flat, (W, SLAB), flat],
                *kept_values, dst_table, dst_sums, src_table, src_sums, ids, passes=5,
            ),
        )
    )
    near, own, own_sums, *_ = relation_update(half, own, own_sums)
    near, *tables = lax.optimization_barrier((near, *tables))
    src_table, src_sums, dst_table, dst_sums = tables
    (sources,) = call(gather_kernel, [(W, EP)], src_table, ids, passes=2)
    mine, other, way, *kept_values = call(
        second_relation_kernel,
        [(W, HALF), (W, HALF), *kept],
        near, swapped(near), sources, dst_table, ids, counts, passes=10,
    )
    half = chip_half(mine, other)
    half, upper, lower = lax.optimization_barrier(
        (
            half,
            *call(
                second_target_kernel,
                [(CUT, SLAB), (W + 8 - CUT, SLAB)],
                *kept_values, dst_table, dst_sums, passes=3,
            ),
        )
    )
    near, own, own_sums, upper, lower, way = relation_update(half, own, own_sums, upper, lower, way)
    near, lower = lax.optimization_barrier((near, lower))
    vector = pl.BlockSpec(memory_space=pltpu.VMEM)
    src_table, dst_table, dst_sums = call(
        last_kernel,
        [(W, SLAB), (W, SLAB), (SLAB,)],
        way, src_table, src_sums, ids, upper, lower,
        scratch=[pltpu.SemaphoreType.DMA((2,))], passes=2, spaces=[vector, pl.BlockSpec(memory_space=pl.ANY), vector],
    )
    far = swapped(near)
    first = core == 0
    relation = jnp.concatenate([jnp.where(first, near, far), jnp.where(first, far, near)], axis=1)
    return (src_table.T, dst_table.T, dst_sums, relation.T)


def solution(mesh):
    left, right = (mesh.shape["left"], mesh.shape["right"])
    devices = mesh.devices.reshape(left // 2, 2, 4, right // 8, 2)
    inner = Mesh(devices, AXES)
    in_specs = (
        P(AXES, None),
        P(AXES),
        P(AXES, None),
        P(AXES),
        P(),
        P(),
        P(AXES, None),
        P(AXES, None),
        P(AXES, None),
        P(AXES, None, None),
        P(AXES),
    )
    out_specs = (P(AXES, None), P(AXES, None), P(AXES), P())
    return jax.shard_map(body, mesh=inner, in_specs=in_specs, out_specs=out_specs, check_vma=False)
```

time: 126 us -> 122 us (0.968)
  blocking collectives: 71.7 us -> 69.4 us
  waiting for transfers between devices: 15.8 us -> 13.6 us
    ppermute x4, waiting for transfers between devices: 3.62 us -> 0.69 us  [swapped(): return lax.ppermute(value, 'c', [(0, 1), (1, 0)])]
    all_to_all x6, blocking collectives: 71.7 us -> 69.4 us  [exchanged(): return lax.all_to_all(value, axes, split_axis=0, concat_axis=0, tiled=True)]
    pallas_call x3 -> x7, Pallas kernels: 10.4 us -> 10.6 us  [call(): pl.pallas_call(kernel, out_shape=shapes, in_specs=[scalar] * scalars + [v...]
    unnamed x18 -> x20, local copies, waits for them, and re-layouts: 5.78 us -> 5.66 us
  transfers between devices with their start and end apart: 8 -> 8, of which waited for: 4 -> 3; matrix products, arithmetic and copies ran while one was open for 2% -> 0% of each run, Pallas kernels for 1% -> 5%
where the time goes in v5:
time: 122 us; the launch traced here: 121 us
  blocking collectives  69.4 us (57%)
  starting transfers between devices  17.9 us (15%)
  waiting for transfers between devices  13.6 us (11%)
  Pallas kernels  10.6 us (9%)
  local copies, waits for them, and re-layouts  6.99 us (6%)
  between operations  1.61 us (1%)
  other arithmetic  1.34 us (1%)
    all_to_all x6, blocking collectives, exchanged(): return lax.all_to_all(value, axes, split_axis=0, concat_axis=0, tiled=True)  69.4 us
    ppermute x4, waiting for transfers between devices, shifted(): return lax.ppermute(value, RIGHT, pairs)  12.9 us
    ppermute x4, starting transfers between devices, shifted(): return lax.ppermute(value, RIGHT, pairs)  10.7 us
    pallas_call x7, Pallas kernels, call(): pl.pallas_call(kernel, out_shape=shapes, in_specs=[scalar] * scalars + [v...  10.6 us
    ppermute x4, starting transfers between devices, swapped(): return lax.ppermute(value, 'c', [(0, 1), (1, 0)])  7.21 us
    unnamed x20, local copies, waits for them, and re-layouts  5.66 us
  transfers between devices with their start and end apart: 8, of which 3 were waited for; matrix products, arithmetic and copies ran while one was open for 0% of the time, Pallas kernels for 5%

profile of v5, /device:TPU:1, one launch (start us, length us, event | category | flops | bytes accessed | tf_op | source)
XLA Modules:
  0.0 121.4 jit_solution(8299078034430233229)
XLA Ops:
  0.6 5.8 %collective-permute-start = (f32[400,384]{1,0:T(8,128)}, f32[400,384]{1,0:T(8,128)S(1)}, u32[]{:S(2)}, u32[]{:S(2)}) collective-permute-start(f32[400,384]{1,0:T(8,128)} %bitcast.62), channel_id=1, source_target_pairs={{0,5},{1,6},{2,7},{3,8},{4,9},{5,10},{6,11},{7,12},{8,13},{9,14},{... | collective-permute-start | bytes 1843208 | tf_op jit(solution)/shard_map/ppermute | solution.py:209
  8.6 0.7 slice-done
  9.3 0.7 copy-done.8
  10.8 1.1 copy-done
  11.9 1.0 copy-done.2
  12.9 1.0 copy-done.3
  13.9 1.0 shard_map.138
  15.1 12.9 %collective-permute-done.1.dst_state_ref = f32[1,384]{1,0:T(1,128)S(1)} collective-permute-done((f32[1,384]{1,0:T(1,128)S(1)}, f32[1,384]{1,0:T(1,128)S(1)}, u32[]{:S(2)}, u32[]{:S(2)}) %collective-permute-start.1) | collective-permute-done | bytes 1568 | tf_op jit(solution)/shard_map/ppermute | solution.py:209
  28.0 2.4 %shard_map.139 = (f32[400,128]{1,0:T(8,128)S(1)}, f32[400,128]{1,0:T(8,128)S(1)}, f32[400,512]{1,0:T(8,128)S(1)}, bf16[400,512]{1,0:T(8,128)(2,1)S(1)}, bf16[400...) custom-call(f32[400,512]{1,0:T(8,128)S(1)} %get-tuple-element.62.sources_ref, ...), custom_call_target="tpu_custom_call" | custom-call | flops 1610612736 | bytes 5106688 | tf_op jit(solution)/shard_map/pallas_call | solution.py:195
  30.5 1.5 %shard_map.140 = (f32[400,384]{1,0:T(8,128)S(1)}, f32[1,384]{1,0:T(1,128)S(1)}, f32[400,384]{1,0:T(8,128)S(1)}, f32[1,384]{1,0:T(1,128)S(1)}) custom-call(f32[400,512]{1,0:T(8,128)S(1)} %get-tuple-element.69.way_ref, bf16[400,512]{1,0:T(8,128)(2,1)S(1)} %get-tuple-element.70.high_ref, bf16[400,512]{1,0:T(8,128)(2,1)S(1)} %get-tuple-element.71.low_ref, ...), custom_call_target="tpu_custom_call" | custom-call | flops 1006632960 | bytes 4904960 | tf_op jit(solution)/shard_map/pallas_call | solution.py:195
  32.0 11.9 %all_to_all.30 = f32[16,1,3200]{2,1,0:T(1,128)S(1)} all-to-all(f32[16,1,3200]{2,1,0:T(1,128)S(1)} %bitcast.46), channel_id=1, replica_groups=mesh['x'=4,'zh'=2,'y'=4,'zl'=4,'c'=2] {'x','y'}, dimensions={0} | all-to-all | bytes 409600 | tf_op jit(solution)/shard_map/all_to_all | solution.py:217
  44.1 15.5 %all_to_all.31 = f32[8,1,3200]{2,1,0:T(1,128)S(1)} all-to-all(f32[8,1,3200]{2,1,0:T(1,128)S(1)} %broadcast_in_dim.23), channel_id=1, replica_groups=mesh['x'=4,'zh'=2,'y'=4,'zl'=4,'c'=2] {'zh','zl'}, dimensions={0} | all-to-all | bytes 204800 | tf_op jit(solution)/shard_map/all_to_all | solution.py:217
  59.8 10.2 %all_to_all.32 = f32[16,1,3200]{2,1,0:T(1,128)S(1)} all-to-all(f32[16,1,3200]{2,1,0:T(1,128)S(1)} %broadcast_in_dim.24), channel_id=1, replica_groups=mesh['x'=4,'zh'=2,'y'=4,'zl'=4,'c'=2] {'x','y'}, dimensions={0} | all-to-all | bytes 409600 | tf_op jit(solution)/shard_map/all_to_all | solution.py:217
  70.1 4.4 %collective-permute-start.3 = (f32[400,128]{1,0:T(8,128)S(1)}, f32[400,128]{1,0:T(8,128)S(1)}, u32[]{:S(2)}, u32[]{:S(2)}) collective-permute-start(f32[400,128]{1,0:T(8,128)S(1)} %bitcast.37), channel_id=1, source_target_pairs={{0,1},{1,0},{2,3},{3,2},{4,5},{5,4},{6,7},{7,6},{8,9},{9,8},{10,11... | collective-permute-start | bytes 614408 | tf_op jit(solution)/shard_map/ppermute | solution.py:213
  75.5 2.5 %shard_map.142 = (f32[400,128]{1,0:T(8,128)S(1)}, f32[400,128]{1,0:T(8,128)S(1)}, f32[400,512]{1,0:T(8,128)S(1)}, bf16[400,512]{1,0:T(8,128)(2,1)S(1)}, bf16[400...) custom-call(f32[400,128]{1,0:T(8,128)S(1)} %bitcast.38, ...), custom_call_target="tpu_custom_call" | custom-call | flops 2013265920 | bytes 4697088 | tf_op jit(solution)/shard_map/pallas_call | solution.py:195
  78.5 0.9 shard_map.143
  79.6 1.3 %collective-permute-start.5 = (f32[200,384]{1,0:T(8,128)S(1)}, f32[200,384]{1,0:T(8,128)S(1)}, u32[]{:S(2)}, u32[]{:S(2)}) collective-permute-start(f32[200,384]{1,0:T(8,128)S(1)} %get-tuple-element.98), channel_id=1, source_target_pairs={{0,27},{1,28},{2,29},{3,30},{4,31},{5,0},{6,1},{7,2},{8,3},{9,4},{... | collective-permute-start | bytes 921608 | tf_op jit(solution)/shard_map/ppermute | solution.py:209
  80.9 10.1 %all_to_all.33 = f32[16,1,3200]{2,1,0:T(1,128)S(1)} all-to-all(f32[16,1,3200]{2,1,0:T(1,128)S(1)} %bitcast.45), channel_id=1, replica_groups=mesh['x'=4,'zh'=2,'y'=4,'zl'=4,'c'=2] {'x','y'}, dimensions={0} | all-to-all | bytes 409600 | tf_op jit(solution)/shard_map/all_to_all | solution.py:217
  91.3 11.7 %all_to_all.34 = f32[8,1,3200]{2,1,0:T(1,128)S(1)} all-to-all(f32[8,1,3200]{2,1,0:T(1,128)S(1)} %broadcast_in_dim.25), channel_id=1, replica_groups=mesh['x'=4,'zh'=2,'y'=4,'zl'=4,'c'=2] {'zh','zl'}, dimensions={0} | all-to-all | bytes 204800 | tf_op jit(solution)/shard_map/all_to_all | solution.py:217
  103.0 3.5 %collective-permute-start.6 = (f32[208,384]{1,0:T(8,128)S(1)}, f32[208,384]{1,0:T(8,128)S(1)}, u32[]{:S(2)}, u32[]{:S(2)}) collective-permute-start(f32[208,384]{1,0:T(8,128)S(1)} %get-tuple-element.106), channel_id=1, source_target_pairs={{0,27},{1,28},{2,29},{3,30},{4,31},{5,0},{6,1},{7,2},{8,3},{9,4},{... | collective-permute-start | bytes 958472 | tf_op jit(solution)/shard_map/ppermute | solution.py:209
  106.6 9.9 %all_to_all.35 = f32[16,1,3200]{2,1,0:T(1,128)S(1)} all-to-all(f32[16,1,3200]{2,1,0:T(1,128)S(1)} %broadcast_in_dim.26), channel_id=1, replica_groups=mesh['x'=4,'zh'=2,'y'=4,'zl'=4,'c'=2] {'x','y'}, dimensions={0} | all-to-all | bytes 409600 | tf_op jit(solution)/shard_map/all_to_all | solution.py:217
  116.5 2.3 %collective-permute-start.7 = (f32[400,128]{1,0:T(8,128)S(1)}, f32[400,128]{1,0:T(8,128)S(1)}, u32[]{:S(2)}, u32[]{:S(2)}) collective-permute-start(f32[400,128]{1,0:T(8,128)S(1)} %bitcast.43), channel_id=1, source_target_pairs={{0,1},{1,0},{2,3},{3,2},{4,5},{5,4},{6,7},{7,6},{8,9},{9,8},{10,11... | collective-permute-start | bytes 614408 | tf_op jit(solution)/shard_map/ppermute | solution.py:213
  118.8 1.7 %shard_map.144 = (f32[400,384]{1,0:T(8,128)}, f32[400,384]{1,0:T(8,128)}, f32[384]{0:T(512)}) custom-call(f32[400,512]{1,0:T(8,128)S(1)} %get-tuple-element.102.way_ref, f32[400,384]{1,0:T(8,128)S(1)} %get-tuple-element.86.src_ref, f32[1,384]{1,0:T(1,128)S(1)} %get-tuple-element.103.src_state_ref, s32[8,512]{1,0:T(8,128)S(1)} %stack.31.ids_ref, ...), custom_call_target="tpu_custom_call" | custom-call | flops 402653184 | bytes 3308544 | tf_op jit(solution)/shard_map/pallas_call | solution.py:195
  120.6 0.8 maximum_bitcast_fusion
  (63 shorter events, 5.1 us)
Async XLA Ops:
  0.6 27.4 %collective-permute-start = (f32[400,384]{1,0:T(8,128)}, f32[400,384]{1,0:T(8,128)S(1)}, u32[]{:S(2)}, u32[]{:S(2)}) collective-permute-start(f32[400,384]{1,0:T(8,128)} %bitcast.62), channel_id=1, source_target_pairs={{0,5},{1,6},{2,7},{3,8},{4,9},{5,10},{6,11},{7,12},{8,13},{9,14},{... | collective-permute-start | bytes 1843208 | tf_op jit(solution)/shard_map/ppermute | solution.py:209
  6.4 0.7 copy-start.4
  7.1 0.7 copy-start.6
  7.8 0.7 copy-start.7
  8.6 0.7 slice-start
  9.3 0.7 copy-start.8
  10.0 0.7 copy-start.5
  10.8 1.1 copy-start
  11.9 1.0 copy-start.2
  12.9 1.0 copy-start.3
  15.0 13.1 %collective-permute-start.1 = (f32[1,384]{1,0:T(1,128)S(1)}, f32[1,384]{1,0:T(1,128)S(1)}, u32[]{:S(2)}, u32[]{:S(2)}) collective-permute-start(f32[1,384]{1,0:T(1,128)S(1)} %get-tuple-element.64), channel_id=1, source_target_pairs={{0,5},{1,6},{2,7},{3,8},{4,9},{5,10},{6,11},{7,12},{8,13},{9,14},{... | collective-permute-start | bytes 4616 | tf_op jit(solution)/shard_map/ppermute | solution.py:209
  28.0 2.5 %copy-start.9 = (f32[384]{0:T(512)S(1)}, f32[384]{0:T(512)}, u32[]{:S(2)}) copy-start(f32[384]{0:T(512)} %param.12) | copy-start | bytes 4612
  28.0 2.5 %copy-start.1 = (f32[384,400]{0,1:T(8,128)S(1)}, f32[384,400]{0,1:T(8,128)}, u32[]{:S(2)}) copy-start(f32[384,400]{0,1:T(8,128)} %param.11) | copy-start | bytes 1843204
  30.4 1.6 %collective-permute-start.2 = (f32[400,128]{1,0:T(8,128)S(1)}, f32[400,128]{1,0:T(8,128)S(1)}, u32[]{:S(2)}, u32[]{:S(2)}) collective-permute-start(f32[400,128]{1,0:T(8,128)S(1)} %get-tuple-element.68), channel_id=1, source_target_pairs={{0,1},{1,0},{2,3},{3,2},{4,5},{5,4},{6,7},{7,6},{8,9},{9,8},{10,11... | collective-permute-start | bytes 614408 | tf_op jit(solution)/shard_map/ppermute | solution.py:213
  70.1 5.4 %collective-permute-start.3 = (f32[400,128]{1,0:T(8,128)S(1)}, f32[400,128]{1,0:T(8,128)S(1)}, u32[]{:S(2)}, u32[]{:S(2)}) collective-permute-start(f32[400,128]{1,0:T(8,128)S(1)} %bitcast.37), channel_id=1, source_target_pairs={{0,1},{1,0},{2,3},{3,2},{4,5},{5,4},{6,7},{7,6},{8,9},{9,8},{10,11... | collective-permute-start | bytes 614408 | tf_op jit(solution)/shard_map/ppermute | solution.py:213
  78.1 1.5 %collective-permute-start.4 = (f32[400,128]{1,0:T(8,128)S(1)}, f32[400,128]{1,0:T(8,128)S(1)}, u32[]{:S(2)}, u32[]{:S(2)}) collective-permute-start(f32[400,128]{1,0:T(8,128)S(1)} %get-tuple-element.89), channel_id=1, source_target_pairs={{0,1},{1,0},{2,3},{3,2},{4,5},{5,4},{6,7},{7,6},{8,9},{9,8},{10,11... | collective-permute-start | bytes 614408 | tf_op jit(solution)/shard_map/ppermute | solution.py:213
  79.6 11.6 %collective-permute-start.5 = (f32[200,384]{1,0:T(8,128)S(1)}, f32[200,384]{1,0:T(8,128)S(1)}, u32[]{:S(2)}, u32[]{:S(2)}) collective-permute-start(f32[200,384]{1,0:T(8,128)S(1)} %get-tuple-element.98), channel_id=1, source_target_pairs={{0,27},{1,28},{2,29},{3,30},{4,31},{5,0},{6,1},{7,2},{8,3},{9,4},{... | collective-permute-start | bytes 921608 | tf_op jit(solution)/shard_map/ppermute | solution.py:209
  103.0 13.5 %collective-permute-start.6 = (f32[208,384]{1,0:T(8,128)S(1)}, f32[208,384]{1,0:T(8,128)S(1)}, u32[]{:S(2)}, u32[]{:S(2)}) collective-permute-start(f32[208,384]{1,0:T(8,128)S(1)} %get-tuple-element.106), channel_id=1, source_target_pairs={{0,27},{1,28},{2,29},{3,30},{4,31},{5,0},{6,1},{7,2},{8,3},{9,4},{... | collective-permute-start | bytes 958472 | tf_op jit(solution)/shard_map/ppermute | solution.py:209
  116.5 4.0 %collective-permute-start.7 = (f32[400,128]{1,0:T(8,128)S(1)}, f32[400,128]{1,0:T(8,128)S(1)}, u32[]{:S(2)}, u32[]{:S(2)}) collective-permute-start(f32[400,128]{1,0:T(8,128)S(1)} %bitcast.43), channel_id=1, source_target_pairs={{0,1},{1,0},{2,3},{3,2},{4,5},{5,4},{6,7},{7,6},{8,9},{9,8},{10,11... | collective-permute-start | bytes 614408 | tf_op jit(solution)/shard_map/ppermute | solution.py:213

commit v6 on v5

--- a/solution.py
+++ b/solution.py
@@ -22,8 +22,8 @@
 REL_RATE = 1.0
 
 AXES = ("x", "zh", "y", "zl", "c")
-PLANE = ("x", "y")
-COLUMN = ("zh", "zl")
+PLANE = ("y", "x")
+COLUMN = ("zl", "zh")
 RIGHT = ("y", "zl", "c")
 
 NN = (((1,), (0,)), ((), ()))
@@ -96,9 +96,10 @@
         ref[...] = value
 
 
-def relation_side(batch, sources, relations, dst_ref, ids_ref, counts_ref, mine_ref, other_ref, way_ref, query_refs, weight_refs):
-    queries, rows = (query(sources, relations), parts(dst_ref[...]))
-    put(query_refs, queries)
+def relation_side(
+    batch, queries, sources, relations, dst_ref, ids_ref, counts_ref, mine_ref, other_ref, way_ref, weight_refs
+):
+    rows = parts(dst_ref[...])
     dst_ids = ids_ref[2 + batch : 3 + batch, :]
     weights = edge_weights(dot3(rows, queries, TN), dst_ids, counts_ref[:, batch : batch + 1])
     put(weight_refs, weights)
@@ -120,10 +121,12 @@
 
 def prepare_kernel(
     place_ref, src_ref, rel_ref, rel_state_ref, ids_ref, neg_ref, dst_state_ref,
-    sources_ref, relations_ref, counts_ref, own_ref, own_sums_ref, dst_state_out,
-):
-    sources_ref[...] = gather(src_ref[...], pick(SLAB, ids_ref[0:1, :]))
-    relations_ref[...] = gather(rel_ref[...], pick(REL, ids_ref[4:5, :]))
+    sources_ref, relations_ref, high_ref, low_ref, counts_ref, own_ref, own_sums_ref, dst_state_out,
+):
+    sources = gather(src_ref[...], pick(SLAB, ids_ref[0:1, :]))
+    relations = gather(rel_ref[...], pick(REL, ids_ref[4:5, :]))
+    put((sources_ref, relations_ref), (sources, relations))
+    put((high_ref, low_ref), query(sources, relations))
     for batch in range(BATCHES):
         same = lax.broadcasted_iota(jnp.int32, (SLAB, NP), 0) == neg_ref[batch : batch + 1, :]
         total = jnp.sum(jnp.where(same, 1.0, 0.0), axis=1, keepdims=True)
@@ -133,9 +136,12 @@
     dst_state_out[...] = dst_state_ref[...]
 
 
-def first_relation_kernel(sources_ref, relations_ref, dst_ref, ids_ref, counts_ref, mine_ref, other_ref, way_ref, *kept):
+def first_relation_kernel(
+    high_ref, low_ref, sources_ref, relations_ref, dst_ref, ids_ref, counts_ref, mine_ref, other_ref, way_ref, *weight_refs
+):
     relation_side(
-        0, sources_ref[...], relations_ref[...], dst_ref, ids_ref, counts_ref, mine_ref, other_ref, way_ref, kept[:2], kept[2:]
+        0, (high_ref[...], low_ref[...]), sources_ref[...], relations_ref[...], dst_ref, ids_ref, counts_ref,
+        mine_ref, other_ref, way_ref, weight_refs,
     )
 
 
@@ -154,12 +160,16 @@
 
 
 def second_relation_kernel(
-    rel_mine_ref, rel_other_ref, sources_ref, dst_ref, ids_ref, counts_ref, mine_ref, other_ref, way_ref, *kept
+    rel_mine_ref, rel_other_ref, sources_ref, dst_ref, ids_ref, counts_ref,
+    mine_ref, other_ref, way_ref, weight_high_ref, weight_low_ref, high_ref, low_ref,
 ):
     relation = jnp.concatenate([rel_mine_ref[...], rel_other_ref[...]], axis=1)
-    relations = gather(relation, pick(REL, ids_ref[6:7, :]))
+    sources, relations = (sources_ref[...], gather(relation, pick(REL, ids_ref[6:7, :])))
+    queries = query(sources, relations)
+    put((high_ref, low_ref), queries)
     relation_side(
-        1, sources_ref[...], relations, dst_ref, ids_ref, counts_ref, mine_ref, other_ref, way_ref, kept[:2], kept[2:]
+        1, queries, sources, relations, dst_ref, ids_ref, counts_ref,
+        mine_ref, other_ref, way_ref, (weight_high_ref, weight_low_ref),
     )
 
 
@@ -271,21 +281,20 @@
     src_table, src_sums = (src_embed.T, src_state.reshape(1, SLAB))
 
     flat = (1, SLAB)
-    sources, relations, counts, own, own_sums, dst_sums = call(
+    query_shapes = [jax.ShapeDtypeStruct((W, EP), jnp.bfloat16)] * 2
+    weight_shapes = [jax.ShapeDtypeStruct((SLAB, EP), jnp.bfloat16)] * 2
+    sources, relations, high, low, counts, own, own_sums, dst_sums = call(
         prepare_kernel,
-        [(W, EP), (W, EP), (SLAB, BATCHES), (W, HALF), (W, HALF), flat],
+        [(W, EP), (W, EP), *query_shapes, (SLAB, BATCHES), (W, HALF), (W, HALF), flat],
         place, src_table, relation.T, rel_state.T, ids, negs, dst_state.reshape(flat),
         scalars=1, passes=4,
     )
     dst_sums, own, own_sums = lax.optimization_barrier((dst_sums, own_part(own), own_part(own_sums)))
     dst_table, dst_sums = lax.optimization_barrier((dst_table, shifted(dst_sums, SHIFT)))
-    kept = [
-        (W, EP),
-        *[jax.ShapeDtypeStruct((W, EP), jnp.bfloat16)] * 2,
-        *[jax.ShapeDtypeStruct((SLAB, EP), jnp.bfloat16)] * 2,
-    ]
-    mine, other, *kept_values = call(
-        first_relation_kernel, [(W, HALF), (W, HALF), *kept], sources, relations, dst_table, ids, counts, passes=8
+    mine, other, way, *weights = call(
+        first_relation_kernel,
+        [(W, HALF), (W, HALF), (W, EP), *weight_shapes],
+        high, low, sources, relations, dst_table, ids, counts, passes=8,
     )
     half = chip_half(mine, other)
     half, *tables = lax.optimization_barrier(
@@ -294,17 +303,16 @@
             *call(
                 first_entity_kernel,
                 [(W, SLAB), flat, (W, SLAB), flat],
-                *kept_values, dst_table, dst_sums, src_table, src_sums, ids, passes=5,
+                way, high, low, *weights, dst_table, dst_sums, src_table, src_sums, ids, passes=5,
             ),
         )
     )
     near, own, own_sums, *_ = relation_update(half, own, own_sums)
-    near, *tables = lax.optimization_barrier((near, *tables))
-    src_table, src_sums, dst_table, dst_sums = tables
+    near, src_table, src_sums, dst_table, dst_sums = lax.optimization_barrier((near, *tables))
     (sources,) = call(gather_kernel, [(W, EP)], src_table, ids, passes=2)
-    mine, other, way, *kept_values = call(
+    mine, other, way, weight_high, weight_low, high, low = call(
         second_relation_kernel,
-        [(W, HALF), (W, HALF), *kept],
+        [(W, HALF), (W, HALF), (W, EP), *weight_shapes, *query_shapes],
         near, swapped(near), sources, dst_table, ids, counts, passes=10,
     )
     half = chip_half(mine, other)
@@ -314,7 +322,7 @@
             *call(
                 second_target_kernel,
                 [(CUT, SLAB), (W + 8 - CUT, SLAB)],
-                *kept_values, dst_table, dst_sums, passes=3,
+                high, low, weight_high, weight_low, dst_table, dst_sums, passes=3,
             ),
         )
     )

time: 122 us -> 121 us (level)
    ppermute x4, starting transfers between devices: 10.7 us -> 12.3 us  [shifted(): return lax.ppermute(value, RIGHT, pairs)]
    ppermute x4, starting transfers between devices: 7.21 us -> 5.94 us  [swapped(): return lax.ppermute(value, 'c', [(0, 1), (1, 0)])]
  transfers between devices with their start and end apart: 8 -> 8, of which waited for: 3 -> 3; matrix products, arithmetic and copies ran while one was open for 0% -> 1% of each run, Pallas kernels for 5% -> 5%
where the time goes in v6:
time: 121 us; the launch traced here: 120 us
  blocking collectives  68.4 us (57%)
  starting transfers between devices  18.3 us (15%)
  waiting for transfers between devices  13.3 us (11%)
  Pallas kernels  10.6 us (9%)
  local copies, waits for them, and re-layouts  7 us (6%)
  between operations  1.61 us (1%)
  other arithmetic  1.34 us (1%)
    all_to_all x6, blocking collectives, exchanged(): return lax.all_to_all(value, axes, split_axis=0, concat_axis=0, tiled=True)  68.4 us
    ppermute x4, waiting for transfers between devices, shifted(): return lax.ppermute(value, RIGHT, pairs)  12.6 us
    ppermute x4, starting transfers between devices, shifted(): return lax.ppermute(value, RIGHT, pairs)  12.3 us
    pallas_call x7, Pallas kernels, call(): pl.pallas_call(kernel, out_shape=shapes, in_specs=[scalar] * scalars + [v...  10.6 us
    ppermute x4, starting transfers between devices, swapped(): return lax.ppermute(value, 'c', [(0, 1), (1, 0)])  5.94 us
    unnamed x20, local copies, waits for them, and re-layouts  5.66 us
  transfers between devices with their start and end apart: 8, of which 3 were waited for; matrix products, arithmetic and copies ran while one was open for 1% of the time, Pallas kernels for 5%

profile of v6, /device:TPU:1, one launch (start us, length us, event | category | flops | bytes accessed | tf_op | source)
XLA Modules:
  0.0 120.5 jit_solution(4524249759188948603)
XLA Ops:
  0.6 5.8 %collective-permute-start = (f32[400,384]{1,0:T(8,128)}, f32[400,384]{1,0:T(8,128)S(1)}, u32[]{:S(2)}, u32[]{:S(2)}) collective-permute-start(f32[400,384]{1,0:T(8,128)} %bitcast.62), channel_id=1, source_target_pairs={{0,5},{1,6},{2,7},{3,8},{4,9},{5,10},{6,11},{7,12},{8,13},{9,14},{... | collective-permute-start | bytes 1843208 | tf_op jit(solution)/shard_map/ppermute | solution.py:219
  8.6 0.7 slice-done
  9.3 0.7 copy-done.8
  10.8 1.1 copy-done
  11.9 1.0 copy-done.2
  12.9 1.0 copy-done.3
  13.9 1.3 %shard_map.138 = (f32[400,512]{1,0:T(8,128)S(1)}, f32[400,512]{1,0:T(8,128)S(1)}, bf16[400,512]{1,0:T(8,128)(2,1)S(1)}, bf16[400,512]{1,0:T(8,128)(2,1)S(1)}, f3...) custom-call(s32[1]{0:T(128)} %bitcast.place_ref, ...), custom_call_target="tpu_custom_call" | custom-call | flops 805306368 | bytes 4331524 | tf_op jit(solution)/shard_map/pallas_call | solution.py:205
  15.4 12.6 %collective-permute-done.1.dst_state_ref = f32[1,384]{1,0:T(1,128)S(1)} collective-permute-done((f32[1,384]{1,0:T(1,128)S(1)}, f32[1,384]{1,0:T(1,128)S(1)}, u32[]{:S(2)}, u32[]{:S(2)}) %collective-permute-start.1) | collective-permute-done | bytes 1568 | tf_op jit(solution)/shard_map/ppermute | solution.py:219
  28.0 2.1 %shard_map.139 = (f32[400,128]{1,0:T(8,128)S(1)}, f32[400,128]{1,0:T(8,128)S(1)}, f32[400,512]{1,0:T(8,128)S(1)}, bf16[384,512]{1,0:T(8,128)(2,1)S(1)}, bf16[384,512]{1,0:T(8,128)(2,1)S(1)}) custom-call(bf16[400,512]{1,0:T(8,128)(2,1)S(1)} %get-tuple-element.62.high_ref, bf16[400,512]{1,0:T(8,128)(2,1)S(1)} %get-tuple-element.63.low_ref, ...), custom_call_target="tpu_custom_call" | custom-call | flops 1610612736 | bytes 5106688 | tf_op jit(solution)/shard_map/pallas_call | solution.py:205
  30.3 1.5 %shard_map.140 = (f32[400,384]{1,0:T(8,128)S(1)}, f32[1,384]{1,0:T(1,128)S(1)}, f32[400,384]{1,0:T(8,128)S(1)}, f32[1,384]{1,0:T(1,128)S(1)}) custom-call(f32[400,512]{1,0:T(8,128)S(1)} %get-tuple-element.71.way_ref, bf16[400,512]{1,0:T(8,128)(2,1)S(1)} %get-tuple-element.62.high_ref, bf16[400,512]{1,0:T(8,128)(2,1)S(1)} %get-tuple-element.63.low_ref, ...), custom_call_target="tpu_custom_call" | custom-call | flops 1006632960 | bytes 4904960 | tf_op jit(solution)/shard_map/pallas_call | solution.py:205
  31.8 11.9 %all_to_all.30 = f32[16,1,3200]{2,1,0:T(1,128)S(1)} all-to-all(f32[16,1,3200]{2,1,0:T(1,128)S(1)} %bitcast.46), channel_id=1, replica_groups=mesh['x'=4,'zh'=2,'y'=4,'zl'=4,'c'=2] {'y','x'}, dimensions={0} | all-to-all | bytes 409600 | tf_op jit(solution)/shard_map/all_to_all | solution.py:227
  43.9 14.5 %all_to_all.31 = f32[8,1,3200]{2,1,0:T(1,128)S(1)} all-to-all(f32[8,1,3200]{2,1,0:T(1,128)S(1)} %broadcast_in_dim.23), channel_id=1, replica_groups=mesh['x'=4,'zh'=2,'y'=4,'zl'=4,'c'=2] {'zl','zh'}, dimensions={0} | all-to-all | bytes 204800 | tf_op jit(solution)/shard_map/all_to_all | solution.py:227
  58.7 10.2 %all_to_all.32 = f32[16,1,3200]{2,1,0:T(1,128)S(1)} all-to-all(f32[16,1,3200]{2,1,0:T(1,128)S(1)} %broadcast_in_dim.24), channel_id=1, replica_groups=mesh['x'=4,'zh'=2,'y'=4,'zl'=4,'c'=2] {'y','x'}, dimensions={0} | all-to-all | bytes 409600 | tf_op jit(solution)/shard_map/all_to_all | solution.py:227
  68.8 4.7 %collective-permute-start.3 = (f32[400,128]{1,0:T(8,128)S(1)}, f32[400,128]{1,0:T(8,128)S(1)}, u32[]{:S(2)}, u32[]{:S(2)}) collective-permute-start(f32[400,128]{1,0:T(8,128)S(1)} %bitcast.37), channel_id=1, source_target_pairs={{0,1},{1,0},{2,3},{3,2},{4,5},{5,4},{6,7},{7,6},{8,9},{9,8},{10,11... | collective-permute-start | bytes 614408 | tf_op jit(solution)/shard_map/ppermute | solution.py:223
  74.6 2.5 %shard_map.142 = (f32[400,128]{1,0:T(8,128)S(1)}, f32[400,128]{1,0:T(8,128)S(1)}, f32[400,512]{1,0:T(8,128)S(1)}, bf16[384,512]{1,0:T(8,128)(2,1)S(1)}, bf16[384...) custom-call(f32[400,128]{1,0:T(8,128)S(1)} %bitcast.38, ...), custom_call_target="tpu_custom_call" | custom-call | flops 2013265920 | bytes 4697088 | tf_op jit(solution)/shard_map/pallas_call | solution.py:205
  77.6 1.0 shard_map.143
  78.7 1.8 %collective-permute-start.5 = (f32[200,384]{1,0:T(8,128)S(1)}, f32[200,384]{1,0:T(8,128)S(1)}, u32[]{:S(2)}, u32[]{:S(2)}) collective-permute-start(f32[200,384]{1,0:T(8,128)S(1)} %get-tuple-element.98), channel_id=1, source_target_pairs={{0,27},{1,28},{2,29},{3,30},{4,31},{5,0},{6,1},{7,2},{8,3},{9,4},{... | collective-permute-start | bytes 921608 | tf_op jit(solution)/shard_map/ppermute | solution.py:219
  80.5 11.1 %all_to_all.33 = f32[16,1,3200]{2,1,0:T(1,128)S(1)} all-to-all(f32[16,1,3200]{2,1,0:T(1,128)S(1)} %bitcast.45), channel_id=1, replica_groups=mesh['x'=4,'zh'=2,'y'=4,'zl'=4,'c'=2] {'y','x'}, dimensions={0} | all-to-all | bytes 409600 | tf_op jit(solution)/shard_map/all_to_all | solution.py:227
  91.8 10.3 %all_to_all.34 = f32[8,1,3200]{2,1,0:T(1,128)S(1)} all-to-all(f32[8,1,3200]{2,1,0:T(1,128)S(1)} %broadcast_in_dim.25), channel_id=1, replica_groups=mesh['x'=4,'zh'=2,'y'=4,'zl'=4,'c'=2] {'zl','zh'}, dimensions={0} | all-to-all | bytes 204800 | tf_op jit(solution)/shard_map/all_to_all | solution.py:227
  102.1 4.5 %collective-permute-start.6 = (f32[208,384]{1,0:T(8,128)S(1)}, f32[208,384]{1,0:T(8,128)S(1)}, u32[]{:S(2)}, u32[]{:S(2)}) collective-permute-start(f32[208,384]{1,0:T(8,128)S(1)} %get-tuple-element.106), channel_id=1, source_target_pairs={{0,27},{1,28},{2,29},{3,30},{4,31},{5,0},{6,1},{7,2},{8,3},{9,4},{... | collective-permute-start | bytes 958472 | tf_op jit(solution)/shard_map/ppermute | solution.py:219
  106.8 10.4 %all_to_all.35 = f32[16,1,3200]{2,1,0:T(1,128)S(1)} all-to-all(f32[16,1,3200]{2,1,0:T(1,128)S(1)} %broadcast_in_dim.26), channel_id=1, replica_groups=mesh['x'=4,'zh'=2,'y'=4,'zl'=4,'c'=2] {'y','x'}, dimensions={0} | all-to-all | bytes 409600 | tf_op jit(solution)/shard_map/all_to_all | solution.py:227
  117.2 0.7 collective-permute-start.7
  118.0 1.7 %shard_map.144 = (f32[400,384]{1,0:T(8,128)}, f32[400,384]{1,0:T(8,128)}, f32[384]{0:T(512)}) custom-call(f32[400,512]{1,0:T(8,128)S(1)} %get-tuple-element.102.way_ref, f32[400,384]{1,0:T(8,128)S(1)} %get-tuple-element.86.src_ref, f32[1,384]{1,0:T(1,128)S(1)} %get-tuple-element.103.src_state_ref, s32[8,512]{1,0:T(8,128)S(1)} %stack.31.ids_ref, ...), custom_call_target="tpu_custom_call" | custom-call | flops 402653184 | bytes 3308544 | tf_op jit(solution)/shard_map/pallas_call | solution.py:205
  119.7 0.8 maximum_bitcast_fusion
  (63 shorter events, 5.1 us)
Async XLA Ops:
  0.6 27.4 %collective-permute-start = (f32[400,384]{1,0:T(8,128)}, f32[400,384]{1,0:T(8,128)S(1)}, u32[]{:S(2)}, u32[]{:S(2)}) collective-permute-start(f32[400,384]{1,0:T(8,128)} %bitcast.62), channel_id=1, source_target_pairs={{0,5},{1,6},{2,7},{3,8},{4,9},{5,10},{6,11},{7,12},{8,13},{9,14},{... | collective-permute-start | bytes 1843208 | tf_op jit(solution)/shard_map/ppermute | solution.py:219
  6.4 0.7 copy-start.4
  7.1 0.7 copy-start.6
  7.8 0.7 copy-start.7
  8.6 0.7 slice-start
  9.3 0.7 copy-start.8
  10.0 0.7 copy-start.5
  10.8 1.1 copy-start
  11.9 1.0 copy-start.2
  12.9 1.0 copy-start.3
  15.2 12.8 %collective-permute-start.1 = (f32[1,384]{1,0:T(1,128)S(1)}, f32[1,384]{1,0:T(1,128)S(1)}, u32[]{:S(2)}, u32[]{:S(2)}) collective-permute-start(f32[1,384]{1,0:T(1,128)S(1)} %get-tuple-element.66), channel_id=1, source_target_pairs={{0,5},{1,6},{2,7},{3,8},{4,9},{5,10},{6,11},{7,12},{8,13},{9,14},{... | collective-permute-start | bytes 4616 | tf_op jit(solution)/shard_map/ppermute | solution.py:219
  28.0 2.3 %copy-start.9 = (f32[384]{0:T(512)S(1)}, f32[384]{0:T(512)}, u32[]{:S(2)}) copy-start(f32[384]{0:T(512)} %param.12) | copy-start | bytes 4612
  28.0 2.3 %copy-start.1 = (f32[384,400]{0,1:T(8,128)S(1)}, f32[384,400]{0,1:T(8,128)}, u32[]{:S(2)}) copy-start(f32[384,400]{0,1:T(8,128)} %param.11) | copy-start | bytes 1843204
  30.2 1.6 %collective-permute-start.2 = (f32[400,128]{1,0:T(8,128)S(1)}, f32[400,128]{1,0:T(8,128)S(1)}, u32[]{:S(2)}, u32[]{:S(2)}) collective-permute-start(f32[400,128]{1,0:T(8,128)S(1)} %get-tuple-element.70), channel_id=1, source_target_pairs={{0,1},{1,0},{2,3},{3,2},{4,5},{5,4},{6,7},{7,6},{8,9},{9,8},{10,11... | collective-permute-start | bytes 614408 | tf_op jit(solution)/shard_map/ppermute | solution.py:223
  68.8 5.7 %collective-permute-start.3 = (f32[400,128]{1,0:T(8,128)S(1)}, f32[400,128]{1,0:T(8,128)S(1)}, u32[]{:S(2)}, u32[]{:S(2)}) collective-permute-start(f32[400,128]{1,0:T(8,128)S(1)} %bitcast.37), channel_id=1, source_target_pairs={{0,1},{1,0},{2,3},{3,2},{4,5},{5,4},{6,7},{7,6},{8,9},{9,8},{10,11... | collective-permute-start | bytes 614408 | tf_op jit(solution)/shard_map/ppermute | solution.py:223
  77.1 1.5 %collective-permute-start.4 = (f32[400,128]{1,0:T(8,128)S(1)}, f32[400,128]{1,0:T(8,128)S(1)}, u32[]{:S(2)}, u32[]{:S(2)}) collective-permute-start(f32[400,128]{1,0:T(8,128)S(1)} %get-tuple-element.89), channel_id=1, source_target_pairs={{0,1},{1,0},{2,3},{3,2},{4,5},{5,4},{6,7},{7,6},{8,9},{9,8},{10,11... | collective-permute-start | bytes 614408 | tf_op jit(solution)/shard_map/ppermute | solution.py:223
  78.7 13.0 %collective-permute-start.5 = (f32[200,384]{1,0:T(8,128)S(1)}, f32[200,384]{1,0:T(8,128)S(1)}, u32[]{:S(2)}, u32[]{:S(2)}) collective-permute-start(f32[200,384]{1,0:T(8,128)S(1)} %get-tuple-element.98), channel_id=1, source_target_pairs={{0,27},{1,28},{2,29},{3,30},{4,31},{5,0},{6,1},{7,2},{8,3},{9,4},{... | collective-permute-start | bytes 921608 | tf_op jit(solution)/shard_map/ppermute | solution.py:219
  102.1 15.1 %collective-permute-start.6 = (f32[208,384]{1,0:T(8,128)S(1)}, f32[208,384]{1,0:T(8,128)S(1)}, u32[]{:S(2)}, u32[]{:S(2)}) collective-permute-start(f32[208,384]{1,0:T(8,128)S(1)} %get-tuple-element.106), channel_id=1, source_target_pairs={{0,27},{1,28},{2,29},{3,30},{4,31},{5,0},{6,1},{7,2},{8,3},{9,4},{... | collective-permute-start | bytes 958472 | tf_op jit(solution)/shard_map/ppermute | solution.py:219
  117.2 2.4 %collective-permute-start.7 = (f32[400,128]{1,0:T(8,128)S(1)}, f32[400,128]{1,0:T(8,128)S(1)}, u32[]{:S(2)}, u32[]{:S(2)}) collective-permute-start(f32[400,128]{1,0:T(8,128)S(1)} %bitcast.43), channel_id=1, source_target_pairs={{0,1},{1,0},{2,3},{3,2},{4,5},{5,4},{6,7},{7,6},{8,9},{9,8},{10,11... | collective-permute-start | bytes 614408 | tf_op jit(solution)/shard_map/ppermute | solution.py:223

commit v7 on v6

--- a/solution.py
+++ b/solution.py
@@ -97,20 +97,19 @@
 
 
 def relation_side(
-    batch, queries, sources, relations, dst_ref, ids_ref, counts_ref, mine_ref, other_ref, way_ref, weight_refs
+    batch, queries, sources, relations, dst_ref, ids_ref, counts_ref, mine_ref, other_ref, way_ref
 ):
     rows = parts(dst_ref[...])
     dst_ids = ids_ref[2 + batch : 3 + batch, :]
     weights = edge_weights(dot3(rows, queries, TN), dst_ids, counts_ref[:, batch : batch + 1])
-    put(weight_refs, weights)
     grads = dot3(rows, weights, NN)
     rel_grad = scatter(against(grads, sources), pick(REL, ids_ref[5 + batch : 6 + batch, :]))
     put((mine_ref, other_ref), (rel_grad[:, :HALF], rel_grad[:, HALF:]))
     way_ref[...] = against(grads, relations)
-
-
-def target_update(query_refs, weight_refs, dst_ref, dst_state_ref):
-    queries, weights = [tuple(ref[...] for ref in refs) for refs in (query_refs, weight_refs)]
+    return weights
+
+
+def target_update(queries, weights, dst_ref, dst_state_ref):
     return entity_update(dst_ref[...], dst_state_ref[...], dot3(queries, weights, NT))
 
 
@@ -139,10 +138,11 @@
 def first_relation_kernel(
     high_ref, low_ref, sources_ref, relations_ref, dst_ref, ids_ref, counts_ref, mine_ref, other_ref, way_ref, *weight_refs
 ):
-    relation_side(
+    weights = relation_side(
         0, (high_ref[...], low_ref[...]), sources_ref[...], relations_ref[...], dst_ref, ids_ref, counts_ref,
-        mine_ref, other_ref, way_ref, weight_refs,
-    )
+        mine_ref, other_ref, way_ref,
+    )
+    put(weight_refs, weights)
 
 
 def first_entity_kernel(
@@ -150,33 +150,25 @@
     src_out, src_state_out, dst_out, dst_state_out,
 ):
     src_out[...], src_state_out[...] = source_update(0, way_ref, src_ref, src_state_ref, ids_ref)
-    dst_out[...], dst_state_out[...] = target_update(
-        (high_ref, low_ref), (weight_high_ref, weight_low_ref), dst_ref, dst_state_ref
-    )
+    queries, weights = ((high_ref[...], low_ref[...]), (weight_high_ref[...], weight_low_ref[...]))
+    dst_out[...], dst_state_out[...] = target_update(queries, weights, dst_ref, dst_state_ref)
 
 
 def gather_kernel(src_ref, ids_ref, sources_ref):
     sources_ref[...] = gather(src_ref[...], pick(SLAB, ids_ref[1:2, :]))
 
 
-def second_relation_kernel(
-    rel_mine_ref, rel_other_ref, sources_ref, dst_ref, ids_ref, counts_ref,
-    mine_ref, other_ref, way_ref, weight_high_ref, weight_low_ref, high_ref, low_ref,
+def second_kernel(
+    rel_mine_ref, rel_other_ref, sources_ref, dst_ref, dst_state_ref, ids_ref, counts_ref,
+    mine_ref, other_ref, way_ref, upper_out, lower_out,
 ):
     relation = jnp.concatenate([rel_mine_ref[...], rel_other_ref[...]], axis=1)
     sources, relations = (sources_ref[...], gather(relation, pick(REL, ids_ref[6:7, :])))
     queries = query(sources, relations)
-    put((high_ref, low_ref), queries)
-    relation_side(
-        1, queries, sources, relations, dst_ref, ids_ref, counts_ref,
-        mine_ref, other_ref, way_ref, (weight_high_ref, weight_low_ref),
-    )
-
-
-def second_target_kernel(
-    high_ref, low_ref, weight_high_ref, weight_low_ref, dst_ref, dst_state_ref, upper_out, lower_out
-):
-    dst_table, dst_state = target_update((high_ref, low_ref), (weight_high_ref, weight_low_ref), dst_ref, dst_state_ref)
+    weights = relation_side(
+        1, queries, sources, relations, dst_ref, ids_ref, counts_ref, mine_ref, other_ref, way_ref
+    )
+    dst_table, dst_state = target_update(queries, weights, dst_ref, dst_state_ref)
     upper_out[...] = dst_table[:CUT]
     lower_out[: W - CUT, :] = dst_table[CUT:]
     lower_out[W - CUT :, :] = jnp.broadcast_to(dst_state, (8, SLAB))
@@ -310,22 +302,12 @@
     near, own, own_sums, *_ = relation_update(half, own, own_sums)
     near, src_table, src_sums, dst_table, dst_sums = lax.optimization_barrier((near, *tables))
     (sources,) = call(gather_kernel, [(W, EP)], src_table, ids, passes=2)
-    mine, other, way, weight_high, weight_low, high, low = call(
-        second_relation_kernel,
-        [(W, HALF), (W, HALF), (W, EP), *weight_shapes, *query_shapes],
-        near, swapped(near), sources, dst_table, ids, counts, passes=10,
+    mine, other, way, upper, lower = call(
+        second_kernel,
+        [(W, HALF), (W, HALF), (W, EP), (CUT, SLAB), (W + 8 - CUT, SLAB)],
+        near, swapped(near), sources, dst_table, dst_sums, ids, counts, passes=13,
     )
     half = chip_half(mine, other)
-    half, upper, lower = lax.optimization_barrier(
-        (
-            half,
-            *call(
-                second_target_kernel,
-                [(CUT, SLAB), (W + 8 - CUT, SLAB)],
-                high, low, weight_high, weight_low, dst_table, dst_sums, passes=3,
-            ),
-        )
-    )
     near, own, own_sums, upper, lower, way = relation_update(half, own, own_sums, upper, lower, way)
     near, lower = lax.optimization_barrier((near, lower))
     vector = pl.BlockSpec(memory_space=pltpu.VMEM)

time: 121 us -> 121 us (level)
    pallas_call x7 -> x6, Pallas kernels: 10.6 us -> 10.4 us  [call(): pl.pallas_call(kernel, out_shape=shapes, in_specs=[scalar] * scalars + [v...]
  transfers between devices with their start and end apart: 8 -> 8, of which waited for: 3 -> 2; matrix products, arithmetic and copies ran while one was open for 1% -> 1% of each run, Pallas kernels for 5% -> 4%
where the time goes in v7:
time: 121 us; the launch traced here: 120 us
  blocking collectives  68.8 us (57%)
  starting transfers between devices  17.7 us (15%)
  waiting for transfers between devices  13.2 us (11%)
  Pallas kernels  10.4 us (9%)
  local copies, waits for them, and re-layouts  7.05 us (6%)
  between operations  1.58 us (1%)
  other arithmetic  1.34 us (1%)
    all_to_all x6, blocking collectives, exchanged(): return lax.all_to_all(value, axes, split_axis=0, concat_axis=0, tiled=True)  68.8 us
    ppermute x4, waiting for transfers between devices, shifted(): return lax.ppermute(value, RIGHT, pairs)  12.6 us
    ppermute x4, starting transfers between devices, shifted(): return lax.ppermute(value, RIGHT, pairs)  11.6 us
    pallas_call x6, Pallas kernels, call(): pl.pallas_call(kernel, out_shape=shapes, in_specs=[scalar] * scalars + [v...  10.4 us
    ppermute x4, starting transfers between devices, swapped(): return lax.ppermute(value, 'c', [(0, 1), (1, 0)])  6.13 us
    unnamed x20, local copies, waits for them, and re-layouts  5.71 us
  transfers between devices with their start and end apart: 8, of which 2 were waited for; matrix products, arithmetic and copies ran while one was open for 1% of the time, Pallas kernels for 4%

profile of v7, /device:TPU:1, one launch (start us, length us, event | category | flops | bytes accessed | tf_op | source)
XLA Modules:
  0.0 120.1 jit_solution(11524061611576551360)
XLA Ops:
  0.6 5.8 %collective-permute-start = (f32[400,384]{1,0:T(8,128)}, f32[400,384]{1,0:T(8,128)S(1)}, u32[]{:S(2)}, u32[]{:S(2)}) collective-permute-start(f32[400,384]{1,0:T(8,128)} %bitcast.62), channel_id=1, source_target_pairs={{0,5},{1,6},{2,7},{3,8},{4,9},{5,10},{6,11},{7,12},{8,13},{9,14},{... | collective-permute-start | bytes 1843208 | tf_op jit(solution)/shard_map/ppermute | solution.py:211
  6.4 0.7 copy-done.4
  8.6 0.7 slice-done
  10.1 0.7 copy-done.8
  10.8 1.1 copy-done
  11.9 1.0 copy-done.2
  12.9 1.0 copy-done.3
  13.9 1.2 %shard_map.138 = (f32[400,512]{1,0:T(8,128)S(1)}, f32[400,512]{1,0:T(8,128)S(1)}, bf16[400,512]{1,0:T(8,128)(2,1)S(1)}, bf16[400,512]{1,0:T(8,128)(2,1)S(1)}, f3...) custom-call(s32[1]{0:T(128)} %bitcast.place_ref, ...), custom_call_target="tpu_custom_call" | custom-call | flops 805306368 | bytes 4331524 | tf_op jit(solution)/shard_map/pallas_call | solution.py:197
  15.4 12.6 %collective-permute-done.1.dst_state_ref = f32[1,384]{1,0:T(1,128)S(1)} collective-permute-done((f32[1,384]{1,0:T(1,128)S(1)}, f32[1,384]{1,0:T(1,128)S(1)}, u32[]{:S(2)}, u32[]{:S(2)}) %collective-permute-start.1) | collective-permute-done | bytes 1568 | tf_op jit(solution)/shard_map/ppermute | solution.py:211
  28.0 2.2 %shard_map.139 = (f32[400,128]{1,0:T(8,128)S(1)}, f32[400,128]{1,0:T(8,128)S(1)}, f32[400,512]{1,0:T(8,128)S(1)}, bf16[384,512]{1,0:T(8,128)(2,1)S(1)}, bf16[384,512]{1,0:T(8,128)(2,1)S(1)}) custom-call(bf16[400,512]{1,0:T(8,128)(2,1)S(1)} %get-tuple-element.55.high_ref, bf16[400,512]{1,0:T(8,128)(2,1)S(1)} %get-tuple-element.56.low_ref, ...), custom_call_target="tpu_custom_call" | custom-call | flops 1610612736 | bytes 5106688 | tf_op jit(solution)/shard_map/pallas_call | solution.py:197
  30.3 1.5 %shard_map.140 = (f32[400,384]{1,0:T(8,128)S(1)}, f32[1,384]{1,0:T(1,128)S(1)}, f32[400,384]{1,0:T(8,128)S(1)}, f32[1,384]{1,0:T(1,128)S(1)}) custom-call(f32[400,512]{1,0:T(8,128)S(1)} %get-tuple-element.64.way_ref, bf16[400,512]{1,0:T(8,128)(2,1)S(1)} %get-tuple-element.55.high_ref, bf16[400,512]{1,0:T(8,128)(2,1)S(1)} %get-tuple-element.56.low_ref, ...), custom_call_target="tpu_custom_call" | custom-call | flops 1006632960 | bytes 4904960 | tf_op jit(solution)/shard_map/pallas_call | solution.py:197
  31.9 11.9 %all_to_all.30 = f32[16,1,3200]{2,1,0:T(1,128)S(1)} all-to-all(f32[16,1,3200]{2,1,0:T(1,128)S(1)} %bitcast.45), channel_id=1, replica_groups=mesh['x'=4,'zh'=2,'y'=4,'zl'=4,'c'=2] {'y','x'}, dimensions={0} | all-to-all | bytes 409600 | tf_op jit(solution)/shard_map/all_to_all | solution.py:219
  43.9 14.5 %all_to_all.31 = f32[8,1,3200]{2,1,0:T(1,128)S(1)} all-to-all(f32[8,1,3200]{2,1,0:T(1,128)S(1)} %broadcast_in_dim.23), channel_id=1, replica_groups=mesh['x'=4,'zh'=2,'y'=4,'zl'=4,'c'=2] {'zl','zh'}, dimensions={0} | all-to-all | bytes 204800 | tf_op jit(solution)/shard_map/all_to_all | solution.py:219
  58.7 10.2 %all_to_all.32 = f32[16,1,3200]{2,1,0:T(1,128)S(1)} all-to-all(f32[16,1,3200]{2,1,0:T(1,128)S(1)} %broadcast_in_dim.24), channel_id=1, replica_groups=mesh['x'=4,'zh'=2,'y'=4,'zl'=4,'c'=2] {'y','x'}, dimensions={0} | all-to-all | bytes 409600 | tf_op jit(solution)/shard_map/all_to_all | solution.py:219
  68.9 4.7 %collective-permute-start.3 = (f32[400,128]{1,0:T(8,128)S(1)}, f32[400,128]{1,0:T(8,128)S(1)}, u32[]{:S(2)}, u32[]{:S(2)}) collective-permute-start(f32[400,128]{1,0:T(8,128)S(1)} %bitcast.37), channel_id=1, source_target_pairs={{0,1},{1,0},{2,3},{3,2},{4,5},{5,4},{6,7},{7,6},{8,9},{9,8},{10,11... | collective-permute-start | bytes 614408 | tf_op jit(solution)/shard_map/ppermute | solution.py:215
  74.6 3.3 %shard_map.142 = (f32[400,128]{1,0:T(8,128)S(1)}, f32[400,128]{1,0:T(8,128)S(1)}, f32[400,512]{1,0:T(8,128)S(1)}, f32[200,384]{1,0:T(8,128)S(1)}, f32[208,384]{1,0:T(8,128)S(1)}) custom-call(f32[400,128]{1,0:T(8,128)S(1)} %bitcast.38, f32[400,128]{1,0:T(8,128)S(1)} %collective-permute-done.3.rel_other_ref, f32[400,512]{1,0:T(8,128)S(1)} %shard_map.141.sources_ref, ...), custom_call_target="tpu_custom_call" | custom-call | flops 2617245696 | bytes 3719680 | tf_op jit(solution)/shard_map/pallas_call | solution.py:197
  78.4 1.4 %collective-permute-start.5 = (f32[200,384]{1,0:T(8,128)S(1)}, f32[200,384]{1,0:T(8,128)S(1)}, u32[]{:S(2)}, u32[]{:S(2)}) collective-permute-start(f32[200,384]{1,0:T(8,128)S(1)} %get-tuple-element.84), channel_id=1, source_target_pairs={{0,27},{1,28},{2,29},{3,30},{4,31},{5,0},{6,1},{7,2},{8,3},{9,4},{... | collective-permute-start | bytes 921608 | tf_op jit(solution)/shard_map/ppermute | solution.py:211
  79.9 11.0 %all_to_all.33 = f32[16,1,3200]{2,1,0:T(1,128)S(1)} all-to-all(f32[16,1,3200]{2,1,0:T(1,128)S(1)} %bitcast.46), channel_id=1, replica_groups=mesh['x'=4,'zh'=2,'y'=4,'zl'=4,'c'=2] {'y','x'}, dimensions={0} | all-to-all | bytes 409600 | tf_op jit(solution)/shard_map/all_to_all | solution.py:219
  91.1 10.6 %all_to_all.34 = f32[8,1,3200]{2,1,0:T(1,128)S(1)} all-to-all(f32[8,1,3200]{2,1,0:T(1,128)S(1)} %broadcast_in_dim.25), channel_id=1, replica_groups=mesh['x'=4,'zh'=2,'y'=4,'zl'=4,'c'=2] {'zl','zh'}, dimensions={0} | all-to-all | bytes 204800 | tf_op jit(solution)/shard_map/all_to_all | solution.py:219
  101.8 4.2 %collective-permute-start.6 = (f32[208,384]{1,0:T(8,128)S(1)}, f32[208,384]{1,0:T(8,128)S(1)}, u32[]{:S(2)}, u32[]{:S(2)}) collective-permute-start(f32[208,384]{1,0:T(8,128)S(1)} %get-tuple-element.92), channel_id=1, source_target_pairs={{0,27},{1,28},{2,29},{3,30},{4,31},{5,0},{6,1},{7,2},{8,3},{9,4},{... | collective-permute-start | bytes 958472 | tf_op jit(solution)/shard_map/ppermute | solution.py:211
  106.0 10.6 %all_to_all.35 = f32[16,1,3200]{2,1,0:T(1,128)S(1)} all-to-all(f32[16,1,3200]{2,1,0:T(1,128)S(1)} %broadcast_in_dim.26), channel_id=1, replica_groups=mesh['x'=4,'zh'=2,'y'=4,'zl'=4,'c'=2] {'y','x'}, dimensions={0} | all-to-all | bytes 409600 | tf_op jit(solution)/shard_map/all_to_all | solution.py:219
  116.7 0.9 collective-permute-start.7
  117.6 1.7 %shard_map.143 = (f32[400,384]{1,0:T(8,128)}, f32[400,384]{1,0:T(8,128)}, f32[384]{0:T(512)}) custom-call(f32[400,512]{1,0:T(8,128)S(1)} %get-tuple-element.88.way_ref, f32[400,384]{1,0:T(8,128)S(1)} %get-tuple-element.79.src_ref, f32[1,384]{1,0:T(1,128)S(1)} %get-tuple-element.89.src_state_ref, s32[8,512]{1,0:T(8,128)S(1)} %stack.31.ids_ref, ...), custom_call_target="tpu_custom_call" | custom-call | flops 402653184 | bytes 3308544 | tf_op jit(solution)/shard_map/pallas_call | solution.py:197
  119.3 0.8 maximum_bitcast_fusion
  (62 shorter events, 4.3 us)
Async XLA Ops:
  0.6 27.4 %collective-permute-start = (f32[400,384]{1,0:T(8,128)}, f32[400,384]{1,0:T(8,128)S(1)}, u32[]{:S(2)}, u32[]{:S(2)}) collective-permute-start(f32[400,384]{1,0:T(8,128)} %bitcast.62), channel_id=1, source_target_pairs={{0,5},{1,6},{2,7},{3,8},{4,9},{5,10},{6,11},{7,12},{8,13},{9,14},{... | collective-permute-start | bytes 1843208 | tf_op jit(solution)/shard_map/ppermute | solution.py:211
  6.4 0.7 copy-start.4
  7.1 0.7 copy-start.6
  7.9 0.7 copy-start.7
  8.6 0.7 slice-start
  9.4 0.7 copy-start.5
  10.1 0.7 copy-start.8
  10.8 1.1 copy-start
  11.9 1.0 copy-start.2
  12.9 1.0 copy-start.3
  15.2 12.8 %collective-permute-start.1 = (f32[1,384]{1,0:T(1,128)S(1)}, f32[1,384]{1,0:T(1,128)S(1)}, u32[]{:S(2)}, u32[]{:S(2)}) collective-permute-start(f32[1,384]{1,0:T(1,128)S(1)} %get-tuple-element.59), channel_id=1, source_target_pairs={{0,5},{1,6},{2,7},{3,8},{4,9},{5,10},{6,11},{7,12},{8,13},{9,14},{... | collective-permute-start | bytes 4616 | tf_op jit(solution)/shard_map/ppermute | solution.py:211
  28.0 2.3 %copy-start.9 = (f32[384]{0:T(512)S(1)}, f32[384]{0:T(512)}, u32[]{:S(2)}) copy-start(f32[384]{0:T(512)} %param.12) | copy-start | bytes 4612
  28.0 2.3 %copy-start.1 = (f32[384,400]{0,1:T(8,128)S(1)}, f32[384,400]{0,1:T(8,128)}, u32[]{:S(2)}) copy-start(f32[384,400]{0,1:T(8,128)} %param.11) | copy-start | bytes 1843204
  30.2 1.6 %collective-permute-start.2 = (f32[400,128]{1,0:T(8,128)S(1)}, f32[400,128]{1,0:T(8,128)S(1)}, u32[]{:S(2)}, u32[]{:S(2)}) collective-permute-start(f32[400,128]{1,0:T(8,128)S(1)} %get-tuple-element.63), channel_id=1, source_target_pairs={{0,1},{1,0},{2,3},{3,2},{4,5},{5,4},{6,7},{7,6},{8,9},{9,8},{10,11... | collective-permute-start | bytes 614408 | tf_op jit(solution)/shard_map/ppermute | solution.py:215
  68.9 5.7 %collective-permute-start.3 = (f32[400,128]{1,0:T(8,128)S(1)}, f32[400,128]{1,0:T(8,128)S(1)}, u32[]{:S(2)}, u32[]{:S(2)}) collective-permute-start(f32[400,128]{1,0:T(8,128)S(1)} %bitcast.37), channel_id=1, source_target_pairs={{0,1},{1,0},{2,3},{3,2},{4,5},{5,4},{6,7},{7,6},{8,9},{9,8},{10,11... | collective-permute-start | bytes 614408 | tf_op jit(solution)/shard_map/ppermute | solution.py:215
  78.0 1.9 %collective-permute-start.4 = (f32[400,128]{1,0:T(8,128)S(1)}, f32[400,128]{1,0:T(8,128)S(1)}, u32[]{:S(2)}, u32[]{:S(2)}) collective-permute-start(f32[400,128]{1,0:T(8,128)S(1)} %get-tuple-element.83), channel_id=1, source_target_pairs={{0,1},{1,0},{2,3},{3,2},{4,5},{5,4},{6,7},{7,6},{8,9},{9,8},{10,11... | collective-permute-start | bytes 614408 | tf_op jit(solution)/shard_map/ppermute | solution.py:215
  78.4 12.6 %collective-permute-start.5 = (f32[200,384]{1,0:T(8,128)S(1)}, f32[200,384]{1,0:T(8,128)S(1)}, u32[]{:S(2)}, u32[]{:S(2)}) collective-permute-start(f32[200,384]{1,0:T(8,128)S(1)} %get-tuple-element.84), channel_id=1, source_target_pairs={{0,27},{1,28},{2,29},{3,30},{4,31},{5,0},{6,1},{7,2},{8,3},{9,4},{... | collective-permute-start | bytes 921608 | tf_op jit(solution)/shard_map/ppermute | solution.py:211
  101.8 14.9 %collective-permute-start.6 = (f32[208,384]{1,0:T(8,128)S(1)}, f32[208,384]{1,0:T(8,128)S(1)}, u32[]{:S(2)}, u32[]{:S(2)}) collective-permute-start(f32[208,384]{1,0:T(8,128)S(1)} %get-tuple-element.92), channel_id=1, source_target_pairs={{0,27},{1,28},{2,29},{3,30},{4,31},{5,0},{6,1},{7,2},{8,3},{9,4},{... | collective-permute-start | bytes 958472 | tf_op jit(solution)/shard_map/ppermute | solution.py:211
  116.7 2.6 %collective-permute-start.7 = (f32[400,128]{1,0:T(8,128)S(1)}, f32[400,128]{1,0:T(8,128)S(1)}, u32[]{:S(2)}, u32[]{:S(2)}) collective-permute-start(f32[400,128]{1,0:T(8,128)S(1)} %bitcast.43), channel_id=1, source_target_pairs={{0,1},{1,0},{2,3},{3,2},{4,5},{5,4},{6,7},{7,6},{8,9},{9,8},{10,11... | collective-permute-start | bytes 614408 | tf_op jit(solution)/shard_map/ppermute | solution.py:215

commit v8 on v7

--- a/solution.py
+++ b/solution.py
@@ -97,11 +97,10 @@
 
 
 def relation_side(
-    batch, queries, sources, relations, dst_ref, ids_ref, counts_ref, mine_ref, other_ref, way_ref
-):
-    rows = parts(dst_ref[...])
+    batch, queries, sources, relations, rows, logits, ids_ref, counts_ref, mine_ref, other_ref, way_ref
+):
     dst_ids = ids_ref[2 + batch : 3 + batch, :]
-    weights = edge_weights(dot3(rows, queries, TN), dst_ids, counts_ref[:, batch : batch + 1])
+    weights = edge_weights(logits, dst_ids, counts_ref[:, batch : batch + 1])
     grads = dot3(rows, weights, NN)
     rel_grad = scatter(against(grads, sources), pick(REL, ids_ref[5 + batch : 6 + batch, :]))
     put((mine_ref, other_ref), (rel_grad[:, :HALF], rel_grad[:, HALF:]))
@@ -138,8 +137,9 @@
 def first_relation_kernel(
     high_ref, low_ref, sources_ref, relations_ref, dst_ref, ids_ref, counts_ref, mine_ref, other_ref, way_ref, *weight_refs
 ):
+    queries, rows = ((high_ref[...], low_ref[...]), parts(dst_ref[...]))
     weights = relation_side(
-        0, (high_ref[...], low_ref[...]), sources_ref[...], relations_ref[...], dst_ref, ids_ref, counts_ref,
+        0, queries, sources_ref[...], relations_ref[...], rows, dot3(rows, queries, TN), ids_ref, counts_ref,
         mine_ref, other_ref, way_ref,
     )
     put(weight_refs, weights)
@@ -154,19 +154,23 @@
     dst_out[...], dst_state_out[...] = target_update(queries, weights, dst_ref, dst_state_ref)
 
 
-def gather_kernel(src_ref, ids_ref, sources_ref):
+def gather_kernel(src_ref, near_ref, dst_ref, ids_ref, sources_ref, near_rows_ref, *row_refs):
     sources_ref[...] = gather(src_ref[...], pick(SLAB, ids_ref[1:2, :]))
+    near_rows_ref[...] = gather(near_ref[...], pick(HALF, ids_ref[6:7, :]))
+    rows = parts(dst_ref[...])
+    put(row_refs, (*rows, *[jnp.transpose(part) for part in rows]))
 
 
 def second_kernel(
-    rel_mine_ref, rel_other_ref, sources_ref, dst_ref, dst_state_ref, ids_ref, counts_ref,
-    mine_ref, other_ref, way_ref, upper_out, lower_out,
-):
-    relation = jnp.concatenate([rel_mine_ref[...], rel_other_ref[...]], axis=1)
-    sources, relations = (sources_ref[...], gather(relation, pick(REL, ids_ref[6:7, :])))
-    queries = query(sources, relations)
+    far_ref, near_rows_ref, sources_ref, high_ref, low_ref, high_across_ref, low_across_ref, dst_ref, dst_state_ref,
+    ids_ref, counts_ref, mine_ref, other_ref, way_ref, upper_out, lower_out,
+):
+    sources = sources_ref[...]
+    relations = near_rows_ref[...] + gather(far_ref[...], pick(HALF, ids_ref[6:7, :] - HALF))
+    queries, rows = (query(sources, relations), (high_ref[...], low_ref[...]))
+    logits = dot3((high_across_ref[...], low_across_ref[...]), queries, NN)
     weights = relation_side(
-        1, queries, sources, relations, dst_ref, ids_ref, counts_ref, mine_ref, other_ref, way_ref
+        1, queries, sources, relations, rows, logits, ids_ref, counts_ref, mine_ref, other_ref, way_ref
     )
     dst_table, dst_state = target_update(queries, weights, dst_ref, dst_state_ref)
     upper_out[...] = dst_table[:CUT]
@@ -301,11 +305,15 @@
     )
     near, own, own_sums, *_ = relation_update(half, own, own_sums)
     near, src_table, src_sums, dst_table, dst_sums = lax.optimization_barrier((near, *tables))
-    (sources,) = call(gather_kernel, [(W, EP)], src_table, ids, passes=2)
+    row_shapes = [jax.ShapeDtypeStruct((W, SLAB), jnp.bfloat16)] * 2 + [jax.ShapeDtypeStruct((SLAB, W), jnp.bfloat16)] * 2
+    sources, *ready = call(
+        gather_kernel, [(W, EP), (W, EP), *row_shapes], src_table, near, dst_table, ids, passes=3
+    )
+    near_rows, *rows = ready
     mine, other, way, upper, lower = call(
         second_kernel,
         [(W, HALF), (W, HALF), (W, EP), (CUT, SLAB), (W + 8 - CUT, SLAB)],
-        near, swapped(near), sources, dst_table, dst_sums, ids, counts, passes=13,
+        swapped(near), near_rows, sources, *rows, dst_table, dst_sums, ids, counts, passes=13,
     )
     half = chip_half(mine, other)
     near, own, own_sums, upper, lower, way = relation_update(half, own, own_sums, upper, lower, way)

time: 121 us -> 121 us (level)
  no operation moved by 1% of the time
where the time goes in v8:
time: 121 us; the launch traced here: 120 us
  blocking collectives  68.8 us (57%)
  starting transfers between devices  17.7 us (15%)
  waiting for transfers between devices  13.1 us (11%)
  Pallas kernels  10.5 us (9%)
  local copies, waits for them, and re-layouts  7 us (6%)
  between operations  1.6 us (1%)
  other arithmetic  1.34 us (1%)
    all_to_all x6, blocking collectives, exchanged(): return lax.all_to_all(value, axes, split_axis=0, concat_axis=0, tiled=True)  68.8 us
    ppermute x4, waiting for transfers between devices, shifted(): return lax.ppermute(value, RIGHT, pairs)  12.7 us
    ppermute x4, starting transfers between devices, shifted(): return lax.ppermute(value, RIGHT, pairs)  11.6 us
    pallas_call x6, Pallas kernels, call(): pl.pallas_call(kernel, out_shape=shapes, in_specs=[scalar] * scalars + [v...  10.5 us
    ppermute x4, starting transfers between devices, swapped(): return lax.ppermute(value, 'c', [(0, 1), (1, 0)])  6.1 us
    unnamed x20, local copies, waits for them, and re-layouts  5.66 us
  transfers between devices with their start and end apart: 8, of which 2 were waited for; matrix products, arithmetic and copies ran while one was open for 1% of the time, Pallas kernels for 4%

profile of v8, /device:TPU:1, one launch (start us, length us, event | category | flops | bytes accessed | tf_op | source)
XLA Modules:
  0.0 120.0 jit_solution(10172373789245882540)
XLA Ops:
  0.6 5.8 %collective-permute-start = (f32[400,384]{1,0:T(8,128)}, f32[400,384]{1,0:T(8,128)S(1)}, u32[]{:S(2)}, u32[]{:S(2)}) collective-permute-start(f32[400,384]{1,0:T(8,128)} %bitcast.62), channel_id=1, source_target_pairs={{0,5},{1,6},{2,7},{3,8},{4,9},{5,10},{6,11},{7,12},{8,13},{9,14},{... | collective-permute-start | bytes 1843208 | tf_op jit(solution)/shard_map/ppermute | solution.py:215
  8.6 0.7 slice-done
  9.3 0.7 copy-done.8
  10.8 1.1 copy-done
  11.9 1.0 copy-done.2
  12.9 1.0 copy-done.3
  13.9 1.2 %shard_map.138 = (f32[400,512]{1,0:T(8,128)S(1)}, f32[400,512]{1,0:T(8,128)S(1)}, bf16[400,512]{1,0:T(8,128)(2,1)S(1)}, bf16[400,512]{1,0:T(8,128)(2,1)S(1)}, f3...) custom-call(s32[1]{0:T(128)} %bitcast.place_ref, ...), custom_call_target="tpu_custom_call" | custom-call | flops 805306368 | bytes 4331524 | tf_op jit(solution)/shard_map/pallas_call | solution.py:201
  15.4 12.7 %collective-permute-done.1.dst_state_ref = f32[1,384]{1,0:T(1,128)S(1)} collective-permute-done((f32[1,384]{1,0:T(1,128)S(1)}, f32[1,384]{1,0:T(1,128)S(1)}, u32[]{:S(2)}, u32[]{:S(2)}) %collective-permute-start.1) | collective-permute-done | bytes 1568 | tf_op jit(solution)/shard_map/ppermute | solution.py:215
  28.0 2.2 %shard_map.139 = (f32[400,128]{1,0:T(8,128)S(1)}, f32[400,128]{1,0:T(8,128)S(1)}, f32[400,512]{1,0:T(8,128)S(1)}, bf16[384,512]{1,0:T(8,128)(2,1)S(1)}, bf16[384,512]{1,0:T(8,128)(2,1)S(1)}) custom-call(bf16[400,512]{1,0:T(8,128)(2,1)S(1)} %get-tuple-element.61.high_ref, bf16[400,512]{1,0:T(8,128)(2,1)S(1)} %get-tuple-element.62.low_ref, ...), custom_call_target="tpu_custom_call" | custom-call | flops 1610612736 | bytes 5106688 | tf_op jit(solution)/shard_map/pallas_call | solution.py:201
  30.3 1.5 %shard_map.140 = (f32[400,384]{1,0:T(8,128)S(1)}, f32[1,384]{1,0:T(1,128)S(1)}, f32[400,384]{1,0:T(8,128)S(1)}, f32[1,384]{1,0:T(1,128)S(1)}) custom-call(f32[400,512]{1,0:T(8,128)S(1)} %get-tuple-element.70.way_ref, bf16[400,512]{1,0:T(8,128)(2,1)S(1)} %get-tuple-element.61.high_ref, bf16[400,512]{1,0:T(8,128)(2,1)S(1)} %get-tuple-element.62.low_ref, ...), custom_call_target="tpu_custom_call" | custom-call | flops 1006632960 | bytes 4904960 | tf_op jit(solution)/shard_map/pallas_call | solution.py:201
  31.9 11.9 %all_to_all.30 = f32[16,1,3200]{2,1,0:T(1,128)S(1)} all-to-all(f32[16,1,3200]{2,1,0:T(1,128)S(1)} %bitcast.45), channel_id=1, replica_groups=mesh['x'=4,'zh'=2,'y'=4,'zl'=4,'c'=2] {'y','x'}, dimensions={0} | all-to-all | bytes 409600 | tf_op jit(solution)/shard_map/all_to_all | solution.py:223
  43.9 14.5 %all_to_all.31 = f32[8,1,3200]{2,1,0:T(1,128)S(1)} all-to-all(f32[8,1,3200]{2,1,0:T(1,128)S(1)} %broadcast_in_dim.23), channel_id=1, replica_groups=mesh['x'=4,'zh'=2,'y'=4,'zl'=4,'c'=2] {'zl','zh'}, dimensions={0} | all-to-all | bytes 204800 | tf_op jit(solution)/shard_map/all_to_all | solution.py:223
  58.7 10.2 %all_to_all.32 = f32[16,1,3200]{2,1,0:T(1,128)S(1)} all-to-all(f32[16,1,3200]{2,1,0:T(1,128)S(1)} %broadcast_in_dim.24), channel_id=1, replica_groups=mesh['x'=4,'zh'=2,'y'=4,'zl'=4,'c'=2] {'y','x'}, dimensions={0} | all-to-all | bytes 409600 | tf_op jit(solution)/shard_map/all_to_all | solution.py:223
  68.9 4.7 %collective-permute-start.3 = (f32[400,128]{1,0:T(8,128)S(1)}, f32[400,128]{1,0:T(8,128)S(1)}, u32[]{:S(2)}, u32[]{:S(2)}) collective-permute-start(f32[400,128]{1,0:T(8,128)S(1)} %bitcast.37), channel_id=1, source_target_pairs={{0,1},{1,0},{2,3},{3,2},{4,5},{5,4},{6,7},{7,6},{8,9},{9,8},{10,11... | collective-permute-start | bytes 614408 | tf_op jit(solution)/shard_map/ppermute | solution.py:219
  73.6 0.7 shard_map.141
  74.6 3.2 %shard_map.142 = (f32[400,128]{1,0:T(8,128)S(1)}, f32[400,128]{1,0:T(8,128)S(1)}, f32[400,512]{1,0:T(8,128)S(1)}, f32[200,384]{1,0:T(8,128)S(1)}, f32[208,384]{1,0:T(8,128)S(1)}) custom-call(f32[400,128]{1,0:T(8,128)S(1)} %collective-permute-done.3.far_ref, f32[400,512]{1,0:T(8,128)S(1)} %get-tuple-element.87.near_rows_ref, ...), custom_call_target="tpu_custom_call" | custom-call | flops 2617245696 | bytes 5562880 | tf_op jit(solution)/shard_map/pallas_call | solution.py:201
  78.3 1.4 %collective-permute-start.5 = (f32[200,384]{1,0:T(8,128)S(1)}, f32[200,384]{1,0:T(8,128)S(1)}, u32[]{:S(2)}, u32[]{:S(2)}) collective-permute-start(f32[200,384]{1,0:T(8,128)S(1)} %get-tuple-element.96), channel_id=1, source_target_pairs={{0,27},{1,28},{2,29},{3,30},{4,31},{5,0},{6,1},{7,2},{8,3},{9,4},{... | collective-permute-start | bytes 921608 | tf_op jit(solution)/shard_map/ppermute | solution.py:215
  79.8 11.0 %all_to_all.33 = f32[16,1,3200]{2,1,0:T(1,128)S(1)} all-to-all(f32[16,1,3200]{2,1,0:T(1,128)S(1)} %bitcast.46), channel_id=1, replica_groups=mesh['x'=4,'zh'=2,'y'=4,'zl'=4,'c'=2] {'y','x'}, dimensions={0} | all-to-all | bytes 409600 | tf_op jit(solution)/shard_map/all_to_all | solution.py:223
  91.0 10.6 %all_to_all.34 = f32[8,1,3200]{2,1,0:T(1,128)S(1)} all-to-all(f32[8,1,3200]{2,1,0:T(1,128)S(1)} %broadcast_in_dim.25), channel_id=1, replica_groups=mesh['x'=4,'zh'=2,'y'=4,'zl'=4,'c'=2] {'zl','zh'}, dimensions={0} | all-to-all | bytes 204800 | tf_op jit(solution)/shard_map/all_to_all | solution.py:223
  101.6 4.2 %collective-permute-start.6 = (f32[208,384]{1,0:T(8,128)S(1)}, f32[208,384]{1,0:T(8,128)S(1)}, u32[]{:S(2)}, u32[]{:S(2)}) collective-permute-start(f32[208,384]{1,0:T(8,128)S(1)} %get-tuple-element.104), channel_id=1, source_target_pairs={{0,27},{1,28},{2,29},{3,30},{4,31},{5,0},{6,1},{7,2},{8,3},{9,4},{... | collective-permute-start | bytes 958472 | tf_op jit(solution)/shard_map/ppermute | solution.py:215
  105.9 10.6 %all_to_all.35 = f32[16,1,3200]{2,1,0:T(1,128)S(1)} all-to-all(f32[16,1,3200]{2,1,0:T(1,128)S(1)} %broadcast_in_dim.26), channel_id=1, replica_groups=mesh['x'=4,'zh'=2,'y'=4,'zl'=4,'c'=2] {'y','x'}, dimensions={0} | all-to-all | bytes 409600 | tf_op jit(solution)/shard_map/all_to_all | solution.py:223
  116.5 0.9 collective-permute-start.7
  117.4 1.7 %shard_map.143 = (f32[400,384]{1,0:T(8,128)}, f32[400,384]{1,0:T(8,128)}, f32[384]{0:T(512)}) custom-call(f32[400,512]{1,0:T(8,128)S(1)} %get-tuple-element.100.way_ref, f32[400,384]{1,0:T(8,128)S(1)} %get-tuple-element.85.src_ref, f32[1,384]{1,0:T(1,128)S(1)} %get-tuple-element.101.src_state_ref, s32[8,512]{1,0:T(8,128)S(1)} %stack.31.ids_ref, ...), custom_call_target="tpu_custom_call" | custom-call | flops 402653184 | bytes 3308544 | tf_op jit(solution)/shard_map/pallas_call | solution.py:201
  119.2 0.8 maximum_bitcast_fusion
  (62 shorter events, 4.3 us)
Async XLA Ops:
  0.6 27.4 %collective-permute-start = (f32[400,384]{1,0:T(8,128)}, f32[400,384]{1,0:T(8,128)S(1)}, u32[]{:S(2)}, u32[]{:S(2)}) collective-permute-start(f32[400,384]{1,0:T(8,128)} %bitcast.62), channel_id=1, source_target_pairs={{0,5},{1,6},{2,7},{3,8},{4,9},{5,10},{6,11},{7,12},{8,13},{9,14},{... | collective-permute-start | bytes 1843208 | tf_op jit(solution)/shard_map/ppermute | solution.py:215
  6.4 0.7 copy-start.4
  7.1 0.7 copy-start.6
  7.8 0.7 copy-start.7
  8.6 0.7 slice-start
  9.3 0.7 copy-start.8
  10.0 0.7 copy-start.5
  10.8 1.1 copy-start
  11.9 1.0 copy-start.2
  12.9 1.0 copy-start.3
  15.2 12.8 %collective-permute-start.1 = (f32[1,384]{1,0:T(1,128)S(1)}, f32[1,384]{1,0:T(1,128)S(1)}, u32[]{:S(2)}, u32[]{:S(2)}) collective-permute-start(f32[1,384]{1,0:T(1,128)S(1)} %get-tuple-element.65), channel_id=1, source_target_pairs={{0,5},{1,6},{2,7},{3,8},{4,9},{5,10},{6,11},{7,12},{8,13},{9,14},{... | collective-permute-start | bytes 4616 | tf_op jit(solution)/shard_map/ppermute | solution.py:215
  28.0 2.3 %copy-start.9 = (f32[384]{0:T(512)S(1)}, f32[384]{0:T(512)}, u32[]{:S(2)}) copy-start(f32[384]{0:T(512)} %param.12) | copy-start | bytes 4612
  28.0 2.3 %copy-start.1 = (f32[384,400]{0,1:T(8,128)S(1)}, f32[384,400]{0,1:T(8,128)}, u32[]{:S(2)}) copy-start(f32[384,400]{0,1:T(8,128)} %param.11) | copy-start | bytes 1843204
  30.2 1.6 %collective-permute-start.2 = (f32[400,128]{1,0:T(8,128)S(1)}, f32[400,128]{1,0:T(8,128)S(1)}, u32[]{:S(2)}, u32[]{:S(2)}) collective-permute-start(f32[400,128]{1,0:T(8,128)S(1)} %get-tuple-element.69), channel_id=1, source_target_pairs={{0,1},{1,0},{2,3},{3,2},{4,5},{5,4},{6,7},{7,6},{8,9},{9,8},{10,11... | collective-permute-start | bytes 614408 | tf_op jit(solution)/shard_map/ppermute | solution.py:219
  68.9 5.7 %collective-permute-start.3 = (f32[400,128]{1,0:T(8,128)S(1)}, f32[400,128]{1,0:T(8,128)S(1)}, u32[]{:S(2)}, u32[]{:S(2)}) collective-permute-start(f32[400,128]{1,0:T(8,128)S(1)} %bitcast.37), channel_id=1, source_target_pairs={{0,1},{1,0},{2,3},{3,2},{4,5},{5,4},{6,7},{7,6},{8,9},{9,8},{10,11... | collective-permute-start | bytes 614408 | tf_op jit(solution)/shard_map/ppermute | solution.py:219
  77.8 1.9 %collective-permute-start.4 = (f32[400,128]{1,0:T(8,128)S(1)}, f32[400,128]{1,0:T(8,128)S(1)}, u32[]{:S(2)}, u32[]{:S(2)}) collective-permute-start(f32[400,128]{1,0:T(8,128)S(1)} %get-tuple-element.95), channel_id=1, source_target_pairs={{0,1},{1,0},{2,3},{3,2},{4,5},{5,4},{6,7},{7,6},{8,9},{9,8},{10,11... | collective-permute-start | bytes 614408 | tf_op jit(solution)/shard_map/ppermute | solution.py:219
  78.3 12.6 %collective-permute-start.5 = (f32[200,384]{1,0:T(8,128)S(1)}, f32[200,384]{1,0:T(8,128)S(1)}, u32[]{:S(2)}, u32[]{:S(2)}) collective-permute-start(f32[200,384]{1,0:T(8,128)S(1)} %get-tuple-element.96), channel_id=1, source_target_pairs={{0,27},{1,28},{2,29},{3,30},{4,31},{5,0},{6,1},{7,2},{8,3},{9,4},{... | collective-permute-start | bytes 921608 | tf_op jit(solution)/shard_map/ppermute | solution.py:215
  101.6 14.9 %collective-permute-start.6 = (f32[208,384]{1,0:T(8,128)S(1)}, f32[208,384]{1,0:T(8,128)S(1)}, u32[]{:S(2)}, u32[]{:S(2)}) collective-permute-start(f32[208,384]{1,0:T(8,128)S(1)} %get-tuple-element.104), channel_id=1, source_target_pairs={{0,27},{1,28},{2,29},{3,30},{4,31},{5,0},{6,1},{7,2},{8,3},{9,4},{... | collective-permute-start | bytes 958472 | tf_op jit(solution)/shard_map/ppermute | solution.py:215
  116.5 2.6 %collective-permute-start.7 = (f32[400,128]{1,0:T(8,128)S(1)}, f32[400,128]{1,0:T(8,128)S(1)}, u32[]{:S(2)}, u32[]{:S(2)}) collective-permute-start(f32[400,128]{1,0:T(8,128)S(1)} %bitcast.43), channel_id=1, source_target_pairs={{0,1},{1,0},{2,3},{3,2},{4,5},{5,4},{6,7},{7,6},{8,9},{9,8},{10,11... | collective-permute-start | bytes 614408 | tf_op jit(solution)/shard_map/ppermute | solution.py:219

commit v9 on v8

--- a/solution.py
+++ b/solution.py
@@ -326,8 +326,9 @@
         scratch=[pltpu.SemaphoreType.DMA((2,))], passes=2, spaces=[vector, pl.BlockSpec(memory_space=pl.ANY), vector],
     )
     far = swapped(near)
-    first = core == 0
-    relation = jnp.concatenate([jnp.where(first, near, far), jnp.where(first, far, near)], axis=1)
+    relation = jnp.zeros((W, REL), jnp.float32)
+    relation = lax.dynamic_update_slice_in_dim(relation, near, core * HALF, 1)
+    relation = lax.dynamic_update_slice_in_dim(relation, far, (1 - core) * HALF, 1)
     return (src_table.T, dst_table.T, dst_sums, relation.T)
 
 

time: 121 us -> 121 us (level)
    unnamed x20 -> x22, local copies, waits for them, and re-layouts: 5.66 us -> 6.46 us
where the time goes in v9:
time: 121 us; the launch traced here: 120 us
  blocking collectives  68.8 us (57%)
  starting transfers between devices  17.7 us (15%)
  waiting for transfers between devices  13 us (11%)
  Pallas kernels  10.5 us (9%)
  local copies, waits for them, and re-layouts  7.87 us (7%)
  between operations  1.61 us (1%)
    all_to_all x6, blocking collectives, exchanged(): return lax.all_to_all(value, axes, split_axis=0, concat_axis=0, tiled=True)  68.8 us
    ppermute x4, waiting for transfers between devices, shifted(): return lax.ppermute(value, RIGHT, pairs)  12.6 us
    ppermute x4, starting transfers between devices, shifted(): return lax.ppermute(value, RIGHT, pairs)  11.6 us
    pallas_call x6, Pallas kernels, call(): pl.pallas_call(kernel, out_shape=shapes, in_specs=[scalar] * scalars + [v...  10.5 us
    unnamed x22, local copies, waits for them, and re-layouts  6.46 us
    ppermute x4, starting transfers between devices, swapped(): return lax.ppermute(value, 'c', [(0, 1), (1, 0)])  6.15 us
  transfers between devices with their start and end apart: 8, of which 2 were waited for; matrix products, arithmetic and copies ran while one was open for 1% of the time, Pallas kernels for 4%

profile of v9, /device:TPU:1, one launch (start us, length us, event | category | flops | bytes accessed | tf_op | source)
XLA Modules:
  0.0 120.0 jit_solution(5202050341508768124)
XLA Ops:
  0.6 5.8 %collective-permute-start = (f32[400,384]{1,0:T(8,128)}, f32[400,384]{1,0:T(8,128)S(1)}, u32[]{:S(2)}, u32[]{:S(2)}) collective-permute-start(f32[400,384]{1,0:T(8,128)} %bitcast.62), channel_id=1, source_target_pairs={{0,5},{1,6},{2,7},{3,8},{4,9},{5,10},{6,11},{7,12},{8,13},{9,14},{... | collective-permute-start | bytes 1843208 | tf_op jit(solution)/shard_map/ppermute | solution.py:215
  6.4 0.7 copy-done.5
  8.6 0.7 slice-done
  10.8 1.1 copy-done
  11.9 1.0 copy-done.2
  12.9 1.0 copy-done.3
  13.9 1.2 %shard_map.138 = (f32[400,512]{1,0:T(8,128)S(1)}, f32[400,512]{1,0:T(8,128)S(1)}, bf16[400,512]{1,0:T(8,128)(2,1)S(1)}, bf16[400,512]{1,0:T(8,128)(2,1)S(1)}, f3...) custom-call(s32[1]{0:T(128)} %bitcast.place_ref, ...), custom_call_target="tpu_custom_call" | custom-call | flops 805306368 | bytes 4331524 | tf_op jit(solution)/shard_map/pallas_call | solution.py:201
  15.4 12.6 %collective-permute-done.1.dst_state_ref = f32[1,384]{1,0:T(1,128)S(1)} collective-permute-done((f32[1,384]{1,0:T(1,128)S(1)}, f32[1,384]{1,0:T(1,128)S(1)}, u32[]{:S(2)}, u32[]{:S(2)}) %collective-permute-start.1) | collective-permute-done | bytes 1568 | tf_op jit(solution)/shard_map/ppermute | solution.py:215
  28.0 2.2 %shard_map.139 = (f32[400,128]{1,0:T(8,128)S(1)}, f32[400,128]{1,0:T(8,128)S(1)}, f32[400,512]{1,0:T(8,128)S(1)}, bf16[384,512]{1,0:T(8,128)(2,1)S(1)}, bf16[384,512]{1,0:T(8,128)(2,1)S(1)}) custom-call(bf16[400,512]{1,0:T(8,128)(2,1)S(1)} %get-tuple-element.61.high_ref, bf16[400,512]{1,0:T(8,128)(2,1)S(1)} %get-tuple-element.62.low_ref, ...), custom_call_target="tpu_custom_call" | custom-call | flops 1610612736 | bytes 5106688 | tf_op jit(solution)/shard_map/pallas_call | solution.py:201
  30.3 1.5 %shard_map.140 = (f32[400,384]{1,0:T(8,128)S(1)}, f32[1,384]{1,0:T(1,128)S(1)}, f32[400,384]{1,0:T(8,128)S(1)}, f32[1,384]{1,0:T(1,128)S(1)}) custom-call(f32[400,512]{1,0:T(8,128)S(1)} %get-tuple-element.70.way_ref, bf16[400,512]{1,0:T(8,128)(2,1)S(1)} %get-tuple-element.61.high_ref, bf16[400,512]{1,0:T(8,128)(2,1)S(1)} %get-tuple-element.62.low_ref, ...), custom_call_target="tpu_custom_call" | custom-call | flops 1006632960 | bytes 4904960 | tf_op jit(solution)/shard_map/pallas_call | solution.py:201
  31.9 11.9 %all_to_all.30 = f32[16,1,3200]{2,1,0:T(1,128)S(1)} all-to-all(f32[16,1,3200]{2,1,0:T(1,128)S(1)} %bitcast.44), channel_id=1, replica_groups=mesh['x'=4,'zh'=2,'y'=4,'zl'=4,'c'=2] {'y','x'}, dimensions={0} | all-to-all | bytes 409600 | tf_op jit(solution)/shard_map/all_to_all | solution.py:223
  43.9 14.5 %all_to_all.31 = f32[8,1,3200]{2,1,0:T(1,128)S(1)} all-to-all(f32[8,1,3200]{2,1,0:T(1,128)S(1)} %broadcast_in_dim.26), channel_id=1, replica_groups=mesh['x'=4,'zh'=2,'y'=4,'zl'=4,'c'=2] {'zl','zh'}, dimensions={0} | all-to-all | bytes 204800 | tf_op jit(solution)/shard_map/all_to_all | solution.py:223
  58.7 10.2 %all_to_all.32 = f32[16,1,3200]{2,1,0:T(1,128)S(1)} all-to-all(f32[16,1,3200]{2,1,0:T(1,128)S(1)} %broadcast_in_dim.27), channel_id=1, replica_groups=mesh['x'=4,'zh'=2,'y'=4,'zl'=4,'c'=2] {'y','x'}, dimensions={0} | all-to-all | bytes 409600 | tf_op jit(solution)/shard_map/all_to_all | solution.py:223
  68.9 4.7 %collective-permute-start.3 = (f32[400,128]{1,0:T(8,128)S(1)}, f32[400,128]{1,0:T(8,128)S(1)}, u32[]{:S(2)}, u32[]{:S(2)}) collective-permute-start(f32[400,128]{1,0:T(8,128)S(1)} %bitcast.36), channel_id=1, source_target_pairs={{0,1},{1,0},{2,3},{3,2},{4,5},{5,4},{6,7},{7,6},{8,9},{9,8},{10,11... | collective-permute-start | bytes 614408 | tf_op jit(solution)/shard_map/ppermute | solution.py:219
  73.6 0.7 shard_map.141
  74.6 3.2 %shard_map.142 = (f32[400,128]{1,0:T(8,128)S(1)}, f32[400,128]{1,0:T(8,128)S(1)}, f32[400,512]{1,0:T(8,128)S(1)}, f32[200,384]{1,0:T(8,128)S(1)}, f32[208,384]{1,0:T(8,128)S(1)}) custom-call(f32[400,128]{1,0:T(8,128)S(1)} %collective-permute-done.3.far_ref, f32[400,512]{1,0:T(8,128)S(1)} %get-tuple-element.87.near_rows_ref, ...), custom_call_target="tpu_custom_call" | custom-call | flops 2617245696 | bytes 5562880 | tf_op jit(solution)/shard_map/pallas_call | solution.py:201
  78.3 1.4 %collective-permute-start.5 = (f32[200,384]{1,0:T(8,128)S(1)}, f32[200,384]{1,0:T(8,128)S(1)}, u32[]{:S(2)}, u32[]{:S(2)}) collective-permute-start(f32[200,384]{1,0:T(8,128)S(1)} %get-tuple-element.96), channel_id=1, source_target_pairs={{0,27},{1,28},{2,29},{3,30},{4,31},{5,0},{6,1},{7,2},{8,3},{9,4},{... | collective-permute-start | bytes 921608 | tf_op jit(solution)/shard_map/ppermute | solution.py:215
  79.8 11.0 %all_to_all.33 = f32[16,1,3200]{2,1,0:T(1,128)S(1)} all-to-all(f32[16,1,3200]{2,1,0:T(1,128)S(1)} %bitcast.45), channel_id=1, replica_groups=mesh['x'=4,'zh'=2,'y'=4,'zl'=4,'c'=2] {'y','x'}, dimensions={0} | all-to-all | bytes 409600 | tf_op jit(solution)/shard_map/all_to_all | solution.py:223
  91.0 10.6 %all_to_all.34 = f32[8,1,3200]{2,1,0:T(1,128)S(1)} all-to-all(f32[8,1,3200]{2,1,0:T(1,128)S(1)} %broadcast_in_dim.28), channel_id=1, replica_groups=mesh['x'=4,'zh'=2,'y'=4,'zl'=4,'c'=2] {'zl','zh'}, dimensions={0} | all-to-all | bytes 204800 | tf_op jit(solution)/shard_map/all_to_all | solution.py:223
  101.6 4.2 %collective-permute-start.6 = (f32[208,384]{1,0:T(8,128)S(1)}, f32[208,384]{1,0:T(8,128)S(1)}, u32[]{:S(2)}, u32[]{:S(2)}) collective-permute-start(f32[208,384]{1,0:T(8,128)S(1)} %get-tuple-element.104), channel_id=1, source_target_pairs={{0,27},{1,28},{2,29},{3,30},{4,31},{5,0},{6,1},{7,2},{8,3},{9,4},{... | collective-permute-start | bytes 958472 | tf_op jit(solution)/shard_map/ppermute | solution.py:215
  105.9 10.6 %all_to_all.35 = f32[16,1,3200]{2,1,0:T(1,128)S(1)} all-to-all(f32[16,1,3200]{2,1,0:T(1,128)S(1)} %broadcast_in_dim.29), channel_id=1, replica_groups=mesh['x'=4,'zh'=2,'y'=4,'zl'=4,'c'=2] {'y','x'}, dimensions={0} | all-to-all | bytes 409600 | tf_op jit(solution)/shard_map/all_to_all | solution.py:223
  116.5 0.9 collective-permute-start.7
  117.5 1.7 %shard_map.143 = (f32[400,384]{1,0:T(8,128)}, f32[400,384]{1,0:T(8,128)}, f32[384]{0:T(512)}) custom-call(f32[400,512]{1,0:T(8,128)S(1)} %get-tuple-element.100.way_ref, f32[400,384]{1,0:T(8,128)S(1)} %get-tuple-element.85.src_ref, f32[1,384]{1,0:T(1,128)S(1)} %get-tuple-element.101.src_state_ref, s32[8,512]{1,0:T(8,128)S(1)} %stack.31.ids_ref, ...), custom_call_target="tpu_custom_call" | custom-call | flops 402653184 | bytes 3308544 | tf_op jit(solution)/shard_map/pallas_call | solution.py:201
  119.3 0.7 copy-done.4
  (65 shorter events, 4.4 us)
Async XLA Ops:
  0.6 27.4 %collective-permute-start = (f32[400,384]{1,0:T(8,128)}, f32[400,384]{1,0:T(8,128)S(1)}, u32[]{:S(2)}, u32[]{:S(2)}) collective-permute-start(f32[400,384]{1,0:T(8,128)} %bitcast.62), channel_id=1, source_target_pairs={{0,5},{1,6},{2,7},{3,8},{4,9},{5,10},{6,11},{7,12},{8,13},{9,14},{... | collective-permute-start | bytes 1843208 | tf_op jit(solution)/shard_map/ppermute | solution.py:215
  6.4 0.7 copy-start.5
  7.1 0.7 copy-start.7
  7.9 0.7 copy-start.8
  8.6 0.7 slice-start
  9.4 0.7 copy-start.6
  10.1 0.7 copy-start.9
  10.8 1.1 copy-start
  11.9 1.0 copy-start.2
  12.9 1.0 copy-start.3
  15.2 12.8 %collective-permute-start.1 = (f32[1,384]{1,0:T(1,128)S(1)}, f32[1,384]{1,0:T(1,128)S(1)}, u32[]{:S(2)}, u32[]{:S(2)}) collective-permute-start(f32[1,384]{1,0:T(1,128)S(1)} %get-tuple-element.65), channel_id=1, source_target_pairs={{0,5},{1,6},{2,7},{3,8},{4,9},{5,10},{6,11},{7,12},{8,13},{9,14},{... | collective-permute-start | bytes 4616 | tf_op jit(solution)/shard_map/ppermute | solution.py:215
  28.0 2.3 %copy-start.10 = (f32[384]{0:T(512)S(1)}, f32[384]{0:T(512)}, u32[]{:S(2)}) copy-start(f32[384]{0:T(512)} %param.12) | copy-start | bytes 4612
  28.0 2.3 %copy-start.1 = (f32[384,400]{0,1:T(8,128)S(1)}, f32[384,400]{0,1:T(8,128)}, u32[]{:S(2)}) copy-start(f32[384,400]{0,1:T(8,128)} %param.11) | copy-start | bytes 1843204
  30.2 1.6 %collective-permute-start.2 = (f32[400,128]{1,0:T(8,128)S(1)}, f32[400,128]{1,0:T(8,128)S(1)}, u32[]{:S(2)}, u32[]{:S(2)}) collective-permute-start(f32[400,128]{1,0:T(8,128)S(1)} %get-tuple-element.69), channel_id=1, source_target_pairs={{0,1},{1,0},{2,3},{3,2},{4,5},{5,4},{6,7},{7,6},{8,9},{9,8},{10,11... | collective-permute-start | bytes 614408 | tf_op jit(solution)/shard_map/ppermute | solution.py:219
  68.9 5.7 %collective-permute-start.3 = (f32[400,128]{1,0:T(8,128)S(1)}, f32[400,128]{1,0:T(8,128)S(1)}, u32[]{:S(2)}, u32[]{:S(2)}) collective-permute-start(f32[400,128]{1,0:T(8,128)S(1)} %bitcast.36), channel_id=1, source_target_pairs={{0,1},{1,0},{2,3},{3,2},{4,5},{5,4},{6,7},{7,6},{8,9},{9,8},{10,11... | collective-permute-start | bytes 614408 | tf_op jit(solution)/shard_map/ppermute | solution.py:219
  77.8 1.9 %collective-permute-start.4 = (f32[400,128]{1,0:T(8,128)S(1)}, f32[400,128]{1,0:T(8,128)S(1)}, u32[]{:S(2)}, u32[]{:S(2)}) collective-permute-start(f32[400,128]{1,0:T(8,128)S(1)} %get-tuple-element.95), channel_id=1, source_target_pairs={{0,1},{1,0},{2,3},{3,2},{4,5},{5,4},{6,7},{7,6},{8,9},{9,8},{10,11... | collective-permute-start | bytes 614408 | tf_op jit(solution)/shard_map/ppermute | solution.py:219
  78.3 12.6 %collective-permute-start.5 = (f32[200,384]{1,0:T(8,128)S(1)}, f32[200,384]{1,0:T(8,128)S(1)}, u32[]{:S(2)}, u32[]{:S(2)}) collective-permute-start(f32[200,384]{1,0:T(8,128)S(1)} %get-tuple-element.96), channel_id=1, source_target_pairs={{0,27},{1,28},{2,29},{3,30},{4,31},{5,0},{6,1},{7,2},{8,3},{9,4},{... | collective-permute-start | bytes 921608 | tf_op jit(solution)/shard_map/ppermute | solution.py:215
  101.6 14.9 %collective-permute-start.6 = (f32[208,384]{1,0:T(8,128)S(1)}, f32[208,384]{1,0:T(8,128)S(1)}, u32[]{:S(2)}, u32[]{:S(2)}) collective-permute-start(f32[208,384]{1,0:T(8,128)S(1)} %get-tuple-element.104), channel_id=1, source_target_pairs={{0,27},{1,28},{2,29},{3,30},{4,31},{5,0},{6,1},{7,2},{8,3},{9,4},{... | collective-permute-start | bytes 958472 | tf_op jit(solution)/shard_map/ppermute | solution.py:215
  116.5 2.7 %collective-permute-start.7 = (f32[400,128]{1,0:T(8,128)S(1)}, f32[400,128]{1,0:T(8,128)S(1)}, u32[]{:S(2)}, u32[]{:S(2)}) collective-permute-start(f32[400,128]{1,0:T(8,128)S(1)} %bitcast.42), channel_id=1, source_target_pairs={{0,1},{1,0},{2,3},{3,2},{4,5},{5,4},{6,7},{7,6},{8,9},{9,8},{10,11... | collective-permute-start | bytes 614408 | tf_op jit(solution)/shard_map/ppermute | solution.py:219
  119.3 0.8 copy-start.4
